TPU v7x, 512 devices: a whole 4x4x16 slice. The times are simulated.
512 devices in a mesh: phase: 64 (over x_lo, z, core), space: 8 (over x_hi, y).
Axes of the slice: x: 4 (x_hi: 2, x_lo: 2; x = x_hi * 2 + x_lo), y: 4, z: 16, core: 2. Of those that a mesh axis runs over, the one named last changes fastest.
Arguments:
- object_field: float32 [2, 64, 272, 2048], P(None, 'phase', None, 'space'), may hold values from -6 to 6
- split_field: float32 [2, 64, 272, 2048], P(None, 'phase', None, 'space'), may hold values from -6 to 6
- scaled_dual: float32 [2, 64, 272, 2048], P(None, 'phase', None, 'space'), may hold values from -4 to 4
- probe: float32 [2, 256, 256], replicated, may hold values from -6 to 6
- amplitudes: float32 [64, 48, 256, 256], P('phase', 'space'), may hold values from 0.1 to 4
- row_offsets: int32 [64, 48], P('phase', 'space'), may hold values from 0 to 16, as said below
- col_offsets: int32 [64, 48], P('phase', 'space'), may hold values from 0 to 255, as said below
Outputs:
- updated_object: float32 [2, 64, 272, 2048], P(None, 'phase', None, 'space')
- updated_split: float32 [2, 64, 272, 2048], P(None, 'phase', None, 'space')
- updated_dual: float32 [2, 64, 272, 2048], P(None, 'phase', None, 'space')
- probe_gradient: float32 [2, 256, 256], replicated
Inputs may be any that keep to these rules, and one draw needn't show every extreme that they name: `row_offsets`: A scan position's rows lie inside the band. `col_offsets`: A scan position may reach into the next tile; positions of the last tile end inside it (offset at most 0).
All inputs are finite; a program needn't handle non-finite values.
Results may differ from a plain program's by a relative error of at most 0.0003.
Values sent between devices are 32-bit elements; how exact they have to be, the bound alone decides.
A program may use at most 64 MiB of HBM per device.

v0:
```python
import math

import jax
import jax.numpy as jnp
from jax import lax
from jax.sharding import PartitionSpec as P

amp_floor = 0.25
ridge = 1.0
tv_step = 0.25
shrink_level = 0.5


def from_behind(block, axis, distance):
    devices = range(lax.axis_size(axis))
    route = [(i - distance, i) for i in devices if i - distance in devices]
    return lax.ppermute(block, axis, route)


def passed_along(value, axis, steps):
    count = lax.axis_size(axis)
    pairs = [(source, (source + steps) % count) for source in range(count)]
    return lax.ppermute(value, axis, pairs)


def dft_tables(length):
    index = lax.iota(jnp.int32, length)
    product = index[:, None] * index[None, :] % length
    angle = 2.0 * math.pi / length * product.astype(jnp.float32)
    scale = 1.0 / math.sqrt(length)
    return (jnp.cos(angle) * scale, -jnp.sin(angle) * scale)


def transform(real_part, imag_part, cosine, sine):
    highest = lax.Precision.HIGHEST
    left_re = jnp.einsum("jk,bkl->bjl", cosine, real_part, precision=highest) - jnp.einsum(
        "jk,bkl->bjl", sine, imag_part, precision=highest
    )
    left_im = jnp.einsum("jk,bkl->bjl", cosine, imag_part, precision=highest) + jnp.einsum(
        "jk,bkl->bjl", sine, real_part, precision=highest
    )
    out_re = jnp.einsum("bjk,kl->bjl", left_re, cosine, precision=highest) - jnp.einsum(
        "bjk,kl->bjl", left_im, sine, precision=highest
    )
    out_im = jnp.einsum("bjk,kl->bjl", left_re, sine, precision=highest) + jnp.einsum(
        "bjk,kl->bjl", left_im, cosine, precision=highest
    )
    return (out_re, out_im)


def shards(object_field, split_field, scaled_dual, probe, amplitudes, row_offsets, col_offsets):
    own = object_field[:, 0]
    split_own = split_field[:, 0]
    dual_own = scaled_dual[:, 0]
    patch = probe.shape[1]
    tile_cols = own.shape[2]
    band_rows = own.shape[1]
    count = amplitudes.shape[1]
    right_part = from_behind(own, "space", -1)
    extended = jnp.concatenate([own, right_part], axis=2)
    probe_re = probe[0]
    probe_im = probe[1]
    probe_power = probe_re * probe_re + probe_im * probe_im
    pieces = []
    for slot in range(count):
        top = row_offsets[0, slot]
        left = col_offsets[0, slot]
        pieces.append(lax.dynamic_slice(extended, (jnp.int32(0), top, left), (2, patch, patch)))
    stack_pieces = jnp.stack(pieces, 1)
    piece_re = stack_pieces[0]
    piece_im = stack_pieces[1]
    wave_re = probe_re * piece_re - probe_im * piece_im
    wave_im = probe_re * piece_im + probe_im * piece_re
    cosine, sine = dft_tables(patch)
    far_re, far_im = transform(wave_re, wave_im, cosine, sine)
    magnitude = jnp.sqrt(far_re * far_re + far_im * far_im)
    factor = amplitudes[0] / jnp.maximum(magnitude, amp_floor)
    back_re, back_im = transform(far_re * factor, far_im * factor, cosine, -sine)
    change_re = back_re - wave_re
    change_im = back_im - wave_im
    numer_re = probe_re * change_re + probe_im * change_im
    numer_im = probe_re * change_im - probe_im * change_re
    accum = jnp.zeros((2, band_rows, tile_cols + patch), jnp.float32)
    weight_acc = jnp.zeros((band_rows, tile_cols + patch), jnp.float32)
    for slot in range(count):
        top = row_offsets[0, slot]
        left = col_offsets[0, slot]
        corner = (jnp.int32(0), top, left)
        current = lax.dynamic_slice(accum, corner, (2, patch, patch))
        addition = jnp.stack([numer_re[slot], numer_im[slot]])
        accum = lax.dynamic_update_slice(accum, current + addition, corner)
        current_w = lax.dynamic_slice(weight_acc, (top, left), (patch, patch))
        weight_acc = lax.dynamic_update_slice(weight_acc, current_w + probe_power, (top, left))
    grad_re = jnp.sum(piece_re * change_re + piece_im * change_im, 0)
    grad_im = jnp.sum(piece_re * change_im - piece_im * change_re, 0)
    incoming_num, incoming_wt = from_behind(
        (accum[:, :, tile_cols:], weight_acc[:, tile_cols:]), "space", 1
    )
    numer = accum[:, :, :tile_cols].at[:, :, :patch].add(incoming_num)
    weight = weight_acc[:, :tile_cols].at[:, :patch].add(incoming_wt)
    data_step = numer / (weight + ridge)[None]
    next_object = passed_along(own, "phase", -1)
    resid_own = next_object - own - split_own + dual_own
    resid_prev = passed_along(resid_own, "phase", 1)
    updated = own + data_step - tv_step * (resid_prev - resid_own)
    next_updated = passed_along(updated, "phase", -1)
    joint = next_updated - updated + dual_own
    size_abs = jnp.sqrt(joint[0] * joint[0] + joint[1] * joint[1])
    shrink = jnp.maximum(size_abs - shrink_level, 0.0) / jnp.maximum(size_abs, shrink_level)
    new_split = joint * shrink[None]
    new_dual = joint - new_split
    total_count = lax.axis_size("phase") * lax.axis_size("space") * count
    summed = lax.psum(jnp.stack([grad_re, grad_im]), ("phase", "space"))
    probe_gradient = summed / math.sqrt(total_count)
    return (updated[:, None], new_split[:, None], new_dual[:, None], probe_gradient)


def solution(mesh):
    in_specs = (
        P(None, "phase", None, "space"),
        P(None, "phase", None, "space"),
        P(None, "phase", None, "space"),
        P(),
        P("phase", "space", None, None),
        P("phase", "space"),
        P("phase", "space"),
    )
    out_specs = (
        P(None, "phase", None, "space"),
        P(None, "phase", None, "space"),
        P(None, "phase", None, "space"),
        P(),
    )
    return jax.shard_map(shards, mesh=mesh, in_specs=in_specs, out_specs=out_specs, check_vma=False)
```

profile of v0, /device:TPU:1, one launch (start us, length us, event | category | flops | bytes accessed | tf_op | source)
XLA Modules:
  0.0 682.3 jit_solution(4456556687792650652)
XLA Ops:
  8.7 8.8 %collective-permute-start.3 = (f32[2,272,256]{2,1,0:T(8,128)}, f32[2,272,256]{2,1,0:T(8,128)}, u32[]{:S(2)}, u32[]{:S(2)}) collective-permute-start(f32[2,272,256]{2,1,0:T(8,128)} %bitcast.191), channel_id=1, source_target_pairs={{0,504},{8,0},{16,8},{24,16},{32,24},{40,32},{48,40},{56,48},{64,5... | collective-permute-start | bytes 1671176 | tf_op jit(solution)/shard_map/ppermute | solution.py:23
  42.4 3.8 dynamic_update_slice.44
  57.3 3.9 dynamic_update_slice.46
  72.4 3.8 convolution_add_fusion.1
  83.5 3.7 convolution_subtract_fusion.1
  87.1 3.9 fusion.18
  91.0 3.7 fusion.21
  94.7 4.2 fusion.68
  98.9 4.6 fusion.65
  103.5 4.2 convolution_add_fusion
  111.3 3.8 fusion
  115.1 4.2 convolution_subtract_fusion
  119.3 3.6 subtract_subtract_fusion
  122.9 5.6 add_reduce_fusion
  130.1 6.4 dynamic_update_slice.36
  137.8 6.8 %dynamic_update_slice.37 = f32[2,272,512]{2,1,0:T(8,128)S(1)} dynamic-update-slice(f32[2,272,512]{2,1,0:T(8,128)S(1)} %dynamic_update_slice.36, f32[2,256,256]{2,1,0:T(8,128)S(1)} %maximum_add_fusion, s32[]{:T(128)} %constant.97.clone.1, s32[]{:T(128)S(6)} %select_n.119, s32[]{:T(128)S(6)} %select_n.120) | dynamic-update-slice | bytes 1048580 | tf_op jit(solution)/shard_map/dynamic_update_slice | solution.py:91
  145.9 7.7 %dynamic_update_slice.38 = f32[2,272,512]{2,1,0:T(8,128)S(1)} dynamic-update-slice(f32[2,272,512]{2,1,0:T(8,128)S(1)} %dynamic_update_slice.37, f32[2,256,256]{2,1,0:T(8,128)S(1)} %maximum_add_fusion.1, s32[]{:T(128)} %constant.97.clone.1, s32[]{:T(128)S(6)} %select_n.121, s32[]{:T(128)S(6)} %select_n.122) | dynamic-update-slice | bytes 1048580 | tf_op jit(solution)/shard_map/dynamic_update_slice | solution.py:91
  154.8 6.9 %dynamic_update_slice.39 = f32[2,272,512]{2,1,0:T(8,128)S(1)} dynamic-update-slice(f32[2,272,512]{2,1,0:T(8,128)S(1)} %dynamic_update_slice.38, f32[2,256,256]{2,1,0:T(8,128)S(1)} %maximum_add_fusion.2, s32[]{:T(128)} %constant.97.clone.1, s32[]{:T(128)S(6)} %select_n.123, s32[]{:T(128)S(6)} %select_n.124) | dynamic-update-slice | bytes 1048580 | tf_op jit(solution)/shard_map/dynamic_update_slice | solution.py:91
  163.0 6.9 %dynamic_update_slice.40 = f32[2,272,512]{2,1,0:T(8,128)S(1)} dynamic-update-slice(f32[2,272,512]{2,1,0:T(8,128)S(1)} %dynamic_update_slice.39, f32[2,256,256]{2,1,0:T(8,128)S(1)} %maximum_add_fusion.3, s32[]{:T(128)} %constant.97.clone.1, s32[]{:T(128)S(6)} %select_n.125, s32[]{:T(128)S(6)} %select_n.126) | dynamic-update-slice | bytes 1048580 | tf_op jit(solution)/shard_map/dynamic_update_slice | solution.py:91
  171.1 6.8 %dynamic_update_slice.41 = f32[2,272,512]{2,1,0:T(8,128)S(1)} dynamic-update-slice(f32[2,272,512]{2,1,0:T(8,128)S(1)} %dynamic_update_slice.40, f32[2,256,256]{2,1,0:T(8,128)S(1)} %maximum_add_fusion.4, s32[]{:T(128)} %constant.97.clone.1, s32[]{:T(128)S(6)} %select_n.127, s32[]{:T(128)S(6)} %select_n.128) | dynamic-update-slice | bytes 1048580 | tf_op jit(solution)/shard_map/dynamic_update_slice | solution.py:91
  178.8 10.4 %collective-permute-start.1 = (f32[2,272,256]{2,1,0:T(8,128)}, f32[2,272,256]{2,1,0:T(8,128)}, u32[]{:S(2)}, u32[]{:S(2)}) collective-permute-start(f32[2,272,256]{2,1,0:T(8,128)} %slice.198), channel_id=1, source_target_pairs={{0,1},{1,2},{2,3},{3,4},{4,5},{5,6},{6,7},{8,9},{9,10},{10,11},{11... | collective-permute-start | bytes 1671176 | tf_op jit(solution)/shard_map/ppermute | solution.py:17
  198.6 5.5 collective-permute-done.2
  205.7 6.9 %collective-permute-start.5 = (f32[2,272,256]{2,1,0:T(8,128)S(1)}, f32[2,272,256]{2,1,0:T(8,128)S(1)}, u32[]{:S(2)}, u32[]{:S(2)}) collective-permute-start(f32[2,272,256]{2,1,0:T(8,128)S(1)} %fusion.31), channel_id=1, source_target_pairs={{0,504},{8,0},{16,8},{24,16},{32,24},{40,32},{48,40},{56,48},{64,5... | collective-permute-start | bytes 1671176 | tf_op jit(solution)/shard_map/ppermute | solution.py:23
  213.4 458.6 %all-reduce.2.cloned.1.call-done = f32[2,256,256]{2,1,0:T(8,128)} async-done(((f32[2,256,256]{2,1,0:T(8,128)}), f32[2,256,256]{2,1,0:T(8,128)}) %all-reduce.2.cloned.1.call-update) | async-done | bytes 524304 | tf_op jit(solution)/shard_map/psum | solution.py:113
  (68 shorter events, 60.4 us)
Async XLA Ops:
  7.2 30.3 %copy-start.1 = (f32[2,256,256]{2,1,0:T(8,128)S(1)}, f32[2,256,256]{2,1,0:T(8,128)}, u32[]{:S(2)}) copy-start(f32[2,256,256]{2,1,0:T(8,128)} %param.18) | copy-start | bytes 1572868
  7.2 664.8 %all-reduce.2.cloned.1.call-start = ((), (), s32[]{:S(2)}) async-start(), calls=%async_computation | async-start | bytes 1048576 | tf_op jit(solution)/shard_map/psum | solution.py:113
  7.2 55.4 %collective-permute-start = (f32[2,272,256]{2,1,0:T(8,128)}, f32[2,272,256]{2,1,0:T(8,128)S(1)}, u32[]{:S(2)}, u32[]{:S(2)}) collective-permute-start(f32[2,272,256]{2,1,0:T(8,128)} %bitcast.190), channel_id=1, source_target_pairs={{1,0},{2,1},{3,2},{4,3},{5,4},{6,5},{7,6},{9,8},{10,9},{11,10},{12... | collective-permute-start | bytes 1671176 | tf_op jit(solution)/shard_map/ppermute | solution.py:17
  8.7 180.6 %collective-permute-start.3 = (f32[2,272,256]{2,1,0:T(8,128)}, f32[2,272,256]{2,1,0:T(8,128)}, u32[]{:S(2)}, u32[]{:S(2)}) collective-permute-start(f32[2,272,256]{2,1,0:T(8,128)} %bitcast.191), channel_id=1, source_target_pairs={{0,504},{8,0},{16,8},{24,16},{32,24},{40,32},{48,40},{56,48},{64,5... | collective-permute-start | bytes 1671176 | tf_op jit(solution)/shard_map/ppermute | solution.py:23
  52.5 10.1 %copy-start = (f32[2,1,272,256]{3,2,1,0:T(8,128)S(1)}, f32[2,1,272,256]{3,2,1,0:T(8,128)}, u32[]{:S(2)}) copy-start(f32[2,1,272,256]{3,2,1,0:T(8,128)} %param.15) | copy-start | bytes 1671172
  91.0 3.7 copy-start.6
  178.8 25.3 %collective-permute-start.1 = (f32[2,272,256]{2,1,0:T(8,128)}, f32[2,272,256]{2,1,0:T(8,128)}, u32[]{:S(2)}, u32[]{:S(2)}) collective-permute-start(f32[2,272,256]{2,1,0:T(8,128)} %slice.198), channel_id=1, source_target_pairs={{0,1},{1,2},{2,3},{3,4},{4,5},{5,6},{6,7},{8,9},{9,10},{10,11},{11... | collective-permute-start | bytes 1671176 | tf_op jit(solution)/shard_map/ppermute | solution.py:17
  190.8 13.4 %collective-permute-start.4 = (f32[2,272,256]{2,1,0:T(8,128)S(1)}, f32[2,272,256]{2,1,0:T(8,128)}, u32[]{:S(2)}, u32[]{:S(2)}) collective-permute-start(f32[2,272,256]{2,1,0:T(8,128)S(1)} %bitcast_add_fusion.1), channel_id=1, source_target_pairs={{0,8},{8,16},{16,24},{24,32},{32,40},{40,48},{48,56},{56,64},{64,7... | collective-permute-start | bytes 1671176 | tf_op jit(solution)/shard_map/ppermute | solution.py:23
  197.2 6.8 collective-permute-start.2
  204.1 8.5 %copy-start.4 = (f32[256,256]{1,0:T(8,128)S(1)}, f32[256,256]{1,0:T(8,128)}, u32[]{:S(2)}) copy-start(f32[256,256]{1,0:T(8,128)} %get-tuple-element.48) | copy-start | bytes 786436
  204.1 8.5 %copy-start.5 = (f32[256,256]{1,0:T(8,128)S(1)}, f32[256,256]{1,0:T(8,128)}, u32[]{:S(2)}) copy-start(f32[256,256]{1,0:T(8,128)} %get-tuple-element.49) | copy-start | bytes 786436
  205.6 468.4 %copy-start.2 = (f32[2,272,256]{2,1,0:T(8,128)}, f32[2,272,256]{2,1,0:T(8,128)S(1)}, u32[]{:S(2)}) copy-start(f32[2,272,256]{2,1,0:T(8,128)S(1)} %fusion.31) | copy-start | bytes 1671172
  205.6 468.2 %copy-start.3 = (f32[2,1,272,256]{3,2,1,0:T(8,128)S(1)}, f32[2,1,272,256]{3,2,1,0:T(8,128)}, u32[]{:S(2)}) copy-start(f32[2,1,272,256]{3,2,1,0:T(8,128)} %param.17) | copy-start | bytes 1671172
  205.7 468.2 %collective-permute-start.5 = (f32[2,272,256]{2,1,0:T(8,128)S(1)}, f32[2,272,256]{2,1,0:T(8,128)S(1)}, u32[]{:S(2)}, u32[]{:S(2)}) collective-permute-start(f32[2,272,256]{2,1,0:T(8,128)S(1)} %fusion.31), channel_id=1, source_target_pairs={{0,504},{8,0},{16,8},{24,16},{32,24},{40,32},{48,40},{56,48},{64,5... | collective-permute-start | bytes 1671176 | tf_op jit(solution)/shard_map/ppermute | solution.py:23
Sparse Core Ops, SparseCore 0:
  213.5 458.4 all-reduce.1
where the time goes:
time: 688 us; the launch traced here: 682 us
  waiting for transfers between devices  464 us (67%)
  local copies, waits for them, and re-layouts  68.6 us (10%)
  matrix products  63.2 us (9%)
  between operations  37.2 us (5%)
  starting transfers between devices  30.9 us (4%)
  other arithmetic  18.4 us (3%)
    psum x1, waiting for transfers between devices, shards(): summed = lax.psum(jnp.stack([grad_re, grad_im]), ('phase', 'space'))  459 us
    dynamic_update_slice x6, local copies, waits for them, and re-layouts, shards(): accum = lax.dynamic_update_slice(accum, current + addition, corner)  41.6 us
    dynamic_update_slice x6, local copies, waits for them, and re-layouts, shards(): lax.dynamic_update_slice(weight_acc, current_w + probe_power, (top, left))  21.4 us
    ppermute x3, starting transfers between devices, passed_along(): return lax.ppermute(value, axis, pairs)  17.6 us
  transfers between devices with their start and end apart: 7, of which 2 were waited for; matrix products, arithmetic and copies ran while one was open for 22% of the time, Pallas kernels for 0%

commit v1 on v0

v1 whole, which is shorter than its diff:
```python
import functools
import math

import jax
import jax.numpy as jnp
import ml_dtypes
import numpy as np
from jax import lax
from jax.experimental import pallas as pl
from jax.experimental.pallas import tpu as pltpu
from jax.sharding import PartitionSpec as P

amp_floor = 0.25
ridge = 1.0
tv_step = 0.25
shrink_level = 0.5

SIDE = 256
HALF = 128
BAND = 272
SPILL = BAND - SIDE
CORES, Z_SIZE, X_LO, Y_SIZE, X_SIZE = 2, 16, 2, 4, 4
GRAD_ROWS = 1024
VMEM_BYTES = 50 * 1024 * 1024


def from_behind(block, axis, distance):
    devices = range(lax.axis_size(axis))
    route = [(i - distance, i) for i in devices if i - distance in devices]
    return lax.ppermute(block, axis, route)


def passed_along(value, axis, steps):
    count = lax.axis_size(axis)
    pairs = [(source, (source + steps) % count) for source in range(count)]
    return lax.ppermute(value, axis, pairs)


def two_parts(table):
    high = table.astype(ml_dtypes.bfloat16)
    low = (table - high.astype(np.float64)).astype(ml_dtypes.bfloat16)
    return np.stack([high, low])


def half_tables():
    place = np.arange(HALF)
    tables = []
    for odd in (0, 1):
        turns = ((2 * place[:, None] + odd) * place[None, :]) % SIDE
        angle = -2.0 * np.pi * turns / SIDE
        re = np.cos(angle) / math.sqrt(SIDE)
        im = np.sin(angle) / math.sqrt(SIDE)
        real_form = np.block([[re, -im], [im, re]])
        tables.append(two_parts(real_form))
        tables.append(two_parts(real_form.T))
    order = np.concatenate([np.arange(0, SIDE, 2), np.arange(1, SIDE, 2)])
    sorter = np.zeros((SIDE, SIDE), np.float32)
    sorter[order, np.arange(SIDE)] = 1.0
    return tables, sorter.astype(ml_dtypes.bfloat16)


def put_split(ref, rows, lanes, value):
    high = value.astype(jnp.bfloat16)
    ref[0, rows, lanes] = high
    ref[1, rows, lanes] = (value - high.astype(jnp.float32)).astype(jnp.bfloat16)


def dot(a, b):
    return jnp.dot(a, b, preferred_element_type=jnp.float32)


def table_dot(table, data):
    return dot(table[0], data[0]) + dot(table[1], data[0]) + dot(table[0], data[1])


def dot_table(data, table):
    return dot(data[0], table[0]) + dot(data[1], table[0]) + dot(data[0], table[1])


def rolled_probe(source, target, left):
    step = 64
    for start in range(0, SIDE, step):
        turned = pltpu.roll(source[start : start + step, :], left, 1)
        for side in range(2):
            lanes = slice(side * HALF, (side + 1) * HALF)
            target[side, SPILL + start : SPILL + start + step, :] = turned[:, lanes]
            if start + step == SIDE:
                target[side, 0:SPILL, :] = turned[step - SPILL :, lanes]


def patch_kernel(
    rows_s, cols_s, own, halo, probe, le, let, lo, lot, sorter, amp,
    numer_own, numer_next, grad,
    prow, pc, piece_s, wave_s, grow, xe, xo, ze, zo, amp_s, amp_c,
):
    slot = pl.program_id(0)
    top = rows_s[0, slot]
    left = cols_s[0, slot]

    @pl.when(slot == 0)
    def _():
        numer_own[...] = jnp.zeros_like(numer_own)
        numer_next[...] = jnp.zeros_like(numer_next)
        grad[...] = jnp.zeros_like(grad)

    rolled_probe(probe.at[0], prow.at[0], left)
    rolled_probe(probe.at[1], prow.at[1], left)

    for side in range(2):
        amp_c[side] = amp[0, 0, :, side * HALF : (side + 1) * HALF]
    for odd in range(2):
        part = jnp.concatenate([amp_c[side, pl.ds(odd, HALF, stride=2), :] for side in range(2)], 1)
        high = part.astype(jnp.bfloat16)
        low = (part - high.astype(jnp.float32)).astype(jnp.bfloat16)
        amp_s[odd * HALF : (odd + 1) * HALF, :] = dot(high, sorter[...]) + dot(low, sorter[...])

    step = 16
    row_id = lax.broadcasted_iota(jnp.int32, (step, HALF), 0)
    lane_id = lax.broadcasted_iota(jnp.int32, (step, HALF), 1)
    row_in = row_id >= top
    lane_in = [lane_id + side * HALF >= left for side in range(2)]

    def wave_rows(start, side):
        rows = slice(start, start + step)
        lanes = slice(side * HALF, (side + 1) * HALF)
        p = [prow[c, side, pl.ds(SPILL - top + start, step), :] for c in range(2)]
        piece = []
        for c in range(2):
            here = own[c, rows, lanes]
            there = halo[c, rows, lanes]
            if start == 0:
                here = jnp.where(row_in, here, own[c, SIDE:BAND, lanes])
                there = jnp.where(row_in, there, halo[c, SIDE:BAND, lanes])
            piece.append(jnp.where(lane_in[side], here, there))
            piece_s[c, rows, lanes] = piece[c]
            pc[c, rows, lanes] = p[c]
        wave = [p[0] * piece[0] - p[1] * piece[1], p[0] * piece[1] + p[1] * piece[0]]
        for c in range(2):
            wave_s[c, rows, lanes] = wave[c]
        return wave

    for start in range(0, HALF, step):
        for side in range(2):
            lanes = slice(side * HALF, (side + 1) * HALF)
            upper = wave_rows(start, side)
            lower = wave_rows(start + HALF, side)
            for c in range(2):
                rows = slice(c * HALF + start, c * HALF + start + step)
                put_split(xe, rows, lanes, upper[c] + lower[c])
                put_split(xo, rows, lanes, upper[c] - lower[c])

    re_half, im_half = slice(0, HALF), slice(HALF, SIDE)
    for odd, (table, data) in enumerate(((le, xe), (lo, xo))):
        mid = table_dot(table, data)
        rows = slice(odd * HALF, (odd + 1) * HALF)
        for part in (re_half, im_half):
            first, second = mid[part, re_half], mid[part, im_half]
            put_split(ze, rows, part, first + second)
            put_split(zo, rows, part, first - second)

    for odd, (table, data, kept) in enumerate(((let, ze, xe), (lot, zo, xo))):
        far = dot_table(data, table)
        far_re, far_im = far[:, re_half], far[:, im_half]
        power = far_re * far_re + far_im * far_im
        factor = amp_s[:, odd * HALF : (odd + 1) * HALF] * lax.rsqrt(
            jnp.maximum(power, amp_floor * amp_floor)
        )
        put_split(kept, slice(0, SIDE), re_half, far_re * factor)
        put_split(kept, slice(0, SIDE), im_half, far_im * factor)

    even = dot_table(xe, le)
    odds = dot_table(xo, lo)
    for c, part in enumerate((re_half, im_half)):
        first, second = even[:, part], odds[:, part]
        for side, value in enumerate((first + second, first - second)):
            lanes = slice(side * HALF, (side + 1) * HALF)
            rows = slice(c * HALF, (c + 1) * HALF)
            put_split(ze, rows, lanes, value[:HALF])
            put_split(zo, rows, lanes, value[HALF:])
    even = table_dot(let, ze)
    odds = table_dot(lot, zo)

    for start in range(0, HALF, step):
        for side in range(2):
            lanes = slice(side * HALF, (side + 1) * HALF)
            first = [even[c * HALF + start : c * HALF + start + step, lanes] for c in range(2)]
            second = [odds[c * HALF + start : c * HALF + start + step, lanes] for c in range(2)]
            for lower in range(2):
                begin = start + lower * HALF
                rows = slice(begin, begin + step)
                change = []
                for c in range(2):
                    back = first[c] - second[c] if lower else first[c] + second[c]
                    change.append(back - wave_s[c, rows, lanes])
                p = [pc[c, rows, lanes] for c in range(2)]
                piece = [piece_s[c, rows, lanes] for c in range(2)]
                numer = [
                    p[0] * change[0] + p[1] * change[1],
                    p[0] * change[1] - p[1] * change[0],
                ]
                turned = [
                    piece[0] * change[0] + piece[1] * change[1],
                    piece[0] * change[1] - piece[1] * change[0],
                ]
                for c in range(2):
                    grow[c, side, rows, :] = turned[c]
                    here = jnp.where(lane_in[side], numer[c], 0.0)
                    there = numer[c] - here
                    if begin == 0:
                        grow[c, side, SIDE:BAND, :] = turned[c]
                        for total, value in ((numer_own, here), (numer_next, there)):
                            inside = jnp.where(row_in, value, 0.0)
                            total[c, rows, lanes] += inside
                            total[c, SIDE:BAND, lanes] += value - inside
                    else:
                        numer_own[c, rows, lanes] += here
                        numer_next[c, rows, lanes] += there

    back_left = lax.rem(SIDE - left, SIDE)
    step = 64
    for c in range(2):
        for start in range(0, SIDE, step):
            pair = [grow[c, side, pl.ds(top + start, step), :] for side in range(2)]
            value = pltpu.roll(jnp.concatenate(pair, 1), back_left, 1)
            for side in range(2):
                begin = (2 * c + side) * SIDE + start
                grad[begin : begin + step, :] += value[:, side * HALF : (side + 1) * HALF]


def patch_terms(rows, cols, own, halo, probe, amplitudes):
    count = amplitudes.shape[1]
    tables, sorter = half_tables()
    whole = lambda *shape: pl.BlockSpec(shape, lambda k: (0,) * len(shape))
    scalars = pl.BlockSpec(memory_space=pltpu.SMEM)
    band = whole(2, BAND, SIDE)
    f32, bf16 = jnp.float32, jnp.bfloat16
    split = pltpu.VMEM((2, SIDE, SIDE), bf16)
    return pl.pallas_call(
        patch_kernel,
        grid=(count,),
        in_specs=[scalars, scalars, band, band, whole(2, SIDE, SIDE)]
        + [whole(2, SIDE, SIDE)] * 4
        + [whole(SIDE, SIDE), pl.BlockSpec((1, 1, SIDE, SIDE), lambda k: (0, k, 0, 0))],
        out_specs=[band, band, whole(GRAD_ROWS, HALF)],
        out_shape=[
            jax.ShapeDtypeStruct((2, BAND, SIDE), f32),
            jax.ShapeDtypeStruct((2, BAND, SIDE), f32),
            jax.ShapeDtypeStruct((GRAD_ROWS, HALF), f32),
        ],
        scratch_shapes=[
            pltpu.VMEM((2, 2, BAND, HALF), f32),
            pltpu.VMEM((2, SIDE, SIDE), f32),
            pltpu.VMEM((2, SIDE, SIDE), f32),
            pltpu.VMEM((2, SIDE, SIDE), f32),
            pltpu.VMEM((2, 2, BAND, HALF), f32),
            split, split, split, split,
            pltpu.VMEM((SIDE, SIDE), f32),
            pltpu.VMEM((2, SIDE, HALF), f32),
        ],
        compiler_params=pltpu.CompilerParams(
            dimension_semantics=("arbitrary",), vmem_limit_bytes=VMEM_BYTES
        ),
        cost_estimate=pl.CostEstimate(
            flops=count * 26 * 2 * SIDE**3, bytes_accessed=6 * 2**20, transcendentals=0
        ),
        name="patch_terms",
    )(rows, cols, own, halo, probe, *[jnp.asarray(t) for t in tables], jnp.asarray(sorter), amplitudes)


def weight_kernel(rows_s, cols_s, rows_b, cols_b, probe, out, power, prow):
    count = rows_s.shape[1]
    power[...] = probe[0] * probe[0] + probe[1] * probe[1]
    out[...] = jnp.full_like(out, ridge)
    step = 16
    row_id = lax.broadcasted_iota(jnp.int32, (step, HALF), 0)
    lane_id = lax.broadcasted_iota(jnp.int32, (step, HALF), 1)

    def place(top, left, behind):
        rolled_probe(power, prow, left)
        row_in = row_id >= top
        for side in range(2):
            lanes = slice(side * HALF, (side + 1) * HALF)
            lane_in = lane_id + side * HALF >= left
            if behind:
                lane_in = jnp.logical_not(lane_in)
            for start in range(0, SIDE, step):
                value = prow[side, pl.ds(SPILL - top + start, step), :]
                value = jnp.where(lane_in, value, 0.0)
                if start == 0:
                    inside = jnp.where(row_in, value, 0.0)
                    out[SIDE:BAND, lanes] += value - inside
                    value = inside
                out[start : start + step, lanes] += value

    def body(slot, carry):
        place(rows_s[0, slot], cols_s[0, slot], False)
        place(rows_b[0, slot], cols_b[0, slot], True)
        return carry

    lax.fori_loop(0, count, body, 0)
    out[...] = 1.0 / out[...]


def weight_inverse(rows, cols, rows_behind, cols_behind, probe):
    scalars = pl.BlockSpec(memory_space=pltpu.SMEM)
    vmem = pl.BlockSpec(memory_space=pltpu.VMEM)
    return pl.pallas_call(
        weight_kernel,
        in_specs=[scalars] * 4 + [vmem],
        out_specs=vmem,
        out_shape=jax.ShapeDtypeStruct((BAND, SIDE), jnp.float32),
        scratch_shapes=[
            pltpu.VMEM((SIDE, SIDE), jnp.float32),
            pltpu.VMEM((2, BAND, HALF), jnp.float32),
        ],
        compiler_params=pltpu.CompilerParams(vmem_limit_bytes=VMEM_BYTES),
        cost_estimate=pl.CostEstimate(flops=2**24, bytes_accessed=2**20, transcendentals=0),
        name="weight_inverse",
    )(rows, cols, rows_behind, cols_behind, probe)


def sum_kernel(
    term, out, r1, a1, r2, a2, r3, r4, a4, f2, f1, f0,
    s1, v1, s2, v2, s3, v3, s4, v4, s5, v5, s6, v6, s7, v7,
):
    phase, space = lax.axis_index("phase"), lax.axis_index("space")
    core = lax.rem(phase, CORES)
    z = lax.rem(phase // CORES, Z_SIZE)
    x_lo = phase // (CORES * Z_SIZE)
    y = lax.rem(space, Y_SIZE)
    x_hi = space // Y_SIZE
    x = x_hi * X_LO + x_lo

    def device(core_=core, z_=z, x_=x, y_=y):
        phase_ = (lax.rem(x_, X_LO) * Z_SIZE + z_) * CORES + core_
        return (phase_, (x_ // X_LO) * Y_SIZE + y_)

    def core_peer():
        return device(core_=1 - core)

    def x_peer(k):
        return device(x_=lax.rem(x + k, X_SIZE))

    def y_peer(k):
        return device(y_=lax.rem(y + k, Y_SIZE))

    def z_peer(k):
        return device(z_=lax.rem(z + k, Z_SIZE))

    def send(src, dst, s, v, target):
        return pltpu.make_async_remote_copy(
            src_ref=src, dst_ref=dst, send_sem=s, recv_sem=v,
            device_id=target, device_id_type=pl.DeviceIdType.MESH,
        )

    barrier = pltpu.get_barrier_semaphore()

    def greet(target):
        pl.semaphore_signal(barrier, inc=1, device_id=target, device_id_type=pl.DeviceIdType.MESH)

    greet(core_peer())
    for k in range(1, X_SIZE):
        greet(x_peer(k))
    for k in range(1, Y_SIZE):
        greet(y_peer(k))

    def greet_z(k, carry):
        greet(z_peer(k))
        return carry

    lax.fori_loop(1, Z_SIZE, greet_z, 0)
    pl.semaphore_wait(barrier, 1 + (X_SIZE - 1) + (Y_SIZE - 1) + (Z_SIZE - 1))

    part1 = GRAD_ROWS // CORES
    part2 = part1 // X_SIZE
    part3 = part2 // Z_SIZE

    def span(index, size):
        return pl.ds(pl.multiple_of(index * size, size), size)

    copy = send(term.at[span(1 - core, part1)], r1, s1, v1, core_peer())
    copy.start()
    copy.wait()
    a1[...] = term[span(core, part1), :] + r1[...]

    copies = []
    for k in range(1, X_SIZE):
        target = lax.rem(x + k, X_SIZE)
        copies.append(
            send(a1.at[span(target, part2)], r2.at[k - 1], s2.at[k - 1], v2.at[k - 1], x_peer(k))
        )
    for copy in copies:
        copy.start()
    for copy in copies:
        copy.wait()
    a2[...] = a1[span(x, part2), :] + r2[0] + r2[1] + r2[2]

    def z_sum(k):
        target = lax.rem(z + k, Z_SIZE)
        return send(a2.at[span(target, part3)], r3.at[k - 1], s3.at[k - 1], v3.at[k - 1], z_peer(k))

    def start_z_sum(k, carry):
        z_sum(k).start()
        return carry

    def wait_z_sum(k, carry):
        z_sum(k).wait()
        return carry

    lax.fori_loop(1, Z_SIZE, start_z_sum, 0)
    lax.fori_loop(1, Z_SIZE, wait_z_sum, 0)
    total = a2[span(z, part3), :]
    for k in range(Z_SIZE - 1):
        total = total + r3[k]

    r4[y] = total
    copies = [
        send(r4.at[y], r4.at[y], s4.at[k - 1], v4.at[k - 1], y_peer(k)) for k in range(1, Y_SIZE)
    ]
    for copy in copies:
        copy.start()
    for copy in copies:
        copy.wait()
    a4[...] = ((r4[0] + r4[1]) + (r4[2] + r4[3])) * (
        1.0 / math.sqrt(6 * lax.axis_size("phase") * lax.axis_size("space"))
    )

    f2[span(z, part3), :] = a4[...]

    def z_spread(k):
        return send(a4, f2.at[span(z, part3)], s5.at[k - 1], v5.at[k - 1], z_peer(k))

    def start_z_spread(k, carry):
        z_spread(k).start()
        return carry

    def wait_z_spread(k, carry):
        z_spread(k).wait()
        return carry

    lax.fori_loop(1, Z_SIZE, start_z_spread, 0)
    lax.fori_loop(1, Z_SIZE, wait_z_spread, 0)

    copies = [
        send(f2, f1.at[span(x, part2)], s6.at[k - 1], v6.at[k - 1], x_peer(k))
        for k in range(1, X_SIZE)
    ]
    for copy in copies:
        copy.start()
    f1[span(x, part2), :] = f2[...]
    for copy in copies:
        copy.wait()

    copy = send(f1, f0.at[span(core, part1)], s7, v7, core_peer())
    copy.start()
    f0[span(core, part1), :] = f1[...]
    copy.wait()
    for c in range(2):
        for side in range(2):
            begin = (2 * c + side) * SIDE
            out[c, :, side * HALF : (side + 1) * HALF] = f0[begin : begin + SIDE, :]


def summed_everywhere(term):
    part1 = GRAD_ROWS // CORES
    part2 = part1 // X_SIZE
    part3 = part2 // Z_SIZE
    f32 = jnp.float32
    dma = pltpu.SemaphoreType.DMA
    vmem = pl.BlockSpec(memory_space=pltpu.VMEM)
    sems = []
    for count in (1, X_SIZE - 1, Z_SIZE - 1, Y_SIZE - 1, Z_SIZE - 1, X_SIZE - 1, 1):
        sems += [dma if count == 1 else dma((count,))] * 2
    return pl.pallas_call(
        sum_kernel,
        in_specs=[vmem],
        out_specs=vmem,
        out_shape=jax.ShapeDtypeStruct((2, SIDE, SIDE), f32),
        scratch_shapes=[
            pltpu.VMEM((part1, HALF), f32),
            pltpu.VMEM((part1, HALF), f32),
            pltpu.VMEM((X_SIZE - 1, part2, HALF), f32),
            pltpu.VMEM((part2, HALF), f32),
            pltpu.VMEM((Z_SIZE - 1, part3, HALF), f32),
            pltpu.VMEM((Y_SIZE, part3, HALF), f32),
            pltpu.VMEM((part3, HALF), f32),
            pltpu.VMEM((part2, HALF), f32),
            pltpu.VMEM((part1, HALF), f32),
            pltpu.VMEM((GRAD_ROWS, HALF), f32),
            *sems,
        ],
        compiler_params=pltpu.CompilerParams(
            collective_id=0, has_side_effects=True, vmem_limit_bytes=VMEM_BYTES
        ),
        cost_estimate=pl.CostEstimate(flops=2**20, bytes_accessed=2**24, transcendentals=0),
        name="summed_everywhere",
    )(term)


def shards(object_field, split_field, scaled_dual, probe, amplitudes, row_offsets, col_offsets):
    own = object_field[:, 0]
    split_own = split_field[:, 0]
    dual_own = scaled_dual[:, 0]
    halo = from_behind(own, "space", -1)
    next_object = passed_along(own, "phase", -1)
    start_point = own + split_own - dual_own
    start_prev = passed_along(start_point, "phase", 1)
    offsets_behind = from_behind(jnp.concatenate([row_offsets, col_offsets], 0), "space", 1)
    inverse = weight_inverse(
        row_offsets, col_offsets, offsets_behind[:1], offsets_behind[1:], probe
    )
    numer_own, numer_next, grad = patch_terms(
        row_offsets, col_offsets, own, halo, probe, amplitudes
    )
    incoming = from_behind(numer_next, "space", 1)
    probe_gradient = summed_everywhere(grad)
    steady = own - tv_step * ((own - start_prev) - (next_object - start_point))
    updated = steady + (numer_own + incoming) * inverse[None]
    next_updated = passed_along(updated, "phase", -1)
    joint = next_updated - updated + dual_own
    size_abs = jnp.sqrt(joint[0] * joint[0] + joint[1] * joint[1])
    shrink = jnp.maximum(size_abs - shrink_level, 0.0) / jnp.maximum(size_abs, shrink_level)
    new_split = joint * shrink[None]
    new_dual = joint - new_split
    return (updated[:, None], new_split[:, None], new_dual[:, None], probe_gradient)


def solution(mesh):
    in_specs = (
        P(None, "phase", None, "space"),
        P(None, "phase", None, "space"),
        P(None, "phase", None, "space"),
        P(),
        P("phase", "space", None, None),
        P("phase", "space"),
        P("phase", "space"),
    )
    out_specs = (
        P(None, "phase", None, "space"),
        P(None, "phase", None, "space"),
        P(None, "phase", None, "space"),
        P(),
    )
    return jax.shard_map(shards, mesh=mesh, in_specs=in_specs, out_specs=out_specs, check_vma=False)
```

time: 688 us -> 115 us (0.17)
  waiting for transfers between devices: 464 us -> 6.36 us
  Pallas kernels: 0 us -> 75.1 us
  local copies, waits for them, and re-layouts: 68.6 us -> 2.55 us
  matrix products: 63.2 us -> 0 us
  between operations: 37.2 us -> 0.91 us
  other arithmetic: 18.4 us -> 3.16 us
    psum x1 -> x0, waiting for transfers between devices: 459 us -> none  [shards(): summed = lax.psum(jnp.stack([grad_re, grad_im]), ('phase', 'space'))]
    pallas_call x0 -> x3, Pallas kernels: none -> 75.1 us  [the longest x1 56.4 us: summed_everywhere(): pl.pallas_call(sum_kernel, in_specs=[vmem], out_specs=vmem, out_shape=jax...]
    dot_general x16 -> x0, matrix products: 63.2 us -> none  [the longest x2 9.25 us: transform(): jnp.einsum('bjk,kl->bjl', left_re, sine, precision=highest)]
    dynamic_update_slice x12 -> x0, local copies, waits for them, and re-layouts: 63 us -> none  [the longest x6 41.6 us: shards(): accum = lax.dynamic_update_slice(accum, current + addition, corner)]
    add x14 -> x1, other arithmetic: 10.7 us -> 0.27 us  [shards(): updated = steady + (numer_own + incoming) * inverse[None]]
  transfers between devices with their start and end apart: 7 -> 6, of which waited for: 2 -> 1; matrix products, arithmetic and copies ran while one was open for 22% -> 1% of each run, Pallas kernels for 0% -> 65%
where the time goes in v1:
time: 115 us
  Pallas kernels  75.1 us (65%)
  starting transfers between devices  26.7 us (23%)
  waiting for transfers between devices  6.36 us (6%)
  other arithmetic  3.16 us (3%)
  local copies, waits for them, and re-layouts  2.55 us (2%)
    pallas_call x1, Pallas kernels, summed_everywhere(): pl.pallas_call(sum_kernel, in_specs=[vmem], out_specs=vmem, out_shape=jax...  56.4 us
    pallas_call x1, Pallas kernels, patch_terms(): pl.pallas_call(patch_kernel, grid=(count,), in_specs=[scalars, scalars, b...  16.6 us
    ppermute x3, starting transfers between devices, passed_along(): return lax.ppermute(value, axis, pairs)  16 us
    ppermute x3, starting transfers between devices, from_behind(): return lax.ppermute(block, axis, route)  10.7 us
    ppermute x3, waiting for transfers between devices, from_behind(): return lax.ppermute(block, axis, route)  6.35 us
    unnamed x25, local copies, waits for them, and re-layouts  2.55 us
  transfers between devices with their start and end apart: 6, of which 1 were waited for; matrix products, arithmetic and copies ran while one was open for 1% of the time, Pallas kernels for 65%

profile of v1, /device:TPU:1, one launch (start us, length us, event | category | flops | bytes accessed | tf_op | source)
XLA Modules:
  0.0 114.8 jit_solution(15915384836819250330)
XLA Ops:
  0.6 0.0 copy-start.4
  0.6 0.0 copy-start.5
  0.7 0.0 copy-start.6
  0.7 0.0 copy-start.7
  0.7 1.4 %collective-permute-start.2 = (f32[2,272,256]{2,1,0:T(8,128)}, f32[2,272,256]{2,1,0:T(8,128)S(1)}, u32[]{:S(2)}, u32[]{:S(2)}) collective-permute-start(f32[2,272,256]{2,1,0:T(8,128)} %bitcast.23), channel_id=1, source_target_pairs={{1,0},{2,1},{3,2},{4,3},{5,4},{6,5},{7,6},{9,8},{10,9},{11,10},{12... | collective-permute-start | bytes 1671176 | tf_op jit(solution)/shard_map/ppermute | solution.py:30
  2.2 8.8 %collective-permute-start.1 = (f32[2,272,256]{2,1,0:T(8,128)}, f32[2,272,256]{2,1,0:T(8,128)S(1)}, u32[]{:S(2)}, u32[]{:S(2)}) collective-permute-start(f32[2,272,256]{2,1,0:T(8,128)} %bitcast.24), channel_id=1, source_target_pairs={{0,504},{8,0},{16,8},{24,16},{32,24},{40,32},{48,40},{56,48},{64,5... | collective-permute-start | bytes 1671176 | tf_op jit(solution)/shard_map/ppermute | solution.py:36
  10.9 1.5 %bitcast_subtract_fusion = f32[2,272,256]{2,1,0:T(8,128)S(1)} fusion(f32[2,1,272,256]{3,2,1,0:T(8,128)} %param.14, f32[2,1,272,256]{3,2,1,0:T(8,128)} %param.13, f32[2,1,272,256]{3,2,1,0:T(8,128)} %param.12), kind=kLoop, calls=%fused_computation.4 | loop fusion | flops 278528 | bytes 2228224 | tf_op jit(solution)/shard_map/sub | solution.py:506
  12.4 1.9 %collective-permute-start = (f32[2,272,256]{2,1,0:T(8,128)S(1)}, f32[2,272,256]{2,1,0:T(8,128)S(1)}, u32[]{:S(2)}, u32[]{:S(2)}) collective-permute-start(f32[2,272,256]{2,1,0:T(8,128)S(1)} %bitcast_subtract_fusion), channel_id=1, source_target_pairs={{0,8},{8,16},{16,24},{24,32},{32,40},{40,48},{48,56},{56,64},{64,7... | collective-permute-start | bytes 1671176 | tf_op jit(solution)/shard_map/ppermute | solution.py:36
  14.4 0.8 copy-done.11
  15.2 0.0 copy-start.8
  15.3 0.9 copy-done.8
  16.2 16.6 %patch_terms.1 = (f32[2,272,256]{2,1,0:T(8,128)S(1)}, f32[2,272,256]{2,1,0:T(8,128)S(1)}, f32[1024,128]{1,0:T(8,128)S(1)}) custom-call(s32[1,6]{1,0:T(1,128)S(1)} %copy-done.2, s32[1,6]{1,0:T(1,128)S(1)} %copy-done.3, f32[2,272,256]{2,1,0:T(8,128)S(1)} %bitcast.25, f32[2,272,256]{2,1,0:T(8,128)} %copy-done.11, f32[2,256,256]{2,1,0:T(8,128)S(1)} %copy-done.1, ...), custom_call_target="tpu_custom_call" | custom-call | flops 5234491392 | bytes 6291456 | tf_op jit(solution)/shard_map/patch_terms/pallas_call | solution.py:238
  32.8 6.2 %collective-permute-start.3 = (f32[2,272,256]{2,1,0:T(8,128)S(1)}, f32[2,272,256]{2,1,0:T(8,128)S(1)}, u32[]{:S(2)}, u32[]{:S(2)}) collective-permute-start(f32[2,272,256]{2,1,0:T(8,128)S(1)} %get-tuple-element.8), channel_id=1, source_target_pairs={{0,1},{1,2},{2,3},{3,4},{4,5},{5,6},{6,7},{8,9},{9,10},{10,11},{11... | collective-permute-start | bytes 1671176 | tf_op jit(solution)/shard_map/ppermute | solution.py:30
  39.0 3.1 %collective-permute-start.4 = (s32[2,6]{1,0:T(2,128)S(1)}, s32[2,6]{1,0:T(2,128)S(1)}, u32[]{:S(2)}, u32[]{:S(2)}) collective-permute-start(s32[2,6]{1,0:T(2,128)S(1)} %pad_add_fusion), channel_id=1, source_target_pairs={{0,1},{1,2},{2,3},{3,4},{4,5},{5,6},{6,7},{8,9},{9,10},{10,11},{11... | collective-permute-start | bytes 152 | tf_op jit(solution)/shard_map/ppermute | solution.py:30
  42.1 6.3 %collective-permute-done.4 = s32[2,6]{1,0:T(2,128)S(1)} collective-permute-done((s32[2,6]{1,0:T(2,128)S(1)}, s32[2,6]{1,0:T(2,128)S(1)}, u32[]{:S(2)}, u32[]{:S(2)}) %collective-permute-start.4) | collective-permute-done | bytes 80 | tf_op jit(solution)/shard_map/ppermute | solution.py:30
  48.4 2.1 %weight_inverse.1 = f32[272,256]{1,0:T(8,128)S(1)} custom-call(s32[1,6]{1,0:T(1,128)S(1)} %copy-done.2, s32[1,6]{1,0:T(1,128)S(1)} %copy-done.3, s32[1,6]{1,0:T(1,128)S(1)} %get-tuple-element.17.rows_b, s32[1,6]{1,0:T(1,128)S(1)} %get-tuple-element.16.cols_b, f32[2,256,256]{2,1,0:T(8,128)S(1)} %copy-done.1), custom_call_target="tpu_custom_call" | custom-call | flops 16777216 | bytes 1048576 | tf_op jit(solution)/shard_map/weight_inverse/pallas_call | solution.py:307
  50.6 0.3 multiply_add_fusion
  50.9 0.0 copy-start.10
  50.9 5.2 %collective-permute-start.5 = (f32[2,272,256]{2,1,0:T(8,128)S(1)}, f32[2,272,256]{2,1,0:T(8,128)S(1)}, u32[]{:S(2)}, u32[]{:S(2)}) collective-permute-start(f32[2,272,256]{2,1,0:T(8,128)S(1)} %multiply_add_fusion), channel_id=1, source_target_pairs={{0,504},{8,0},{16,8},{24,16},{32,24},{40,32},{48,40},{56,48},{64,5... | collective-permute-start | bytes 1671176 | tf_op jit(solution)/shard_map/ppermute | solution.py:36
  56.2 56.4 %summed_everywhere.1 = f32[2,256,256]{2,1,0:T(8,128)S(1)} custom-call(f32[1024,128]{1,0:T(8,128)S(1)} %get-tuple-element.9.term), custom_call_target="tpu_custom_call" | custom-call | flops 1048576 | bytes 16777216 | tf_op jit(solution)/shard_map/summed_everywhere/pallas_call | solution.py:474
  112.6 0.1 bitcast_add_fusion
  112.7 0.1 divide_bitcast_fusion
  112.9 1.1 fusion
  114.0 0.8 copy.20
  (23 shorter events, 0.1 us)
Async XLA Ops:
  0.6 14.6 %copy-start.4 = (bf16[2,256,256]{2,1,0:T(8,128)(2,1)S(1)}, bf16[2,256,256]{2,1,0:T(8,128)(2,1)}, u32[]{:S(2)}) copy-start(bf16[2,256,256]{2,1,0:T(8,128)(2,1)} %constant.18.clone.le) | copy-start | bytes 786436
  0.6 14.6 %copy-start.5 = (bf16[2,256,256]{2,1,0:T(8,128)(2,1)S(1)}, bf16[2,256,256]{2,1,0:T(8,128)(2,1)}, u32[]{:S(2)}) copy-start(bf16[2,256,256]{2,1,0:T(8,128)(2,1)} %constant.19.clone.let) | copy-start | bytes 786436
  0.7 14.5 %copy-start.6 = (bf16[2,256,256]{2,1,0:T(8,128)(2,1)S(1)}, bf16[2,256,256]{2,1,0:T(8,128)(2,1)}, u32[]{:S(2)}) copy-start(bf16[2,256,256]{2,1,0:T(8,128)(2,1)} %constant.20.clone.lo) | copy-start | bytes 786436
  0.7 14.5 %copy-start.7 = (bf16[2,256,256]{2,1,0:T(8,128)(2,1)S(1)}, bf16[2,256,256]{2,1,0:T(8,128)(2,1)}, u32[]{:S(2)}) copy-start(bf16[2,256,256]{2,1,0:T(8,128)(2,1)} %constant.21.clone.lot) | copy-start | bytes 786436
  0.7 14.5 %copy-start = (f32[2,1,272,256]{3,2,1,0:T(8,128)S(1)}, f32[2,1,272,256]{3,2,1,0:T(8,128)}, u32[]{:S(2)}) copy-start(f32[2,1,272,256]{3,2,1,0:T(8,128)} %param.12) | copy-start | bytes 1671172
  0.7 14.5 %copy-start.2 = (s32[1,6]{1,0:T(1,128)S(1)}, s32[1,6]{1,0:T(1,128)}, u32[]{:S(2)}) copy-start(s32[1,6]{1,0:T(1,128)} %rows_s.3) | copy-start | bytes 76
  0.7 14.5 %copy-start.3 = (s32[1,6]{1,0:T(1,128)S(1)}, s32[1,6]{1,0:T(1,128)}, u32[]{:S(2)}) copy-start(s32[1,6]{1,0:T(1,128)} %cols_s.3) | copy-start | bytes 76
  0.7 14.5 %copy-start.1 = (f32[2,256,256]{2,1,0:T(8,128)S(1)}, f32[2,256,256]{2,1,0:T(8,128)}, u32[]{:S(2)}) copy-start(f32[2,256,256]{2,1,0:T(8,128)} %probe.3) | copy-start | bytes 1572868
  0.7 13.7 %collective-permute-start.2 = (f32[2,272,256]{2,1,0:T(8,128)}, f32[2,272,256]{2,1,0:T(8,128)S(1)}, u32[]{:S(2)}, u32[]{:S(2)}) collective-permute-start(f32[2,272,256]{2,1,0:T(8,128)} %bitcast.23), channel_id=1, source_target_pairs={{1,0},{2,1},{3,2},{4,3},{5,4},{6,5},{7,6},{9,8},{10,9},{11,10},{12... | collective-permute-start | bytes 1671176 | tf_op jit(solution)/shard_map/ppermute | solution.py:30
  2.2 48.4 %collective-permute-start.1 = (f32[2,272,256]{2,1,0:T(8,128)}, f32[2,272,256]{2,1,0:T(8,128)S(1)}, u32[]{:S(2)}, u32[]{:S(2)}) collective-permute-start(f32[2,272,256]{2,1,0:T(8,128)} %bitcast.24), channel_id=1, source_target_pairs={{0,504},{8,0},{16,8},{24,16},{32,24},{40,32},{48,40},{56,48},{64,5... | collective-permute-start | bytes 1671176 | tf_op jit(solution)/shard_map/ppermute | solution.py:36
  12.4 38.2 %collective-permute-start = (f32[2,272,256]{2,1,0:T(8,128)S(1)}, f32[2,272,256]{2,1,0:T(8,128)S(1)}, u32[]{:S(2)}, u32[]{:S(2)}) collective-permute-start(f32[2,272,256]{2,1,0:T(8,128)S(1)} %bitcast_subtract_fusion), channel_id=1, source_target_pairs={{0,8},{8,16},{16,24},{24,32},{32,40},{40,48},{48,56},{56,64},{64,7... | collective-permute-start | bytes 1671176 | tf_op jit(solution)/shard_map/ppermute | solution.py:36
  14.4 0.8 copy-start.11
  15.2 0.9 copy-start.8
  32.8 17.9 %collective-permute-start.3 = (f32[2,272,256]{2,1,0:T(8,128)S(1)}, f32[2,272,256]{2,1,0:T(8,128)S(1)}, u32[]{:S(2)}, u32[]{:S(2)}) collective-permute-start(f32[2,272,256]{2,1,0:T(8,128)S(1)} %get-tuple-element.8), channel_id=1, source_target_pairs={{0,1},{1,2},{2,3},{3,4},{4,5},{5,6},{6,7},{8,9},{9,10},{10,11},{11... | collective-permute-start | bytes 1671176 | tf_op jit(solution)/shard_map/ppermute | solution.py:30
  39.0 9.5 %collective-permute-start.4 = (s32[2,6]{1,0:T(2,128)S(1)}, s32[2,6]{1,0:T(2,128)S(1)}, u32[]{:S(2)}, u32[]{:S(2)}) collective-permute-start(s32[2,6]{1,0:T(2,128)S(1)} %pad_add_fusion), channel_id=1, source_target_pairs={{0,1},{1,2},{2,3},{3,4},{4,5},{5,6},{6,7},{8,9},{9,10},{10,11},{11... | collective-permute-start | bytes 152 | tf_op jit(solution)/shard_map/ppermute | solution.py:30
  50.6 62.0 %copy-start.9 = (f32[2,1,272,256]{3,2,1,0:T(8,128)S(1)}, f32[2,1,272,256]{3,2,1,0:T(8,128)}, u32[]{:S(2)}) copy-start(f32[2,1,272,256]{3,2,1,0:T(8,128)} %param.14) | copy-start | bytes 1671172
  50.9 61.8 %copy-start.10 = (f32[2,272,256]{2,1,0:T(8,128)}, f32[2,272,256]{2,1,0:T(8,128)S(1)}, u32[]{:S(2)}) copy-start(f32[2,272,256]{2,1,0:T(8,128)S(1)} %multiply_add_fusion) | copy-start | bytes 1671172
  50.9 61.6 %collective-permute-start.5 = (f32[2,272,256]{2,1,0:T(8,128)S(1)}, f32[2,272,256]{2,1,0:T(8,128)S(1)}, u32[]{:S(2)}, u32[]{:S(2)}) collective-permute-start(f32[2,272,256]{2,1,0:T(8,128)S(1)} %multiply_add_fusion), channel_id=1, source_target_pairs={{0,504},{8,0},{16,8},{24,16},{32,24},{40,32},{48,40},{56,48},{64,5... | collective-permute-start | bytes 1671176 | tf_op jit(solution)/shard_map/ppermute | solution.py:36

commit v2 on v1

--- a/solution.py
+++ b/solution.py
@@ -1,4 +1,3 @@
-import functools
 import math
 
 import jax
@@ -21,19 +20,9 @@
 SPILL = BAND - SIDE
 CORES, Z_SIZE, X_LO, Y_SIZE, X_SIZE = 2, 16, 2, 4, 4
 GRAD_ROWS = 1024
+TILES = X_SIZE // X_LO * Y_SIZE
+PATCHES = 6
 VMEM_BYTES = 50 * 1024 * 1024
-
-
-def from_behind(block, axis, distance):
-    devices = range(lax.axis_size(axis))
-    route = [(i - distance, i) for i in devices if i - distance in devices]
-    return lax.ppermute(block, axis, route)
-
-
-def passed_along(value, axis, steps):
-    count = lax.axis_size(axis)
-    pairs = [(source, (source + steps) % count) for source in range(count)]
-    return lax.ppermute(value, axis, pairs)
 
 
 def two_parts(table):
@@ -89,9 +78,9 @@
 
 
 def patch_kernel(
-    rows_s, cols_s, own, halo, probe, le, let, lo, lot, sorter, amp,
-    numer_own, numer_next, grad,
-    prow, pc, piece_s, wave_s, grow, xe, xo, ze, zo, amp_s, amp_c,
+    rows_s, cols_s, behind, own, halo, probe, le, let, lo, lot, sorter, amp,
+    numer_own, numer_next, grad, weight,
+    power, brow, prow, pc, piece_s, wave_s, grow, xe, xo, ze, zo, amp_s, amp_c,
 ):
     slot = pl.program_id(0)
     top = rows_s[0, slot]
@@ -102,9 +91,14 @@
         numer_own[...] = jnp.zeros_like(numer_own)
         numer_next[...] = jnp.zeros_like(numer_next)
         grad[...] = jnp.zeros_like(grad)
+        weight[...] = jnp.full_like(weight, ridge)
+        power[...] = probe[0] * probe[0] + probe[1] * probe[1]
 
     rolled_probe(probe.at[0], prow.at[0], left)
     rolled_probe(probe.at[1], prow.at[1], left)
+    top_b = behind[0, slot]
+    left_b = behind[1, slot]
+    rolled_probe(power, brow, left_b)
 
     for side in range(2):
         amp_c[side] = amp[0, 0, :, side * HALF : (side + 1) * HALF]
@@ -119,6 +113,7 @@
     lane_id = lax.broadcasted_iota(jnp.int32, (step, HALF), 1)
     row_in = row_id >= top
     lane_in = [lane_id + side * HALF >= left for side in range(2)]
+    lane_behind = [lane_id + side * HALF < left_b for side in range(2)]
 
     def wave_rows(start, side):
         rows = slice(start, start + step)
@@ -137,6 +132,15 @@
         wave = [p[0] * piece[0] - p[1] * piece[1], p[0] * piece[1] + p[1] * piece[0]]
         for c in range(2):
             wave_s[c, rows, lanes] = wave[c]
+        mine = jnp.where(lane_in[side], p[0] * p[0] + p[1] * p[1], 0.0)
+        theirs = brow[side, pl.ds(SPILL - top_b + start, step), :]
+        theirs = jnp.where(lane_behind[side], theirs, 0.0)
+        if start == 0:
+            mine_in = jnp.where(row_in, mine, 0.0)
+            theirs_in = jnp.where(row_id >= top_b, theirs, 0.0)
+            weight[SIDE:BAND, lanes] += (mine - mine_in) + (theirs - theirs_in)
+            mine, theirs = mine_in, theirs_in
+        weight[rows, lanes] += mine + theirs
         return wave
 
     for start in range(0, HALF, step):
@@ -226,8 +230,12 @@
                 begin = (2 * c + side) * SIDE + start
                 grad[begin : begin + step, :] += value[:, side * HALF : (side + 1) * HALF]
 
-
-def patch_terms(rows, cols, own, halo, probe, amplitudes):
+    @pl.when(slot == pl.num_programs(0) - 1)
+    def _():
+        weight[...] = 1.0 / weight[...]
+
+
+def patch_terms(rows, cols, behind, own, halo, probe, amplitudes):
     count = amplitudes.shape[1]
     tables, sorter = half_tables()
     whole = lambda *shape: pl.BlockSpec(shape, lambda k: (0,) * len(shape))
@@ -238,16 +246,19 @@
     return pl.pallas_call(
         patch_kernel,
         grid=(count,),
-        in_specs=[scalars, scalars, band, band, whole(2, SIDE, SIDE)]
+        in_specs=[scalars, scalars, scalars, band, band, whole(2, SIDE, SIDE)]
         + [whole(2, SIDE, SIDE)] * 4
         + [whole(SIDE, SIDE), pl.BlockSpec((1, 1, SIDE, SIDE), lambda k: (0, k, 0, 0))],
-        out_specs=[band, band, whole(GRAD_ROWS, HALF)],
+        out_specs=[band, band, whole(GRAD_ROWS, HALF), whole(BAND, SIDE)],
         out_shape=[
             jax.ShapeDtypeStruct((2, BAND, SIDE), f32),
             jax.ShapeDtypeStruct((2, BAND, SIDE), f32),
             jax.ShapeDtypeStruct((GRAD_ROWS, HALF), f32),
+            jax.ShapeDtypeStruct((BAND, SIDE), f32),
         ],
         scratch_shapes=[
+            pltpu.VMEM((SIDE, SIDE), f32),
+            pltpu.VMEM((2, BAND, HALF), f32),
             pltpu.VMEM((2, 2, BAND, HALF), f32),
             pltpu.VMEM((2, SIDE, SIDE), f32),
             pltpu.VMEM((2, SIDE, SIDE), f32),
@@ -264,112 +275,224 @@
             flops=count * 26 * 2 * SIDE**3, bytes_accessed=6 * 2**20, transcendentals=0
         ),
         name="patch_terms",
-    )(rows, cols, own, halo, probe, *[jnp.asarray(t) for t in tables], jnp.asarray(sorter), amplitudes)
-
-
-def weight_kernel(rows_s, cols_s, rows_b, cols_b, probe, out, power, prow):
-    count = rows_s.shape[1]
-    power[...] = probe[0] * probe[0] + probe[1] * probe[1]
-    out[...] = jnp.full_like(out, ridge)
-    step = 16
-    row_id = lax.broadcasted_iota(jnp.int32, (step, HALF), 0)
-    lane_id = lax.broadcasted_iota(jnp.int32, (step, HALF), 1)
-
-    def place(top, left, behind):
-        rolled_probe(power, prow, left)
-        row_in = row_id >= top
-        for side in range(2):
-            lanes = slice(side * HALF, (side + 1) * HALF)
-            lane_in = lane_id + side * HALF >= left
-            if behind:
-                lane_in = jnp.logical_not(lane_in)
-            for start in range(0, SIDE, step):
-                value = prow[side, pl.ds(SPILL - top + start, step), :]
-                value = jnp.where(lane_in, value, 0.0)
-                if start == 0:
-                    inside = jnp.where(row_in, value, 0.0)
-                    out[SIDE:BAND, lanes] += value - inside
-                    value = inside
-                out[start : start + step, lanes] += value
-
-    def body(slot, carry):
-        place(rows_s[0, slot], cols_s[0, slot], False)
-        place(rows_b[0, slot], cols_b[0, slot], True)
-        return carry
-
-    lax.fori_loop(0, count, body, 0)
-    out[...] = 1.0 / out[...]
-
-
-def weight_inverse(rows, cols, rows_behind, cols_behind, probe):
-    scalars = pl.BlockSpec(memory_space=pltpu.SMEM)
+    )(rows, cols, behind, own, halo, probe, *[jnp.asarray(t) for t in tables], jnp.asarray(sorter), amplitudes)
+
+
+class Place:
+    def __init__(self):
+        self.phase, self.space = lax.axis_index("phase"), lax.axis_index("space")
+        self.core = lax.rem(self.phase, CORES)
+        self.z = lax.rem(self.phase // CORES, Z_SIZE)
+        x_lo = self.phase // (CORES * Z_SIZE)
+        self.y = lax.rem(self.space, Y_SIZE)
+        self.x_hi = self.space // Y_SIZE
+        self.x = self.x_hi * X_LO + x_lo
+
+    def device(self, core, z, x, y):
+        phase = (lax.rem(x, X_LO) * Z_SIZE + z) * CORES + core
+        return (phase, (x // X_LO) * Y_SIZE + y)
+
+    def core_peer(self):
+        return self.device(1 - self.core, self.z, self.x, self.y)
+
+    def x_peer(self, k):
+        return self.device(self.core, self.z, lax.rem(self.x + k, X_SIZE), self.y)
+
+    def y_peer(self, k):
+        return self.device(self.core, self.z, self.x, lax.rem(self.y + k, Y_SIZE))
+
+    def z_peer(self, k):
+        return self.device(self.core, lax.rem(self.z + k, Z_SIZE), self.x, self.y)
+
+    def bin_at(self, k):
+        count = lax.axis_size("phase")
+        return (lax.rem(self.phase + k + count, count), self.space)
+
+    def tile_at(self, k):
+        count = lax.axis_size("space")
+        return (self.phase, lax.rem(self.space + k + count, count))
+
+
+def remote(src, dst, s, v, target):
+    return pltpu.make_async_remote_copy(
+        src_ref=src, dst_ref=dst, send_sem=s, recv_sem=v,
+        device_id=target, device_id_type=pl.DeviceIdType.MESH,
+    )
+
+
+def greet(target):
+    pl.semaphore_signal(
+        pltpu.get_barrier_semaphore(), inc=1, device_id=target, device_id_type=pl.DeviceIdType.MESH
+    )
+
+
+CHUNKS = 4
+CHUNK_ROWS = BAND // 2
+
+
+def chunk_of(ref, index):
+    return ref.at[index // 2, pl.ds((index % 2) * CHUNK_ROWS, CHUNK_ROWS), :]
+
+
+def opening_kernel(
+    own, split, dual, rows, cols,
+    halo, steady, behind,
+    start_point, following, preceding, offsets,
+    hs, hv, rs, ns, nv, ps, pv, os, ov,
+):
+    me = Place()
+    last = TILES - 1
+    for target in (me.tile_at(1), me.tile_at(-1), me.tile_at(TILES // 2), me.bin_at(1), me.bin_at(-1)):
+        greet(target)
+    greet(me.device(me.core, me.z, me.x, Y_SIZE - 1 - me.y))
+    start_point[...] = own[...] + split[...] - dual[...]
+    offsets[...] = jnp.zeros_like(offsets)
+    offsets[0:1, 0 : rows.shape[1]] = rows[...]
+    offsets[1:2, 0 : cols.shape[1]] = cols[...]
+
+    @pl.when(me.space == 0)
+    def _():
+        behind[...] = jnp.zeros_like(behind)
+
+    pl.semaphore_wait(pltpu.get_barrier_semaphore(), 6)
+
+    def halo_copy(index):
+        target = me.tile_at(-1) if index < CHUNKS // 2 else me.y_peer(Y_SIZE - 1)
+        return remote(chunk_of(own, index), chunk_of(halo, index), hs.at[index], hv.at[index], target)
+
+    def relay(index):
+        place = chunk_of(halo, index)
+        return remote(place, place, rs.at[index - CHUNKS // 2], hv.at[index], me.tile_at(TILES // 2))
+
+    order = (2, 0, 3, 1)
+
+    @pl.when(me.space > 0)
+    def _():
+        for index in order:
+            halo_copy(index).start()
+
+    to_preceding = remote(own, following, ns, nv, me.bin_at(-1))
+    to_following = remote(start_point, preceding, ps, pv, me.bin_at(1))
+    offsets_on = remote(offsets, behind, os, ov, me.tile_at(1))
+    to_preceding.start()
+    to_following.start()
+
+    @pl.when(me.space < last)
+    def _():
+        offsets_on.start()
+
+    @pl.when(me.space == last)
+    def _():
+        for index in (2, 3):
+            halo_copy(index).wait_recv()
+            relay(index).start()
+
+    to_preceding.wait()
+    to_following.wait()
+    steady[...] = own[...] - tv_step * (
+        (own[...] - preceding[...]) - (following[...] - start_point[...])
+    )
+
+    @pl.when(me.space > 0)
+    def _():
+        offsets_on.wait_recv()
+        for index in order:
+            halo_copy(index).wait_send()
+
+    @pl.when(me.space < last)
+    def _():
+        offsets_on.wait_send()
+        for index in order:
+            halo_copy(index).wait_recv()
+
+    @pl.when(me.space == last)
+    def _():
+        for index in (2, 3):
+            relay(index).wait_send()
+
+
+def opening(own, split, dual, rows, cols):
+    f32, i32 = jnp.float32, jnp.int32
+    dma = pltpu.SemaphoreType.DMA
     vmem = pl.BlockSpec(memory_space=pltpu.VMEM)
+    band = jax.ShapeDtypeStruct((2, BAND, SIDE), f32)
     return pl.pallas_call(
-        weight_kernel,
-        in_specs=[scalars] * 4 + [vmem],
-        out_specs=vmem,
-        out_shape=jax.ShapeDtypeStruct((BAND, SIDE), jnp.float32),
+        opening_kernel,
+        in_specs=[vmem] * 5,
+        out_specs=[vmem] * 3,
+        out_shape=[band, band, jax.ShapeDtypeStruct((8, HALF), i32)],
         scratch_shapes=[
-            pltpu.VMEM((SIDE, SIDE), jnp.float32),
-            pltpu.VMEM((2, BAND, HALF), jnp.float32),
+            pltpu.VMEM((2, BAND, SIDE), f32),
+            pltpu.VMEM((2, BAND, SIDE), f32),
+            pltpu.VMEM((2, BAND, SIDE), f32),
+            pltpu.VMEM((8, HALF), i32),
+            dma((CHUNKS,)), dma((CHUNKS,)), dma((CHUNKS // 2,)),
+            dma, dma, dma, dma, dma, dma,
         ],
-        compiler_params=pltpu.CompilerParams(vmem_limit_bytes=VMEM_BYTES),
-        cost_estimate=pl.CostEstimate(flops=2**24, bytes_accessed=2**20, transcendentals=0),
-        name="weight_inverse",
-    )(rows, cols, rows_behind, cols_behind, probe)
-
-
-def sum_kernel(
-    term, out, r1, a1, r2, a2, r3, r4, a4, f2, f1, f0,
+        compiler_params=pltpu.CompilerParams(
+            collective_id=0, has_side_effects=True, vmem_limit_bytes=VMEM_BYTES
+        ),
+        cost_estimate=pl.CostEstimate(flops=2**20, bytes_accessed=2**24, transcendentals=0),
+        name="opening",
+    )(own, split, dual, rows, cols)
+
+
+def tail_kernel(
+    numer_own, numer_next, inverse, steady, term,
+    updated, next_updated, out,
+    inc, r1, a1, r2, a2, r3, r4, a4, f2, f1, f0,
+    cs, cv, rs, us, uv,
     s1, v1, s2, v2, s3, v3, s4, v4, s5, v5, s6, v6, s7, v7,
 ):
-    phase, space = lax.axis_index("phase"), lax.axis_index("space")
-    core = lax.rem(phase, CORES)
-    z = lax.rem(phase // CORES, Z_SIZE)
-    x_lo = phase // (CORES * Z_SIZE)
-    y = lax.rem(space, Y_SIZE)
-    x_hi = space // Y_SIZE
-    x = x_hi * X_LO + x_lo
-
-    def device(core_=core, z_=z, x_=x, y_=y):
-        phase_ = (lax.rem(x_, X_LO) * Z_SIZE + z_) * CORES + core_
-        return (phase_, (x_ // X_LO) * Y_SIZE + y_)
-
-    def core_peer():
-        return device(core_=1 - core)
-
-    def x_peer(k):
-        return device(x_=lax.rem(x + k, X_SIZE))
-
-    def y_peer(k):
-        return device(y_=lax.rem(y + k, Y_SIZE))
-
-    def z_peer(k):
-        return device(z_=lax.rem(z + k, Z_SIZE))
-
-    def send(src, dst, s, v, target):
-        return pltpu.make_async_remote_copy(
-            src_ref=src, dst_ref=dst, send_sem=s, recv_sem=v,
-            device_id=target, device_id_type=pl.DeviceIdType.MESH,
+    me = Place()
+    core, x, y, z = me.core, me.x, me.y, me.z
+    last = TILES - 1
+
+    greet(me.core_peer())
+    for k in range(1, X_SIZE):
+        greet(me.x_peer(k))
+    for k in range(1, Y_SIZE):
+        greet(me.y_peer(k))
+    for target in (me.tile_at(1), me.tile_at(-1), me.bin_at(1), me.bin_at(-1)):
+        greet(target)
+
+    def greet_z(k, carry):
+        greet(me.z_peer(k))
+        return carry
+
+    lax.fori_loop(1, Z_SIZE, greet_z, 0)
+    pl.semaphore_wait(
+        pltpu.get_barrier_semaphore(), 1 + (X_SIZE - 1) + (Y_SIZE - 1) + 4 + (Z_SIZE - 1)
+    )
+
+    def correction(index):
+        target = me.tile_at(1) if index < CHUNKS // 2 else me.y_peer(1)
+        return remote(
+            chunk_of(numer_next, index), chunk_of(inc, index), cs.at[index], cv.at[index], target
         )
 
-    barrier = pltpu.get_barrier_semaphore()
-
-    def greet(target):
-        pl.semaphore_signal(barrier, inc=1, device_id=target, device_id_type=pl.DeviceIdType.MESH)
-
-    greet(core_peer())
-    for k in range(1, X_SIZE):
-        greet(x_peer(k))
-    for k in range(1, Y_SIZE):
-        greet(y_peer(k))
-
-    def greet_z(k, carry):
-        greet(z_peer(k))
-        return carry
-
-    lax.fori_loop(1, Z_SIZE, greet_z, 0)
-    pl.semaphore_wait(barrier, 1 + (X_SIZE - 1) + (Y_SIZE - 1) + (Z_SIZE - 1))
+    def relay(index):
+        place = chunk_of(inc, index)
+        return remote(place, place, rs.at[index - CHUNKS // 2], cv.at[index], me.tile_at(TILES // 2))
+
+    def updated_copy(index):
+        return remote(
+            chunk_of(updated, index), chunk_of(next_updated, index), us.at[index], uv.at[index],
+            me.bin_at(-1),
+        )
+
+    order = (2, 0, 3, 1)
+
+    @pl.when(me.space < last)
+    def _():
+        for index in order:
+            correction(index).start()
+
+    def relay_on(index):
+        @pl.when(me.space == 0)
+        def _():
+            correction(index).wait_recv()
+            relay(index).start()
 
     part1 = GRAD_ROWS // CORES
     part2 = part1 // X_SIZE
@@ -378,7 +501,7 @@
     def span(index, size):
         return pl.ds(pl.multiple_of(index * size, size), size)
 
-    copy = send(term.at[span(1 - core, part1)], r1, s1, v1, core_peer())
+    copy = remote(term.at[span(1 - core, part1)], r1, s1, v1, me.core_peer())
     copy.start()
     copy.wait()
     a1[...] = term[span(core, part1), :] + r1[...]
@@ -387,17 +510,18 @@
     for k in range(1, X_SIZE):
         target = lax.rem(x + k, X_SIZE)
         copies.append(
-            send(a1.at[span(target, part2)], r2.at[k - 1], s2.at[k - 1], v2.at[k - 1], x_peer(k))
+            remote(a1.at[span(target, part2)], r2.at[k - 1], s2.at[k - 1], v2.at[k - 1], me.x_peer(k))
         )
     for copy in copies:
         copy.start()
+    relay_on(2)
     for copy in copies:
         copy.wait()
     a2[...] = a1[span(x, part2), :] + r2[0] + r2[1] + r2[2]
 
     def z_sum(k):
         target = lax.rem(z + k, Z_SIZE)
-        return send(a2.at[span(target, part3)], r3.at[k - 1], s3.at[k - 1], v3.at[k - 1], z_peer(k))
+        return remote(a2.at[span(target, part3)], r3.at[k - 1], s3.at[k - 1], v3.at[k - 1], me.z_peer(k))
 
     def start_z_sum(k, carry):
         z_sum(k).start()
@@ -408,6 +532,7 @@
         return carry
 
     lax.fori_loop(1, Z_SIZE, start_z_sum, 0)
+    relay_on(3)
     lax.fori_loop(1, Z_SIZE, wait_z_sum, 0)
     total = a2[span(z, part3), :]
     for k in range(Z_SIZE - 1):
@@ -415,20 +540,19 @@
 
     r4[y] = total
     copies = [
-        send(r4.at[y], r4.at[y], s4.at[k - 1], v4.at[k - 1], y_peer(k)) for k in range(1, Y_SIZE)
+        remote(r4.at[y], r4.at[y], s4.at[k - 1], v4.at[k - 1], me.y_peer(k)) for k in range(1, Y_SIZE)
     ]
     for copy in copies:
         copy.start()
     for copy in copies:
         copy.wait()
-    a4[...] = ((r4[0] + r4[1]) + (r4[2] + r4[3])) * (
-        1.0 / math.sqrt(6 * lax.axis_size("phase") * lax.axis_size("space"))
-    )
+    count = PATCHES * lax.axis_size("phase") * lax.axis_size("space")
+    a4[...] = ((r4[0] + r4[1]) + (r4[2] + r4[3])) * (1.0 / math.sqrt(count))
 
     f2[span(z, part3), :] = a4[...]
 
     def z_spread(k):
-        return send(a4, f2.at[span(z, part3)], s5.at[k - 1], v5.at[k - 1], z_peer(k))
+        return remote(a4, f2.at[span(z, part3)], s5.at[k - 1], v5.at[k - 1], me.z_peer(k))
 
     def start_z_spread(k, carry):
         z_spread(k).start()
@@ -439,10 +563,26 @@
         return carry
 
     lax.fori_loop(1, Z_SIZE, start_z_spread, 0)
+
+    for index in order:
+        part, rows = index // 2, pl.ds((index % 2) * CHUNK_ROWS, CHUNK_ROWS)
+
+        @pl.when(me.space > 0)
+        def _():
+            correction(index).wait_recv()
+            numer = numer_own[part, rows, :] + inc[part, rows, :]
+            updated[part, rows, :] = steady[part, rows, :] + numer * inverse[rows, :]
+
+        @pl.when(me.space == 0)
+        def _():
+            updated[part, rows, :] = steady[part, rows, :] + numer_own[part, rows, :] * inverse[rows, :]
+
+        updated_copy(index).start()
+
     lax.fori_loop(1, Z_SIZE, wait_z_spread, 0)
 
     copies = [
-        send(f2, f1.at[span(x, part2)], s6.at[k - 1], v6.at[k - 1], x_peer(k))
+        remote(f2, f1.at[span(x, part2)], s6.at[k - 1], v6.at[k - 1], me.x_peer(k))
         for k in range(1, X_SIZE)
     ]
     for copy in copies:
@@ -451,7 +591,7 @@
     for copy in copies:
         copy.wait()
 
-    copy = send(f1, f0.at[span(core, part1)], s7, v7, core_peer())
+    copy = remote(f1, f0.at[span(core, part1)], s7, v7, me.core_peer())
     copy.start()
     f0[span(core, part1), :] = f1[...]
     copy.wait()
@@ -460,23 +600,38 @@
             begin = (2 * c + side) * SIDE
             out[c, :, side * HALF : (side + 1) * HALF] = f0[begin : begin + SIDE, :]
 
-
-def summed_everywhere(term):
+    for index in order:
+        updated_copy(index).wait()
+
+    @pl.when(me.space < last)
+    def _():
+        for index in order:
+            correction(index).wait_send()
+
+    @pl.when(me.space == 0)
+    def _():
+        for index in (2, 3):
+            relay(index).wait_send()
+
+
+def tail(numer_own, numer_next, inverse, steady, term):
     part1 = GRAD_ROWS // CORES
     part2 = part1 // X_SIZE
     part3 = part2 // Z_SIZE
     f32 = jnp.float32
     dma = pltpu.SemaphoreType.DMA
     vmem = pl.BlockSpec(memory_space=pltpu.VMEM)
+    band = jax.ShapeDtypeStruct((2, BAND, SIDE), f32)
     sems = []
     for count in (1, X_SIZE - 1, Z_SIZE - 1, Y_SIZE - 1, Z_SIZE - 1, X_SIZE - 1, 1):
         sems += [dma if count == 1 else dma((count,))] * 2
     return pl.pallas_call(
-        sum_kernel,
-        in_specs=[vmem],
-        out_specs=vmem,
-        out_shape=jax.ShapeDtypeStruct((2, SIDE, SIDE), f32),
+        tail_kernel,
+        in_specs=[vmem] * 5,
+        out_specs=[vmem] * 3,
+        out_shape=[band, band, jax.ShapeDtypeStruct((2, SIDE, SIDE), f32)],
         scratch_shapes=[
+            pltpu.VMEM((2, BAND, SIDE), f32),
             pltpu.VMEM((part1, HALF), f32),
             pltpu.VMEM((part1, HALF), f32),
             pltpu.VMEM((X_SIZE - 1, part2, HALF), f32),
@@ -487,41 +642,59 @@
             pltpu.VMEM((part2, HALF), f32),
             pltpu.VMEM((part1, HALF), f32),
             pltpu.VMEM((GRAD_ROWS, HALF), f32),
+            dma((CHUNKS,)), dma((CHUNKS,)), dma((CHUNKS // 2,)), dma((CHUNKS,)), dma((CHUNKS,)),
             *sems,
         ],
         compiler_params=pltpu.CompilerParams(
-            collective_id=0, has_side_effects=True, vmem_limit_bytes=VMEM_BYTES
+            collective_id=1, has_side_effects=True, vmem_limit_bytes=VMEM_BYTES
         ),
         cost_estimate=pl.CostEstimate(flops=2**20, bytes_accessed=2**24, transcendentals=0),
-        name="summed_everywhere",
-    )(term)
+        name="tail",
+    )(numer_own, numer_next, inverse, steady, term)
+
+
+def finish_kernel(updated, next_updated, dual, summed, out_object, out_split, out_dual, out_sum):
+    out_object[...] = updated[...]
+    out_sum[...] = summed[...]
+    joint = [next_updated[c] - updated[c] + dual[c] for c in range(2)]
+    size_abs = jnp.sqrt(joint[0] * joint[0] + joint[1] * joint[1])
+    shrink = jnp.maximum(size_abs - shrink_level, 0.0) / jnp.maximum(size_abs, shrink_level)
+    for c in range(2):
+        new_split = joint[c] * shrink
+        out_split[c] = new_split
+        out_dual[c] = joint[c] - new_split
+
+
+def finish(updated, next_updated, dual, summed):
+    steps = 2
+    f32 = jnp.float32
+    band = pl.BlockSpec((2, BAND // steps, SIDE), lambda i: (0, i, 0))
+    grad = pl.BlockSpec((2, SIDE // steps, SIDE), lambda i: (0, i, 0))
+    band_shape = jax.ShapeDtypeStruct((2, BAND, SIDE), f32)
+    return pl.pallas_call(
+        finish_kernel,
+        grid=(steps,),
+        in_specs=[band, band, band, grad],
+        out_specs=[band, band, band, grad],
+        out_shape=[band_shape] * 3 + [jax.ShapeDtypeStruct((2, SIDE, SIDE), f32)],
+        compiler_params=pltpu.CompilerParams(
+            dimension_semantics=("arbitrary",), vmem_limit_bytes=VMEM_BYTES
+        ),
+        cost_estimate=pl.CostEstimate(flops=2**20, bytes_accessed=2**22, transcendentals=0),
+        name="finish",
+    )(updated, next_updated, dual, summed)
 
 
 def shards(object_field, split_field, scaled_dual, probe, amplitudes, row_offsets, col_offsets):
     own = object_field[:, 0]
     split_own = split_field[:, 0]
     dual_own = scaled_dual[:, 0]
-    halo = from_behind(own, "space", -1)
-    next_object = passed_along(own, "phase", -1)
-    start_point = own + split_own - dual_own
-    start_prev = passed_along(start_point, "phase", 1)
-    offsets_behind = from_behind(jnp.concatenate([row_offsets, col_offsets], 0), "space", 1)
-    inverse = weight_inverse(
-        row_offsets, col_offsets, offsets_behind[:1], offsets_behind[1:], probe
+    halo, steady, behind = opening(own, split_own, dual_own, row_offsets, col_offsets)
+    numer_own, numer_next, grad, inverse = patch_terms(
+        row_offsets, col_offsets, behind, own, halo, probe, amplitudes
     )
-    numer_own, numer_next, grad = patch_terms(
-        row_offsets, col_offsets, own, halo, probe, amplitudes
-    )
-    incoming = from_behind(numer_next, "space", 1)
-    probe_gradient = summed_everywhere(grad)
-    steady = own - tv_step * ((own - start_prev) - (next_object - start_point))
-    updated = steady + (numer_own + incoming) * inverse[None]
-    next_updated = passed_along(updated, "phase", -1)
-    joint = next_updated - updated + dual_own
-    size_abs = jnp.sqrt(joint[0] * joint[0] + joint[1] * joint[1])
-    shrink = jnp.maximum(size_abs - shrink_level, 0.0) / jnp.maximum(size_abs, shrink_level)
-    new_split = joint * shrink[None]
-    new_dual = joint - new_split
+    updated, next_updated, summed = tail(numer_own, numer_next, inverse, steady, grad)
+    updated, new_split, new_dual, probe_gradient = finish(updated, next_updated, dual_own, summed)
     return (updated[:, None], new_split[:, None], new_dual[:, None], probe_gradient)
 
 

time: 115 us -> 98.2 us (0.85)
  starting transfers between devices: 26.7 us -> 0 us
  Pallas kernels: 75.1 us -> 90.9 us
  waiting for transfers between devices: 6.36 us -> 0 us
  local copies, waits for them, and re-layouts: 2.55 us -> 6.21 us
  other arithmetic: 3.16 us -> 0 us
    ppermute x6 -> x0, starting transfers between devices: 26.7 us -> none  [the longest x3 16 us: passed_along(): return lax.ppermute(value, axis, pairs)]
    pallas_call x3 -> x4, Pallas kernels: 75.1 us -> 90.9 us  [the longest x1 55.2 us: tail(): pl.pallas_call(tail_kernel, in_specs=[vmem] * 5, out_specs=[vmem] * 3, ou...]
    ppermute x6 -> x0, waiting for transfers between devices: 6.36 us -> none  [the longest x3 6.35 us: from_behind(): return lax.ppermute(block, axis, route)]
    unnamed x25 -> x30, local copies, waits for them, and re-layouts: 2.55 us -> 6.21 us
    sub x1 -> x0, other arithmetic: 1.5 us -> none  [shards(): start_point = own + split_own - dual_own]
  transfers between devices with their start and end apart: 6 -> 0, of which waited for: 1 -> 0; matrix products, arithmetic and copies ran while one was open for 1% -> 0% of each run, Pallas kernels for 65% -> 0%
where the time goes in v2:
time: 98.2 us; the launch traced here: 97.9 us
  Pallas kernels  90.9 us (93%)
  local copies, waits for them, and re-layouts  6.21 us (6%)
    pallas_call x1, Pallas kernels, tail(): pl.pallas_call(tail_kernel, in_specs=[vmem] * 5, out_specs=[vmem] * 3, ou...  55.2 us
    pallas_call x1, Pallas kernels, opening(): pl.pallas_call(opening_kernel, in_specs=[vmem] * 5, out_specs=[vmem] * 3,...  17.1 us
    pallas_call x1, Pallas kernels, patch_terms(): pl.pallas_call(patch_kernel, grid=(count,), in_specs=[scalars, scalars, s...  16.9 us
    unnamed x30, local copies, waits for them, and re-layouts  6.21 us

profile of v2, /device:TPU:1, one launch (start us, length us, event | category | flops | bytes accessed | tf_op | source)
XLA Modules:
  0.0 97.9 jit_solution(6308938889248969699)
XLA Ops:
  0.6 0.0 copy-start.7
  0.6 0.0 copy-start.5
  0.7 0.0 copy-start
  0.7 1.1 %copy-done = f32[2,1,272,256]{3,2,1,0:T(8,128)S(1)} copy-done((f32[2,1,272,256]{3,2,1,0:T(8,128)S(1)}, f32[2,1,272,256]{3,2,1,0:T(8,128)}, u32[]{:S(2)}) %copy-start) | copy-done | bytes 557080
  1.7 1.1 %copy-done.2 = f32[2,1,272,256]{3,2,1,0:T(8,128)S(1)} copy-done((f32[2,1,272,256]{3,2,1,0:T(8,128)S(1)}, f32[2,1,272,256]{3,2,1,0:T(8,128)}, u32[]{:S(2)}) %copy-start.2) | copy-done | bytes 557080
  2.8 1.1 %copy-done.3 = f32[2,1,272,256]{3,2,1,0:T(8,128)S(1)} copy-done((f32[2,1,272,256]{3,2,1,0:T(8,128)S(1)}, f32[2,1,272,256]{3,2,1,0:T(8,128)}, u32[]{:S(2)}) %copy-start.3) | copy-done | bytes 557080
  3.8 0.7 copy-done.4
  4.5 0.7 copy-done.6
  5.1 0.0 copy-start.13
  5.2 17.1 %opening.1 = (f32[2,272,256]{2,1,0:T(8,128)S(1)}, f32[2,272,256]{2,1,0:T(8,128)S(1)}, s32[8,128]{1,0:T(8,128)S(1)}) custom-call(f32[2,272,256]{2,1,0:T(8,128)S(1)} %bitcast.16, f32[2,272,256]{2,1,0:T(8,128)S(1)} %bitcast.14, f32[2,272,256]{2,1,0:T(8,128)S(1)} %bitcast.12, s32[1,6]{1,0:T(1,128)S(1)} %copy-done.4, s32[1,6]{1,0:T(1,128)S(1)} %copy-done.6), custom_call_target="tpu_custom_call" | custom-call | flops 1048576 | bytes 16777216 | tf_op jit(solution)/shard_map/opening/pallas_call | solution.py:419
  22.3 0.0 copy-start.8
  22.3 0.8 copy-done.8
  23.1 0.0 copy-done.7
  23.1 0.0 copy-done.5
  23.1 0.0 copy-done.9
  23.1 0.0 copy-done.10
  23.1 0.0 copy-done.11
  23.1 0.0 copy-done.12
  23.1 0.0 copy-start.14
  23.2 0.9 copy-done.14
  24.1 16.9 %patch_terms.1 = (f32[2,272,256]{2,1,0:T(8,128)S(1)}, f32[2,272,256]{2,1,0:T(8,128)S(1)}, f32[1024,128]{1,0:T(8,128)S(1)}, f32[272,256]{1,0:T(8,128)S(1)}) custom-call(s32[1,6]{1,0:T(1,128)S(1)} %copy-done.5, s32[1,6]{1,0:T(1,128)S(1)} %copy-done.7, s32[8,128]{1,0:T(8,128)S(1)} %get-tuple-element.18.behind, f32[2,272,256]{2,1,0:T(8,128)} %bitcast.15, ...), custom_call_target="tpu_custom_call" | custom-call | flops 5234491392 | bytes 6291456 | tf_op jit(solution)/shard_map/patch_terms/pallas_call | solution.py:246
  41.0 0.0 copy-start.1
  41.0 55.2 %tail.1 = (f32[2,272,256]{2,1,0:T(8,128)S(1)}, f32[2,272,256]{2,1,0:T(8,128)S(1)}, f32[2,256,256]{2,1,0:T(8,128)S(1)}) custom-call(f32[2,272,256]{2,1,0:T(8,128)S(1)} %get-tuple-element.20.numer_own, f32[2,272,256]{2,1,0:T(8,128)S(1)} %get-tuple-element.21.numer_next, f32[272,256]{1,0:T(8,128)S(1)} %get-tuple-element.22.inverse, ...), custom_call_target="tpu_custom_call" | custom-call | flops 1048576 | bytes 16777216 | tf_op jit(solution)/shard_map/tail/pallas_call | solution.py:628
  96.2 1.7 %finish.1 = (f32[2,272,256]{2,1,0:T(8,128)}, f32[2,272,256]{2,1,0:T(8,128)}, f32[2,272,256]{2,1,0:T(8,128)}, f32[2,256,256]{2,1,0:T(8,128)}) custom-call(f32[2,272,256]{2,1,0:T(8,128)S(1)} %get-tuple-element.25.updated, f32[2,272,256]{2,1,0:T(8,128)S(1)} %get-tuple-element.26.next_updated, f32[2,272,256]{2,1,0:T(8,128)S(1)} %bitcast.13, ...), custom_call_target="tpu_custom_call" | custom-call | flops 1048576 | bytes 4194304 | tf_op jit(solution)/shard_map/finish/pallas_call | solution.py:674
  (10 shorter events, 0.0 us)
Async XLA Ops:
  0.6 22.5 %copy-start.7 = (s32[1,6]{1,0:T(1,128)S(1)}, s32[1,6]{1,0:T(1,128)}, u32[]{:S(2)}) copy-start(s32[1,6]{1,0:T(1,128)} %cols_s.1) | copy-start | bytes 76
  0.6 22.5 %copy-start.5 = (s32[1,6]{1,0:T(1,128)S(1)}, s32[1,6]{1,0:T(1,128)}, u32[]{:S(2)}) copy-start(s32[1,6]{1,0:T(1,128)} %rows_s.1) | copy-start | bytes 76
  0.7 1.1 %copy-start = (f32[2,1,272,256]{3,2,1,0:T(8,128)S(1)}, f32[2,1,272,256]{3,2,1,0:T(8,128)}, u32[]{:S(2)}) copy-start(f32[2,1,272,256]{3,2,1,0:T(8,128)} %param.14) | copy-start | bytes 1671172
  1.7 1.1 %copy-start.2 = (f32[2,1,272,256]{3,2,1,0:T(8,128)S(1)}, f32[2,1,272,256]{3,2,1,0:T(8,128)}, u32[]{:S(2)}) copy-start(f32[2,1,272,256]{3,2,1,0:T(8,128)} %param.13) | copy-start | bytes 1671172
  2.8 1.1 %copy-start.3 = (f32[2,1,272,256]{3,2,1,0:T(8,128)S(1)}, f32[2,1,272,256]{3,2,1,0:T(8,128)}, u32[]{:S(2)}) copy-start(f32[2,1,272,256]{3,2,1,0:T(8,128)} %param.12) | copy-start | bytes 1671172
  3.8 0.7 copy-start.4
  4.5 0.7 copy-start.6
  5.1 18.0 %copy-start.9 = (f32[2,256,256]{2,1,0:T(8,128)S(1)}, f32[2,256,256]{2,1,0:T(8,128)}, u32[]{:S(2)}) copy-start(f32[2,256,256]{2,1,0:T(8,128)} %probe.1) | copy-start | bytes 1572868
  5.1 18.0 %copy-start.10 = (bf16[2,256,256]{2,1,0:T(8,128)(2,1)S(1)}, bf16[2,256,256]{2,1,0:T(8,128)(2,1)}, u32[]{:S(2)}) copy-start(bf16[2,256,256]{2,1,0:T(8,128)(2,1)} %constant.13.clone.lot) | copy-start | bytes 786436
  5.1 18.0 %copy-start.11 = (bf16[2,256,256]{2,1,0:T(8,128)(2,1)S(1)}, bf16[2,256,256]{2,1,0:T(8,128)(2,1)}, u32[]{:S(2)}) copy-start(bf16[2,256,256]{2,1,0:T(8,128)(2,1)} %constant.12.clone.lo) | copy-start | bytes 786436
  5.1 18.0 %copy-start.12 = (bf16[2,256,256]{2,1,0:T(8,128)(2,1)S(1)}, bf16[2,256,256]{2,1,0:T(8,128)(2,1)}, u32[]{:S(2)}) copy-start(bf16[2,256,256]{2,1,0:T(8,128)(2,1)} %constant.11.clone.let) | copy-start | bytes 786436
  5.1 18.0 %copy-start.13 = (bf16[2,256,256]{2,1,0:T(8,128)(2,1)S(1)}, bf16[2,256,256]{2,1,0:T(8,128)(2,1)}, u32[]{:S(2)}) copy-start(bf16[2,256,256]{2,1,0:T(8,128)(2,1)} %constant.10.clone.le) | copy-start | bytes 786436
  22.3 0.8 copy-start.8
  23.1 0.9 copy-start.14
  41.0 55.2 %copy-start.1 = (f32[2,1,272,256]{3,2,1,0:T(8,128)S(1)}, f32[2,1,272,256]{3,2,1,0:T(8,128)}, u32[]{:S(2)}) copy-start(f32[2,1,272,256]{3,2,1,0:T(8,128)} %param.14) | copy-start | bytes 1671172

commit v3 on v2

v3 whole, which is shorter than its diff:
```python
import math

import jax
import jax.numpy as jnp
import ml_dtypes
import numpy as np
from jax import lax
from jax.experimental import pallas as pl
from jax.experimental.pallas import tpu as pltpu
from jax.sharding import PartitionSpec as P

amp_floor = 0.25
ridge = 1.0
tv_step = 0.25
shrink_level = 0.5

SIDE = 256
HALF = 128
BAND = 272
SPILL = BAND - SIDE
CORES, Z_SIZE, X_LO, Y_SIZE, X_SIZE = 2, 16, 2, 4, 4
GRAD_ROWS = 1024
TILES = X_SIZE // X_LO * Y_SIZE
PATCHES = 6
VMEM_BYTES = 50 * 1024 * 1024
PATCH_VMEM_BYTES = 36 * 1024 * 1024
GROUP = 2


def two_parts(table):
    high = table.astype(ml_dtypes.bfloat16)
    low = (table - high.astype(np.float64)).astype(ml_dtypes.bfloat16)
    return np.stack([high, low])


def half_tables():
    place = np.arange(HALF)
    tables = []
    for odd in (0, 1):
        turns = ((2 * place[:, None] + odd) * place[None, :]) % SIDE
        angle = -2.0 * np.pi * turns / SIDE
        re = np.cos(angle) / math.sqrt(SIDE)
        im = np.sin(angle) / math.sqrt(SIDE)
        real_form = np.block([[re, -im], [im, re]])
        tables.append(two_parts(real_form))
        tables.append(two_parts(real_form.T))
    return tables


def put_split(ref, rows, lanes, value):
    high = value.astype(jnp.bfloat16)
    ref[0, rows, lanes] = high
    ref[1, rows, lanes] = (value - high.astype(jnp.float32)).astype(jnp.bfloat16)


def dot(a, b):
    return jnp.dot(a, b, preferred_element_type=jnp.float32)


def table_dot(table, data):
    high, low = table[0], table[1]
    return dot(
        jnp.concatenate([high, high, low], 1),
        jnp.concatenate([data[0], data[1], data[0]], 0),
    )


def dot_table(data, table):
    high, low = table[0], table[1]
    return dot(
        jnp.concatenate([data[0], data[1], data[0]], 1),
        jnp.concatenate([high, high, low], 0),
    )


def rolled_probe(source, target, left):
    step = 64
    for start in range(0, SIDE, step):
        turned = pltpu.roll(source[start : start + step, :], left, 1)
        for side in range(2):
            lanes = slice(side * HALF, (side + 1) * HALF)
            target[side, SPILL + start : SPILL + start + step, :] = turned[:, lanes]
            if start + step == SIDE:
                target[side, 0:SPILL, :] = turned[step - SPILL :, lanes]


def patch_kernel(
    rows_s, cols_s, behind, own, halo, probe, le, let, lo, lot, amp,
    numer_own, numer_next, grad, weight,
    power, sorter, *scratch,
):
    first_slot = pl.program_id(0) * GROUP
    step = 16
    row_id = lax.broadcasted_iota(jnp.int32, (step, HALF), 0)
    lane_id = lax.broadcasted_iota(jnp.int32, (step, HALF), 1)
    re_half, im_half = slice(0, HALF), slice(HALF, SIDE)

    @pl.when(pl.program_id(0) == 0)
    def _():
        numer_own[...] = jnp.zeros_like(numer_own)
        numer_next[...] = jnp.zeros_like(numer_next)
        grad[...] = jnp.zeros_like(grad)
        weight[...] = jnp.full_like(weight, ridge)
        power[...] = probe[0] * probe[0] + probe[1] * probe[1]
        place = lax.broadcasted_iota(jnp.int32, (SIDE, SIDE), 0)
        target = lax.broadcasted_iota(jnp.int32, (SIDE, SIDE), 1)
        source = jnp.where(target < HALF, 2 * target, 2 * (target - HALF) + 1)
        sorter[...] = jnp.where(place == source, 1.0, 0.0).astype(jnp.bfloat16)

    def stages(member):
        brow, prow, pc, piece_s, wave_s, grow, xe, xo, ze, zo, amp_s, amp_c = scratch[
            member * 12 : member * 12 + 12
        ]
        slot = first_slot + member
        top, left = rows_s[0, slot], cols_s[0, slot]
        top_b, left_b = behind[0, slot], behind[1, slot]
        row_in = row_id >= top
        lane_in = [lane_id + side * HALF >= left for side in range(2)]
        lane_behind = [lane_id + side * HALF < left_b for side in range(2)]
        kept = {}

        def turn_probe():
            rolled_probe(probe.at[0], prow.at[0], left)
            rolled_probe(probe.at[1], prow.at[1], left)
            rolled_probe(power, brow, left_b)

        def sort_amplitudes():
            for side in range(2):
                amp_c[side] = amp[0, member, :, side * HALF : (side + 1) * HALF]
            for odd in range(2):
                part = jnp.concatenate(
                    [amp_c[side, pl.ds(odd, HALF, stride=2), :] for side in range(2)], 1
                )
                high = part.astype(jnp.bfloat16)
                low = (part - high.astype(jnp.float32)).astype(jnp.bfloat16)
                amp_s[odd * HALF : (odd + 1) * HALF, :] = dot(high, sorter[...]) + dot(low, sorter[...])

        def wave_rows(start, side):
            rows = slice(start, start + step)
            lanes = slice(side * HALF, (side + 1) * HALF)
            p = [prow[c, side, pl.ds(SPILL - top + start, step), :] for c in range(2)]
            piece = []
            for c in range(2):
                here = own[c, rows, lanes]
                there = halo[c, rows, lanes]
                if start == 0:
                    here = jnp.where(row_in, here, own[c, SIDE:BAND, lanes])
                    there = jnp.where(row_in, there, halo[c, SIDE:BAND, lanes])
                piece.append(jnp.where(lane_in[side], here, there))
                piece_s[c, rows, lanes] = piece[c]
                pc[c, rows, lanes] = p[c]
            wave = [p[0] * piece[0] - p[1] * piece[1], p[0] * piece[1] + p[1] * piece[0]]
            for c in range(2):
                wave_s[c, rows, lanes] = wave[c]
            mine = jnp.where(lane_in[side], p[0] * p[0] + p[1] * p[1], 0.0)
            theirs = brow[side, pl.ds(SPILL - top_b + start, step), :]
            theirs = jnp.where(lane_behind[side], theirs, 0.0)
            if start == 0:
                mine_in = jnp.where(row_in, mine, 0.0)
                theirs_in = jnp.where(row_id >= top_b, theirs, 0.0)
                weight[SIDE:BAND, lanes] += (mine - mine_in) + (theirs - theirs_in)
                mine, theirs = mine_in, theirs_in
            weight[rows, lanes] += mine + theirs
            return wave

        def waves():
            for start in range(0, HALF, step):
                for side in range(2):
                    lanes = slice(side * HALF, (side + 1) * HALF)
                    upper = wave_rows(start, side)
                    lower = wave_rows(start + HALF, side)
                    for c in range(2):
                        rows = slice(c * HALF + start, c * HALF + start + step)
                        put_split(xe, rows, lanes, upper[c] + lower[c])
                        put_split(xo, rows, lanes, upper[c] - lower[c])

        def over_rows(odd):
            mid = table_dot((le, lo)[odd], (xe, xo)[odd])
            rows = slice(odd * HALF, (odd + 1) * HALF)
            for part in (re_half, im_half):
                first, second = mid[part, re_half], mid[part, im_half]
                put_split(ze, rows, part, first + second)
                put_split(zo, rows, part, first - second)

        def over_columns(odd):
            far = dot_table((ze, zo)[odd], (let, lot)[odd])
            far_re, far_im = far[:, re_half], far[:, im_half]
            square = far_re * far_re + far_im * far_im
            factor = amp_s[:, odd * HALF : (odd + 1) * HALF] * lax.rsqrt(
                jnp.maximum(square, amp_floor * amp_floor)
            )
            put_split((xe, xo)[odd], slice(0, SIDE), re_half, far_re * factor)
            put_split((xe, xo)[odd], slice(0, SIDE), im_half, far_im * factor)

        def back_columns():
            even = dot_table(xe, le)
            odds = dot_table(xo, lo)
            for c, part in enumerate((re_half, im_half)):
                first, second = even[:, part], odds[:, part]
                for side, value in enumerate((first + second, first - second)):
                    lanes = slice(side * HALF, (side + 1) * HALF)
                    rows = slice(c * HALF, (c + 1) * HALF)
                    put_split(ze, rows, lanes, value[:HALF])
                    put_split(zo, rows, lanes, value[HALF:])

        def back_rows():
            kept["even"] = table_dot(let, ze)
            kept["odds"] = table_dot(lot, zo)

        def changes():
            even, odds = kept["even"], kept["odds"]
            for start in range(0, HALF, step):
                for side in range(2):
                    lanes = slice(side * HALF, (side + 1) * HALF)
                    spans = [slice(c * HALF + start, c * HALF + start + step) for c in range(2)]
                    first = [even[spans[c], lanes] for c in range(2)]
                    second = [odds[spans[c], lanes] for c in range(2)]
                    for lower in range(2):
                        begin = start + lower * HALF
                        rows = slice(begin, begin + step)
                        change = []
                        for c in range(2):
                            back = first[c] - second[c] if lower else first[c] + second[c]
                            change.append(back - wave_s[c, rows, lanes])
                        p = [pc[c, rows, lanes] for c in range(2)]
                        piece = [piece_s[c, rows, lanes] for c in range(2)]
                        numer = [
                            p[0] * change[0] + p[1] * change[1],
                            p[0] * change[1] - p[1] * change[0],
                        ]
                        turned = [
                            piece[0] * change[0] + piece[1] * change[1],
                            piece[0] * change[1] - piece[1] * change[0],
                        ]
                        for c in range(2):
                            grow[c, side, rows, :] = turned[c]
                            here = jnp.where(lane_in[side], numer[c], 0.0)
                            there = numer[c] - here
                            if begin == 0:
                                grow[c, side, SIDE:BAND, :] = turned[c]
                                for total, value in ((numer_own, here), (numer_next, there)):
                                    inside = jnp.where(row_in, value, 0.0)
                                    total[c, rows, lanes] += inside
                                    total[c, SIDE:BAND, lanes] += value - inside
                            else:
                                numer_own[c, rows, lanes] += here
                                numer_next[c, rows, lanes] += there

        def gradient():
            back_left = lax.rem(SIDE - left, SIDE)
            tall = 64
            for c in range(2):
                for start in range(0, SIDE, tall):
                    pair = [grow[c, side, pl.ds(top + start, tall), :] for side in range(2)]
                    value = pltpu.roll(jnp.concatenate(pair, 1), back_left, 1)
                    for side in range(2):
                        begin = (2 * c + side) * SIDE + start
                        grad[begin : begin + tall, :] += value[:, side * HALF : (side + 1) * HALF]

        return [
            turn_probe,
            waves,
            lambda: (over_rows(0), sort_amplitudes(), over_rows(1)),
            lambda: (over_columns(0), over_columns(1)),
            back_columns,
            back_rows,
            changes,
            gradient,
        ]

    ahead, after = stages(0), stages(1)
    lag = 3
    for turn in range(len(ahead) + lag):
        if turn < len(ahead):
            ahead[turn]()
        if turn >= lag:
            after[turn - lag]()

    @pl.when(pl.program_id(0) == pl.num_programs(0) - 1)
    def _():
        weight[...] = 1.0 / weight[...]


def patch_terms(rows, cols, behind, own, halo, probe, amplitudes):
    count = amplitudes.shape[1]
    tables = half_tables()
    whole = lambda *shape: pl.BlockSpec(shape, lambda k: (0,) * len(shape))
    scalars = pl.BlockSpec(memory_space=pltpu.SMEM)
    band = whole(2, BAND, SIDE)
    f32, bf16 = jnp.float32, jnp.bfloat16
    split = pltpu.VMEM((2, SIDE, SIDE), bf16)
    square = pltpu.VMEM((2, SIDE, SIDE), f32)
    member = [
        pltpu.VMEM((2, BAND, HALF), f32),
        pltpu.VMEM((2, 2, BAND, HALF), f32),
        square, square, square,
        pltpu.VMEM((2, 2, BAND, HALF), f32),
        split, split, split, split,
        pltpu.VMEM((SIDE, SIDE), f32),
        pltpu.VMEM((2, SIDE, HALF), f32),
    ]
    return pl.pallas_call(
        patch_kernel,
        grid=(count // GROUP,),
        in_specs=[scalars, scalars, scalars, band, band, whole(2, SIDE, SIDE)]
        + [whole(2, SIDE, SIDE)] * 4
        + [pl.BlockSpec((1, GROUP, SIDE, SIDE), lambda k: (0, k, 0, 0))],
        out_specs=[band, band, whole(GRAD_ROWS, HALF), whole(BAND, SIDE)],
        out_shape=[
            jax.ShapeDtypeStruct((2, BAND, SIDE), f32),
            jax.ShapeDtypeStruct((2, BAND, SIDE), f32),
            jax.ShapeDtypeStruct((GRAD_ROWS, HALF), f32),
            jax.ShapeDtypeStruct((BAND, SIDE), f32),
        ],
        scratch_shapes=[pltpu.VMEM((SIDE, SIDE), f32), pltpu.VMEM((SIDE, SIDE), bf16)]
        + member * GROUP,
        compiler_params=pltpu.CompilerParams(
            dimension_semantics=("arbitrary",), vmem_limit_bytes=PATCH_VMEM_BYTES
        ),
        cost_estimate=pl.CostEstimate(
            flops=count * 26 * 2 * SIDE**3, bytes_accessed=6 * 2**20, transcendentals=0
        ),
        name="patch_terms",
    )(rows, cols, behind, own, halo, probe, *[jnp.asarray(t) for t in tables], amplitudes)


class Place:
    def __init__(self):
        self.phase, self.space = lax.axis_index("phase"), lax.axis_index("space")
        self.core = lax.rem(self.phase, CORES)
        self.z = lax.rem(self.phase // CORES, Z_SIZE)
        x_lo = self.phase // (CORES * Z_SIZE)
        self.y = lax.rem(self.space, Y_SIZE)
        self.x_hi = self.space // Y_SIZE
        self.x = self.x_hi * X_LO + x_lo

    def device(self, core, z, x, y):
        phase = (lax.rem(x, X_LO) * Z_SIZE + z) * CORES + core
        return (phase, (x // X_LO) * Y_SIZE + y)

    def core_peer(self):
        return self.device(1 - self.core, self.z, self.x, self.y)

    def x_peer(self, k):
        return self.device(self.core, self.z, lax.rem(self.x + k, X_SIZE), self.y)

    def y_peer(self, k):
        return self.device(self.core, self.z, self.x, lax.rem(self.y + k, Y_SIZE))

    def z_peer(self, k):
        return self.device(self.core, lax.rem(self.z + k, Z_SIZE), self.x, self.y)

    def over_cut(self):
        return self.device(self.core, self.z, X_SIZE - 1 - self.x, self.y)

    def beside(self, k):
        other = self.x + 1 - 2 * lax.rem(self.x, X_LO)
        return self.device(self.core, self.z, other, lax.rem(self.y + k, Y_SIZE))

    def bin_at(self, k):
        count = lax.axis_size("phase")
        return (lax.rem(self.phase + k + count, count), self.space)

    def tile_at(self, k):
        count = lax.axis_size("space")
        return (self.phase, lax.rem(self.space + k + count, count))


def remote(src, dst, s, v, target):
    return pltpu.make_async_remote_copy(
        src_ref=src, dst_ref=dst, send_sem=s, recv_sem=v,
        device_id=target, device_id_type=pl.DeviceIdType.MESH,
    )


def greet(target):
    pl.semaphore_signal(
        pltpu.get_barrier_semaphore(), inc=1, device_id=target, device_id_type=pl.DeviceIdType.MESH
    )


ROW_CUTS = (0, 72, 136, 208, 272)
CHUNKS = tuple(
    (part, slice(ROW_CUTS[i], ROW_CUTS[i + 1])) for i in range(len(ROW_CUTS) - 1) for part in range(2)
)
EDGE = Y_SIZE


def chunk_of(ref, index):
    part, rows = CHUNKS[index]
    return ref.at[part, pl.ds(rows.start, rows.stop - rows.start), :]


def opening_kernel(
    own_h, split_h, dual_h, rows_h, cols_h,
    halo, steady, behind,
    own, split, dual, rows, cols, start_point, following, preceding, offsets, via,
    ls, hs, hv, rs, rv, ns, nv, ps, pv, os, ov,
):
    me = Place()
    last = TILES - 1
    count = range(len(CHUNKS))
    loads = [
        pltpu.make_async_copy(src, dst, ls.at[i])
        for i, (src, dst) in enumerate(
            ((own_h, own), (split_h, split), (dual_h, dual), (rows_h, rows), (cols_h, cols))
        )
    ]
    for load in loads:
        load.start()
    for target in (me.tile_at(1), me.tile_at(-1), me.bin_at(1), me.bin_at(-1)):
        greet(target)
    greet(me.over_cut())
    greet(me.beside(1))
    greet(me.beside(Y_SIZE - 1))

    @pl.when(me.space == 0)
    def _():
        behind[...] = jnp.zeros_like(behind)

    loads[0].wait()
    pl.semaphore_wait(pltpu.get_barrier_semaphore(), 7)

    def halo_copy(index):
        return remote(
            chunk_of(own, index), chunk_of(halo, index), hs.at[index], hv.at[index], me.tile_at(-1)
        )

    def cut_copy(index):
        return remote(
            chunk_of(own, index), chunk_of(via, index), hs.at[index], rv.at[index], me.over_cut()
        )

    def relay(index):
        return remote(
            chunk_of(via, index), chunk_of(halo, index), rs.at[index], hv.at[index],
            me.beside(Y_SIZE - 1),
        )

    @pl.when(me.space == EDGE)
    def _():
        for index in count:
            cut_copy(index).start()

    @pl.when(jnp.logical_and(me.space > 0, me.space != EDGE))
    def _():
        for index in count:
            halo_copy(index).start()

    to_preceding = remote(own, following, ns, nv, me.bin_at(-1))
    to_following = remote(start_point, preceding, ps, pv, me.bin_at(1))
    offsets_on = remote(offsets, behind, os, ov, me.tile_at(1))
    to_preceding.start()
    for load in loads[1:]:
        load.wait()
    offsets[...] = jnp.zeros_like(offsets)
    offsets[0:1, 0 : rows.shape[1]] = rows[...]
    offsets[1:2, 0 : cols.shape[1]] = cols[...]

    @pl.when(me.space < last)
    def _():
        offsets_on.start()

    start_point[...] = own[...] + split[...] - dual[...]
    to_following.start()

    @pl.when(me.space == 0)
    def _():
        for index in count:
            cut_copy(index).wait_recv()
            relay(index).start()

    to_preceding.wait()
    to_following.wait()
    steady[...] = own[...] - tv_step * (
        (own[...] - preceding[...]) - (following[...] - start_point[...])
    )

    @pl.when(me.space > 0)
    def _():
        offsets_on.wait_recv()
        for index in count:
            halo_copy(index).wait_send()

    @pl.when(me.space < last)
    def _():
        offsets_on.wait_send()
        for index in count:
            halo_copy(index).wait_recv()

    @pl.when(me.space == 0)
    def _():
        for index in count:
            relay(index).wait_send()


def opening(own, split, dual, rows, cols):
    f32, i32 = jnp.float32, jnp.int32
    dma = pltpu.SemaphoreType.DMA
    vmem = pl.BlockSpec(memory_space=pltpu.VMEM)
    room = pltpu.VMEM((2, BAND, SIDE), f32)
    many = dma((len(CHUNKS),))
    band = jax.ShapeDtypeStruct((2, BAND, SIDE), f32)
    return pl.pallas_call(
        opening_kernel,
        in_specs=[pl.BlockSpec(memory_space=pl.ANY)] * 5,
        out_specs=[vmem] * 3,
        out_shape=[band, band, jax.ShapeDtypeStruct((8, HALF), i32)],
        scratch_shapes=[
            room, room, room, pltpu.VMEM(rows.shape, i32), pltpu.VMEM(cols.shape, i32),
            room, room, room, pltpu.VMEM((8, HALF), i32), room,
            dma((5,)), many, many, many, many,
            dma, dma, dma, dma, dma, dma,
        ],
        compiler_params=pltpu.CompilerParams(
            collective_id=0, has_side_effects=True, vmem_limit_bytes=VMEM_BYTES
        ),
        cost_estimate=pl.CostEstimate(flops=2**20, bytes_accessed=2**24, transcendentals=0),
        name="opening",
    )(own, split, dual, rows, cols)


def tail_kernel(
    numer_own, numer_next, inverse, steady, term,
    updated, next_updated, out,
    inc, via, r1, a1, r2, a2, r3, r4, a4, f2, f1, f0,
    cs, cv, rs, rv, us, uv,
    s1, v1, s2, v2, s3, v3, s4, v4, s5, v5, s6, v6, s7, v7,
):
    me = Place()
    core, x, y, z = me.core, me.x, me.y, me.z
    last = TILES - 1

    greet(me.core_peer())
    for k in range(1, X_SIZE):
        greet(me.x_peer(k))
    for k in range(1, Y_SIZE):
        greet(me.y_peer(k))
    for target in (me.tile_at(1), me.tile_at(-1), me.bin_at(1), me.bin_at(-1)):
        greet(target)
    greet(me.over_cut())
    greet(me.beside(1))
    greet(me.beside(Y_SIZE - 1))

    def greet_z(k, carry):
        greet(me.z_peer(k))
        return carry

    lax.fori_loop(1, Z_SIZE, greet_z, 0)
    pl.semaphore_wait(
        pltpu.get_barrier_semaphore(), 1 + (X_SIZE - 1) + (Y_SIZE - 1) + 7 + (Z_SIZE - 1)
    )

    count = range(len(CHUNKS))

    def correction(index):
        return remote(
            chunk_of(numer_next, index), chunk_of(inc, index), cs.at[index], cv.at[index], me.tile_at(1)
        )

    def cut_copy(index):
        return remote(
            chunk_of(numer_next, index), chunk_of(via, index), cs.at[index], rv.at[index], me.over_cut()
        )

    def relay(index):
        return remote(
            chunk_of(via, index), chunk_of(inc, index), rs.at[index], cv.at[index], me.beside(1)
        )

    def relay_on(index):
        @pl.when(me.space == last)
        def _():
            cut_copy(index).wait_recv()
            relay(index).start()

    def updated_copy(index):
        return remote(
            chunk_of(updated, index), chunk_of(next_updated, index), us.at[index], uv.at[index],
            me.bin_at(-1),
        )

    @pl.when(jnp.logical_and(me.space < last, me.space != EDGE - 1))
    def _():
        for index in count:
            correction(index).start()

    part1 = GRAD_ROWS // CORES
    part2 = part1 // X_SIZE
    part3 = part2 // Z_SIZE

    def span(index, size):
        return pl.ds(pl.multiple_of(index * size, size), size)

    copy = remote(term.at[span(1 - core, part1)], r1, s1, v1, me.core_peer())
    copy.start()
    copy.wait()
    a1[...] = term[span(core, part1), :] + r1[...]

    copies = []
    for k in range(1, X_SIZE):
        target = lax.rem(x + k, X_SIZE)
        copies.append(
            remote(a1.at[span(target, part2)], r2.at[k - 1], s2.at[k - 1], v2.at[k - 1], me.x_peer(k))
        )
    for copy in copies:
        copy.start()
    for copy in copies:
        copy.wait()
    @pl.when(me.space == EDGE - 1)
    def _():
        for index in count:
            cut_copy(index).start()

    a2[...] = a1[span(x, part2), :] + r2[0] + r2[1] + r2[2]

    def z_sum(k):
        target = lax.rem(z + k, Z_SIZE)
        return remote(a2.at[span(target, part3)], r3.at[k - 1], s3.at[k - 1], v3.at[k - 1], me.z_peer(k))

    def start_z_sum(k, carry):
        z_sum(k).start()
        return carry

    def wait_z_sum(k, carry):
        z_sum(k).wait()
        return carry

    lax.fori_loop(1, Z_SIZE, start_z_sum, 0)
    lax.fori_loop(1, Z_SIZE, wait_z_sum, 0)
    relay_on(0)
    relay_on(1)
    total = a2[span(z, part3), :]
    for k in range(Z_SIZE - 1):
        total = total + r3[k]

    r4[y] = total
    copies = [
        remote(r4.at[y], r4.at[y], s4.at[k - 1], v4.at[k - 1], me.y_peer(k)) for k in range(1, Y_SIZE)
    ]
    for copy in copies:
        copy.start()
    relay_on(2)
    for copy in copies:
        copy.wait()
    terms = PATCHES * lax.axis_size("phase") * lax.axis_size("space")
    a4[...] = ((r4[0] + r4[1]) + (r4[2] + r4[3])) * (1.0 / math.sqrt(terms))

    f2[span(z, part3), :] = a4[...]

    def z_spread(k):
        return remote(a4, f2.at[span(z, part3)], s5.at[k - 1], v5.at[k - 1], me.z_peer(k))

    def start_z_spread(k, carry):
        z_spread(k).start()
        return carry

    def wait_z_spread(k, carry):
        z_spread(k).wait()
        return carry

    lax.fori_loop(1, Z_SIZE, start_z_spread, 0)

    for index in count:
        part, rows = CHUNKS[index]
        if index + 3 < len(CHUNKS):
            relay_on(index + 3)

        @pl.when(me.space > 0)
        def _():
            correction(index).wait_recv()
            numer = numer_own[part, rows, :] + inc[part, rows, :]
            updated[part, rows, :] = steady[part, rows, :] + numer * inverse[rows, :]

        @pl.when(me.space == 0)
        def _():
            updated[part, rows, :] = steady[part, rows, :] + numer_own[part, rows, :] * inverse[rows, :]

        updated_copy(index).start()

    lax.fori_loop(1, Z_SIZE, wait_z_spread, 0)

    copies = [
        remote(f2, f1.at[span(x, part2)], s6.at[k - 1], v6.at[k - 1], me.x_peer(k))
        for k in range(1, X_SIZE)
    ]
    for copy in copies:
        copy.start()
    f1[span(x, part2), :] = f2[...]
    for copy in copies:
        copy.wait()

    copy = remote(f1, f0.at[span(core, part1)], s7, v7, me.core_peer())
    copy.start()
    f0[span(core, part1), :] = f1[...]
    copy.wait()
    for c in range(2):
        for side in range(2):
            begin = (2 * c + side) * SIDE
            out[c, :, side * HALF : (side + 1) * HALF] = f0[begin : begin + SIDE, :]

    for index in count:
        updated_copy(index).wait()

    @pl.when(me.space < last)
    def _():
        for index in count:
            correction(index).wait_send()

    @pl.when(me.space == last)
    def _():
        for index in count:
            relay(index).wait_send()


def tail(numer_own, numer_next, inverse, steady, term):
    part1 = GRAD_ROWS // CORES
    part2 = part1 // X_SIZE
    part3 = part2 // Z_SIZE
    f32 = jnp.float32
    dma = pltpu.SemaphoreType.DMA
    vmem = pl.BlockSpec(memory_space=pltpu.VMEM)
    room = pltpu.VMEM((2, BAND, SIDE), f32)
    many = dma((len(CHUNKS),))
    band = jax.ShapeDtypeStruct((2, BAND, SIDE), f32)
    sems = []
    for count in (1, X_SIZE - 1, Z_SIZE - 1, Y_SIZE - 1, Z_SIZE - 1, X_SIZE - 1, 1):
        sems += [dma if count == 1 else dma((count,))] * 2
    return pl.pallas_call(
        tail_kernel,
        in_specs=[vmem] * 5,
        out_specs=[vmem] * 3,
        out_shape=[band, band, jax.ShapeDtypeStruct((2, SIDE, SIDE), f32)],
        scratch_shapes=[
            room, room,
            pltpu.VMEM((part1, HALF), f32),
            pltpu.VMEM((part1, HALF), f32),
            pltpu.VMEM((X_SIZE - 1, part2, HALF), f32),
            pltpu.VMEM((part2, HALF), f32),
            pltpu.VMEM((Z_SIZE - 1, part3, HALF), f32),
            pltpu.VMEM((Y_SIZE, part3, HALF), f32),
            pltpu.VMEM((part3, HALF), f32),
            pltpu.VMEM((part2, HALF), f32),
            pltpu.VMEM((part1, HALF), f32),
            pltpu.VMEM((GRAD_ROWS, HALF), f32),
            many, many, many, many, many, many,
            *sems,
        ],
        compiler_params=pltpu.CompilerParams(
            collective_id=1, has_side_effects=True, vmem_limit_bytes=VMEM_BYTES
        ),
        cost_estimate=pl.CostEstimate(flops=2**20, bytes_accessed=2**24, transcendentals=0),
        name="tail",
    )(numer_own, numer_next, inverse, steady, term)


def finish_kernel(updated, next_updated, dual, summed, out_object, out_split, out_dual, out_sum):
    out_object[...] = updated[...]
    out_sum[...] = summed[...]
    joint = [next_updated[c] - updated[c] + dual[c] for c in range(2)]
    size_abs = jnp.sqrt(joint[0] * joint[0] + joint[1] * joint[1])
    shrink = jnp.maximum(size_abs - shrink_level, 0.0) / jnp.maximum(size_abs, shrink_level)
    for c in range(2):
        new_split = joint[c] * shrink
        out_split[c] = new_split
        out_dual[c] = joint[c] - new_split


def finish(updated, next_updated, dual, summed):
    steps = 2
    f32 = jnp.float32
    band = pl.BlockSpec((2, BAND // steps, SIDE), lambda i: (0, i, 0))
    grad = pl.BlockSpec((2, SIDE // steps, SIDE), lambda i: (0, i, 0))
    band_shape = jax.ShapeDtypeStruct((2, BAND, SIDE), f32)
    return pl.pallas_call(
        finish_kernel,
        grid=(steps,),
        in_specs=[band, band, band, grad],
        out_specs=[band, band, band, grad],
        out_shape=[band_shape] * 3 + [jax.ShapeDtypeStruct((2, SIDE, SIDE), f32)],
        compiler_params=pltpu.CompilerParams(
            dimension_semantics=("arbitrary",), vmem_limit_bytes=VMEM_BYTES
        ),
        cost_estimate=pl.CostEstimate(flops=2**20, bytes_accessed=2**22, transcendentals=0),
        name="finish",
    )(updated, next_updated, dual, summed)


def shards(object_field, split_field, scaled_dual, probe, amplitudes, row_offsets, col_offsets):
    own = object_field[:, 0]
    split_own = split_field[:, 0]
    dual_own = scaled_dual[:, 0]
    halo, steady, behind = opening(own, split_own, dual_own, row_offsets, col_offsets)
    numer_own, numer_next, grad, inverse = patch_terms(
        row_offsets, col_offsets, behind, own, halo, probe, amplitudes
    )
    updated, next_updated, summed = tail(numer_own, numer_next, inverse, steady, grad)
    updated, new_split, new_dual, probe_gradient = finish(updated, next_updated, dual_own, summed)
    return (updated[:, None], new_split[:, None], new_dual[:, None], probe_gradient)


def solution(mesh):
    in_specs = (
        P(None, "phase", None, "space"),
        P(None, "phase", None, "space"),
        P(None, "phase", None, "space"),
        P(),
        P("phase", "space", None, None),
        P("phase", "space"),
        P("phase", "space"),
    )
    out_specs = (
        P(None, "phase", None, "space"),
        P(None, "phase", None, "space"),
        P(None, "phase", None, "space"),
        P(),
    )
    return jax.shard_map(shards, mesh=mesh, in_specs=in_specs, out_specs=out_specs, check_vma=False)
```

time: 98.2 us -> 102 us (1.039)
  Pallas kernels: 90.9 us -> 92.9 us
  local copies, waits for them, and re-layouts: 6.21 us -> 7.8 us
    pallas_call x1, Pallas kernels: 55.2 us -> 59.2 us  [tail(): pl.pallas_call(tail_kernel, in_specs=[vmem] * 5, out_specs=[vmem] * 3, ou...]
    pallas_call x2, Pallas kernels: 34 us -> 31.9 us  [the longest x1 17.6 us: opening(): pl.pallas_call(opening_kernel, in_specs=[pl.BlockSpec(memory_space=pl.ANY...]
    unnamed x30, local copies, waits for them, and re-layouts: 6.21 us -> 7.8 us
where the time goes in v3:
time: 102 us; the launch traced here: 101 us
  Pallas kernels  92.9 us (91%)
  local copies, waits for them, and re-layouts  7.8 us (8%)
    pallas_call x1, Pallas kernels, tail(): pl.pallas_call(tail_kernel, in_specs=[vmem] * 5, out_specs=[vmem] * 3, ou...  59.2 us
    pallas_call x1, Pallas kernels, opening(): pl.pallas_call(opening_kernel, in_specs=[pl.BlockSpec(memory_space=pl.ANY...  17.6 us
    pallas_call x1, Pallas kernels, patch_terms(): pl.pallas_call(patch_kernel, grid=(count // GROUP,), in_specs=[scalars, s...  14.3 us
    unnamed x30, local copies, waits for them, and re-layouts  7.8 us

profile of v3, /device:TPU:1, one launch (start us, length us, event | category | flops | bytes accessed | tf_op | source)
XLA Modules:
  0.0 101.4 jit_solution(7563025159375871138)
XLA Ops:
  0.6 0.0 copy-start.8
  0.6 0.0 copy-start.6
  0.7 0.0 copy-start
  0.7 1.1 %copy-done = f32[2,1,272,256]{3,2,1,0:T(8,128)S(1)} copy-done((f32[2,1,272,256]{3,2,1,0:T(8,128)S(1)}, f32[2,1,272,256]{3,2,1,0:T(8,128)}, u32[]{:S(2)}) %copy-start) | copy-done | bytes 557080
  1.7 1.1 %copy-done.2 = f32[2,1,272,256]{3,2,1,0:T(8,128)S(1)} copy-done((f32[2,1,272,256]{3,2,1,0:T(8,128)S(1)}, f32[2,1,272,256]{3,2,1,0:T(8,128)}, u32[]{:S(2)}) %copy-start.2) | copy-done | bytes 557080
  2.8 1.1 %copy-done.3 = f32[2,1,272,256]{3,2,1,0:T(8,128)S(1)} copy-done((f32[2,1,272,256]{3,2,1,0:T(8,128)S(1)}, f32[2,1,272,256]{3,2,1,0:T(8,128)}, u32[]{:S(2)}) %copy-start.3) | copy-done | bytes 557080
  3.8 0.7 copy-done.5
  4.5 0.7 copy-done.7
  5.1 17.6 %opening.1 = (f32[2,272,256]{2,1,0:T(8,128)S(1)}, f32[2,272,256]{2,1,0:T(8,128)S(1)}, s32[8,128]{1,0:T(8,128)S(1)}) custom-call(f32[2,272,256]{2,1,0:T(8,128)S(1)} %bitcast.15, f32[2,272,256]{2,1,0:T(8,128)S(1)} %bitcast.14, f32[2,272,256]{2,1,0:T(8,128)S(1)} %bitcast.12, s32[1,6]{1,0:T(1,128)S(1)} %copy-done.5, s32[1,6]{1,0:T(1,128)S(1)} %copy-done.7), custom_call_target="tpu_custom_call" | custom-call | flops 1048576 | bytes 16777216 | tf_op jit(solution)/shard_map/opening/pallas_call | solution.py:504
  22.8 0.0 copy-done.8
  22.8 0.0 copy-done.6
  22.8 0.0 copy-done.4
  22.8 0.0 copy-done.10
  22.8 0.0 copy-done.11
  22.8 0.0 copy-done.12
  22.8 0.0 copy-start.9
  22.9 1.4 %copy-done.9 = f32[1,6,256,256]{3,2,1,0:T(8,128)S(1)} copy-done((f32[1,6,256,256]{3,2,1,0:T(8,128)S(1)}, f32[1,6,256,256]{3,2,1,0:T(8,128)}, u32[]{:S(2)}) %copy-start.9) | copy-done | bytes 1572888
  24.3 0.9 copy-done.13
  25.2 0.9 copy-done.14
  26.2 14.3 %patch_terms.1 = (f32[2,272,256]{2,1,0:T(8,128)S(1)}, f32[2,272,256]{2,1,0:T(8,128)S(1)}, f32[1024,128]{1,0:T(8,128)S(1)}, f32[272,256]{1,0:T(8,128)S(1)}) custom-call(s32[1,6]{1,0:T(1,128)S(1)} %copy-done.6, s32[1,6]{1,0:T(1,128)S(1)} %copy-done.8, s32[8,128]{1,0:T(8,128)S(1)} %get-tuple-element.18.behind, f32[2,272,256]{2,1,0:T(8,128)S(1)} %bitcast.16, ...), custom_call_target="tpu_custom_call" | custom-call | flops 5234491392 | bytes 6291456 | tf_op jit(solution)/shard_map/patch_terms/pallas_call | solution.py:302
  40.5 0.0 copy-start.1
  40.5 59.2 %tail.1 = (f32[2,272,256]{2,1,0:T(8,128)S(1)}, f32[2,272,256]{2,1,0:T(8,128)S(1)}, f32[2,256,256]{2,1,0:T(8,128)S(1)}) custom-call(f32[2,272,256]{2,1,0:T(8,128)S(1)} %get-tuple-element.20.numer_own, f32[2,272,256]{2,1,0:T(8,128)S(1)} %get-tuple-element.21.numer_next, f32[272,256]{1,0:T(8,128)S(1)} %get-tuple-element.22.inverse, ...), custom_call_target="tpu_custom_call" | custom-call | flops 1048576 | bytes 16777216 | tf_op jit(solution)/shard_map/tail/pallas_call | solution.py:729
  99.7 0.0 copy-done.1
  99.7 1.7 %finish.1 = (f32[2,272,256]{2,1,0:T(8,128)}, f32[2,272,256]{2,1,0:T(8,128)}, f32[2,272,256]{2,1,0:T(8,128)}, f32[2,256,256]{2,1,0:T(8,128)}) custom-call(f32[2,272,256]{2,1,0:T(8,128)S(1)} %get-tuple-element.25.updated, f32[2,272,256]{2,1,0:T(8,128)S(1)} %get-tuple-element.26.next_updated, f32[2,272,256]{2,1,0:T(8,128)S(1)} %bitcast.13, ...), custom_call_target="tpu_custom_call" | custom-call | flops 1048576 | bytes 4194304 | tf_op jit(solution)/shard_map/finish/pallas_call | solution.py:775
  (10 shorter events, 0.0 us)
Async XLA Ops:
  0.6 22.2 %copy-start.8 = (s32[1,6]{1,0:T(1,128)S(1)}, s32[1,6]{1,0:T(1,128)}, u32[]{:S(2)}) copy-start(s32[1,6]{1,0:T(1,128)} %cols_s.1) | copy-start | bytes 76
  0.6 22.2 %copy-start.6 = (s32[1,6]{1,0:T(1,128)S(1)}, s32[1,6]{1,0:T(1,128)}, u32[]{:S(2)}) copy-start(s32[1,6]{1,0:T(1,128)} %rows_s.1) | copy-start | bytes 76
  0.7 1.1 %copy-start = (f32[2,1,272,256]{3,2,1,0:T(8,128)S(1)}, f32[2,1,272,256]{3,2,1,0:T(8,128)}, u32[]{:S(2)}) copy-start(f32[2,1,272,256]{3,2,1,0:T(8,128)} %param.13) | copy-start | bytes 1671172
  1.7 1.1 %copy-start.2 = (f32[2,1,272,256]{3,2,1,0:T(8,128)S(1)}, f32[2,1,272,256]{3,2,1,0:T(8,128)}, u32[]{:S(2)}) copy-start(f32[2,1,272,256]{3,2,1,0:T(8,128)} %param.12) | copy-start | bytes 1671172
  2.8 1.1 %copy-start.3 = (f32[2,1,272,256]{3,2,1,0:T(8,128)S(1)}, f32[2,1,272,256]{3,2,1,0:T(8,128)}, u32[]{:S(2)}) copy-start(f32[2,1,272,256]{3,2,1,0:T(8,128)} %param.11) | copy-start | bytes 1671172
  3.8 0.7 copy-start.5
  4.5 0.7 copy-start.7
  5.1 17.7 %copy-start.4 = (f32[2,1,272,256]{3,2,1,0:T(8,128)S(1)}, f32[2,1,272,256]{3,2,1,0:T(8,128)}, u32[]{:S(2)}) copy-start(f32[2,1,272,256]{3,2,1,0:T(8,128)} %param.11) | copy-start | bytes 1671172
  5.1 17.7 %copy-start.10 = (f32[2,256,256]{2,1,0:T(8,128)S(1)}, f32[2,256,256]{2,1,0:T(8,128)}, u32[]{:S(2)}) copy-start(f32[2,256,256]{2,1,0:T(8,128)} %probe.1) | copy-start | bytes 1572868
  5.1 17.7 %copy-start.11 = (bf16[2,256,256]{2,1,0:T(8,128)(2,1)S(1)}, bf16[2,256,256]{2,1,0:T(8,128)(2,1)}, u32[]{:S(2)}) copy-start(bf16[2,256,256]{2,1,0:T(8,128)(2,1)} %constant.11.clone.lot) | copy-start | bytes 786436
  5.1 17.7 %copy-start.12 = (bf16[2,256,256]{2,1,0:T(8,128)(2,1)S(1)}, bf16[2,256,256]{2,1,0:T(8,128)(2,1)}, u32[]{:S(2)}) copy-start(bf16[2,256,256]{2,1,0:T(8,128)(2,1)} %constant.10.clone.lo) | copy-start | bytes 786436
  22.8 1.4 %copy-start.9 = (f32[1,6,256,256]{3,2,1,0:T(8,128)S(1)}, f32[1,6,256,256]{3,2,1,0:T(8,128)}, u32[]{:S(2)}) copy-start(f32[1,6,256,256]{3,2,1,0:T(8,128)} %amp.1) | copy-start | bytes 4718596
  24.3 0.9 copy-start.13
  25.2 0.9 copy-start.14
  40.5 59.2 %copy-start.1 = (f32[2,1,272,256]{3,2,1,0:T(8,128)S(1)}, f32[2,1,272,256]{3,2,1,0:T(8,128)}, u32[]{:S(2)}) copy-start(f32[2,1,272,256]{3,2,1,0:T(8,128)} %param.13) | copy-start | bytes 1671172

commit v4 on v3

--- a/solution.py
+++ b/solution.py
@@ -22,8 +22,7 @@
 GRAD_ROWS = 1024
 TILES = X_SIZE // X_LO * Y_SIZE
 PATCHES = 6
-VMEM_BYTES = 50 * 1024 * 1024
-PATCH_VMEM_BYTES = 36 * 1024 * 1024
+VMEM_BYTES = 58 * 1024 * 1024
 GROUP = 2
 
 
@@ -85,18 +84,33 @@
 
 
 def patch_kernel(
-    rows_s, cols_s, behind, own, halo, probe, le, let, lo, lot, amp,
+    rows_s, cols_s, behind, own, halo, probe, le_h, let_h, lo_h, lot_h, amp_h,
     numer_own, numer_next, grad, weight,
-    power, sorter, *scratch,
+    power, sorter, le, let, lo, lot, amp, table_sems, amp_sems, *scratch,
 ):
+    group = pl.program_id(0)
+    groups = amp.shape[0] // GROUP
+    tables = [
+        pltpu.make_async_copy(src, dst, table_sems.at[i])
+        for i, (src, dst) in enumerate(((le_h, le), (let_h, let), (lo_h, lo), (lot_h, lot)))
+    ]
+
+    def amp_load(index):
+        rows = pl.ds(index * GROUP, GROUP)
+        return pltpu.make_async_copy(amp_h.at[0, rows], amp.at[rows], amp_sems.at[index])
+
     first_slot = pl.program_id(0) * GROUP
     step = 16
     row_id = lax.broadcasted_iota(jnp.int32, (step, HALF), 0)
     lane_id = lax.broadcasted_iota(jnp.int32, (step, HALF), 1)
     re_half, im_half = slice(0, HALF), slice(HALF, SIDE)
 
-    @pl.when(pl.program_id(0) == 0)
-    def _():
+    @pl.when(group == 0)
+    def _():
+        for load in tables:
+            load.start()
+        for index in range(groups):
+            amp_load(index).start()
         numer_own[...] = jnp.zeros_like(numer_own)
         numer_next[...] = jnp.zeros_like(numer_next)
         grad[...] = jnp.zeros_like(grad)
@@ -106,6 +120,10 @@
         target = lax.broadcasted_iota(jnp.int32, (SIDE, SIDE), 1)
         source = jnp.where(target < HALF, 2 * target, 2 * (target - HALF) + 1)
         sorter[...] = jnp.where(place == source, 1.0, 0.0).astype(jnp.bfloat16)
+        for load in tables:
+            load.wait()
+
+    amp_load(group).wait()
 
     def stages(member):
         brow, prow, pc, piece_s, wave_s, grow, xe, xo, ze, zo, amp_s, amp_c = scratch[
@@ -126,7 +144,7 @@
 
         def sort_amplitudes():
             for side in range(2):
-                amp_c[side] = amp[0, member, :, side * HALF : (side + 1) * HALF]
+                amp_c[side] = amp[slot, :, side * HALF : (side + 1) * HALF]
             for odd in range(2):
                 part = jnp.concatenate(
                     [amp_c[side, pl.ds(odd, HALF, stride=2), :] for side in range(2)], 1
@@ -303,8 +321,7 @@
         patch_kernel,
         grid=(count // GROUP,),
         in_specs=[scalars, scalars, scalars, band, band, whole(2, SIDE, SIDE)]
-        + [whole(2, SIDE, SIDE)] * 4
-        + [pl.BlockSpec((1, GROUP, SIDE, SIDE), lambda k: (0, k, 0, 0))],
+        + [pl.BlockSpec(memory_space=pltpu.HBM)] * 5,
         out_specs=[band, band, whole(GRAD_ROWS, HALF), whole(BAND, SIDE)],
         out_shape=[
             jax.ShapeDtypeStruct((2, BAND, SIDE), f32),
@@ -313,9 +330,15 @@
             jax.ShapeDtypeStruct((BAND, SIDE), f32),
         ],
         scratch_shapes=[pltpu.VMEM((SIDE, SIDE), f32), pltpu.VMEM((SIDE, SIDE), bf16)]
+        + [split] * 4
+        + [
+            pltpu.VMEM((count, SIDE, SIDE), f32),
+            pltpu.SemaphoreType.DMA((4,)),
+            pltpu.SemaphoreType.DMA((count // GROUP,)),
+        ]
         + member * GROUP,
         compiler_params=pltpu.CompilerParams(
-            dimension_semantics=("arbitrary",), vmem_limit_bytes=PATCH_VMEM_BYTES
+            dimension_semantics=("arbitrary",), vmem_limit_bytes=VMEM_BYTES
         ),
         cost_estimate=pl.CostEstimate(
             flops=count * 26 * 2 * SIDE**3, bytes_accessed=6 * 2**20, transcendentals=0
@@ -392,34 +415,28 @@
 
 
 def opening_kernel(
-    own_h, split_h, dual_h, rows_h, cols_h,
-    halo, steady, behind,
-    own, split, dual, rows, cols, start_point, following, preceding, offsets, via,
-    ls, hs, hv, rs, rv, ns, nv, ps, pv, os, ov,
+    own, rows_h, cols_h,
+    halo, behind,
+    rows, cols, offsets, via,
+    ls, hs, hv, rs, rv, os, ov,
 ):
     me = Place()
     last = TILES - 1
     count = range(len(CHUNKS))
     loads = [
-        pltpu.make_async_copy(src, dst, ls.at[i])
-        for i, (src, dst) in enumerate(
-            ((own_h, own), (split_h, split), (dual_h, dual), (rows_h, rows), (cols_h, cols))
-        )
+        pltpu.make_async_copy(rows_h, rows, ls.at[0]),
+        pltpu.make_async_copy(cols_h, cols, ls.at[1]),
     ]
     for load in loads:
         load.start()
-    for target in (me.tile_at(1), me.tile_at(-1), me.bin_at(1), me.bin_at(-1)):
+    for target in (me.tile_at(1), me.tile_at(-1), me.over_cut(), me.beside(1), me.beside(Y_SIZE - 1)):
         greet(target)
-    greet(me.over_cut())
-    greet(me.beside(1))
-    greet(me.beside(Y_SIZE - 1))
 
     @pl.when(me.space == 0)
     def _():
         behind[...] = jnp.zeros_like(behind)
 
-    loads[0].wait()
-    pl.semaphore_wait(pltpu.get_barrier_semaphore(), 7)
+    pl.semaphore_wait(pltpu.get_barrier_semaphore(), 5)
 
     def halo_copy(index):
         return remote(
@@ -447,22 +464,16 @@
         for index in count:
             halo_copy(index).start()
 
-    to_preceding = remote(own, following, ns, nv, me.bin_at(-1))
-    to_following = remote(start_point, preceding, ps, pv, me.bin_at(1))
-    offsets_on = remote(offsets, behind, os, ov, me.tile_at(1))
-    to_preceding.start()
-    for load in loads[1:]:
+    for load in loads:
         load.wait()
     offsets[...] = jnp.zeros_like(offsets)
     offsets[0:1, 0 : rows.shape[1]] = rows[...]
     offsets[1:2, 0 : cols.shape[1]] = cols[...]
+    offsets_on = remote(offsets, behind, os, ov, me.tile_at(1))
 
     @pl.when(me.space < last)
     def _():
         offsets_on.start()
-
-    start_point[...] = own[...] + split[...] - dual[...]
-    to_following.start()
 
     @pl.when(me.space == 0)
     def _():
@@ -470,12 +481,6 @@
             cut_copy(index).wait_recv()
             relay(index).start()
 
-    to_preceding.wait()
-    to_following.wait()
-    steady[...] = own[...] - tv_step * (
-        (own[...] - preceding[...]) - (following[...] - start_point[...])
-    )
-
     @pl.when(me.space > 0)
     def _():
         offsets_on.wait_recv()
@@ -494,53 +499,58 @@
             relay(index).wait_send()
 
 
-def opening(own, split, dual, rows, cols):
+def opening(own, rows, cols):
     f32, i32 = jnp.float32, jnp.int32
     dma = pltpu.SemaphoreType.DMA
-    vmem = pl.BlockSpec(memory_space=pltpu.VMEM)
-    room = pltpu.VMEM((2, BAND, SIDE), f32)
     many = dma((len(CHUNKS),))
-    band = jax.ShapeDtypeStruct((2, BAND, SIDE), f32)
     return pl.pallas_call(
         opening_kernel,
-        in_specs=[pl.BlockSpec(memory_space=pl.ANY)] * 5,
-        out_specs=[vmem] * 3,
-        out_shape=[band, band, jax.ShapeDtypeStruct((8, HALF), i32)],
+        in_specs=[pl.BlockSpec(memory_space=pltpu.HBM)] * 3,
+        out_specs=[
+            pl.BlockSpec(memory_space=pltpu.HBM),
+            pl.BlockSpec(memory_space=pltpu.VMEM),
+        ],
+        out_shape=[
+            jax.ShapeDtypeStruct((2, BAND, SIDE), f32),
+            jax.ShapeDtypeStruct((8, HALF), i32),
+        ],
         scratch_shapes=[
-            room, room, room, pltpu.VMEM(rows.shape, i32), pltpu.VMEM(cols.shape, i32),
-            room, room, room, pltpu.VMEM((8, HALF), i32), room,
-            dma((5,)), many, many, many, many,
-            dma, dma, dma, dma, dma, dma,
+            pltpu.VMEM(rows.shape, i32), pltpu.VMEM(cols.shape, i32), pltpu.VMEM((8, HALF), i32),
+            pltpu.VMEM((2, BAND, SIDE), f32),
+            dma((2,)), many, many, many, many, dma, dma,
         ],
         compiler_params=pltpu.CompilerParams(
             collective_id=0, has_side_effects=True, vmem_limit_bytes=VMEM_BYTES
         ),
         cost_estimate=pl.CostEstimate(flops=2**20, bytes_accessed=2**24, transcendentals=0),
         name="opening",
-    )(own, split, dual, rows, cols)
+    )(own, rows, cols)
 
 
 def tail_kernel(
-    numer_own, numer_next, inverse, steady, term,
+    numer_own, numer_next, inverse, term, own_h, split_h, dual_h,
     updated, next_updated, out,
-    inc, via, r1, a1, r2, a2, r3, r4, a4, f2, f1, f0,
-    cs, cv, rs, rv, us, uv,
+    own, split, dual, start_point, following, preceding, inc, via, r1, a1, r2, a2, r3, r4, a4, f2, f1, f0,
+    ls, ns, nv, ps, pv, cs, cv, rs, rv, us, uv,
     s1, v1, s2, v2, s3, v3, s4, v4, s5, v5, s6, v6, s7, v7,
 ):
     me = Place()
     core, x, y, z = me.core, me.x, me.y, me.z
     last = TILES - 1
 
+    loads = [
+        pltpu.make_async_copy(src, dst, ls.at[i])
+        for i, (src, dst) in enumerate(((own_h, own), (split_h, split), (dual_h, dual)))
+    ]
+    for load in loads:
+        load.start()
     greet(me.core_peer())
     for k in range(1, X_SIZE):
         greet(me.x_peer(k))
     for k in range(1, Y_SIZE):
         greet(me.y_peer(k))
-    for target in (me.tile_at(1), me.tile_at(-1), me.bin_at(1), me.bin_at(-1)):
+    for target in (me.bin_at(1), me.bin_at(-1), me.beside(1), me.beside(Y_SIZE - 1)):
         greet(target)
-    greet(me.over_cut())
-    greet(me.beside(1))
-    greet(me.beside(Y_SIZE - 1))
 
     def greet_z(k, carry):
         greet(me.z_peer(k))
@@ -548,14 +558,21 @@
 
     lax.fori_loop(1, Z_SIZE, greet_z, 0)
     pl.semaphore_wait(
-        pltpu.get_barrier_semaphore(), 1 + (X_SIZE - 1) + (Y_SIZE - 1) + 7 + (Z_SIZE - 1)
+        pltpu.get_barrier_semaphore(), 1 + (X_SIZE - 1) + (Y_SIZE - 1) + 4 + (Z_SIZE - 1)
     )
+    for load in loads:
+        load.wait()
+    start_point[...] = own[...] + split[...] - dual[...]
+    to_preceding = remote(own, following, ns, nv, me.bin_at(-1))
+    to_following = remote(start_point, preceding, ps, pv, me.bin_at(1))
+    first_end = jnp.logical_and(z == 0, core == 0)
+    last_end = jnp.logical_and(z == Z_SIZE - 1, core == CORES - 1)
 
     count = range(len(CHUNKS))
 
     def correction(index):
         return remote(
-            chunk_of(numer_next, index), chunk_of(inc, index), cs.at[index], cv.at[index], me.tile_at(1)
+            chunk_of(numer_next, index), chunk_of(inc, index), cs.at[index], cv.at[index], me.y_peer(1)
         )
 
     def cut_copy(index):
@@ -594,6 +611,15 @@
 
     copy = remote(term.at[span(1 - core, part1)], r1, s1, v1, me.core_peer())
     copy.start()
+
+    @pl.when(jnp.logical_not(first_end))
+    def _():
+        to_preceding.start()
+
+    @pl.when(jnp.logical_not(last_end))
+    def _():
+        to_following.start()
+
     copy.wait()
     a1[...] = term[span(core, part1), :] + r1[...]
 
@@ -612,6 +638,14 @@
         for index in count:
             cut_copy(index).start()
 
+    @pl.when(first_end)
+    def _():
+        to_preceding.start()
+
+    @pl.when(last_end)
+    def _():
+        to_following.start()
+
     a2[...] = a1[span(x, part2), :] + r2[0] + r2[1] + r2[2]
 
     def z_sum(k):
@@ -641,6 +675,33 @@
     for copy in copies:
         copy.start()
     relay_on(2)
+
+    def send_updated(index, corrected):
+        part, rows = CHUNKS[index]
+        numer = numer_own[part, rows, :]
+        if corrected:
+            correction(index).wait_recv()
+            numer = numer + inc[part, rows, :]
+        here = own[part, rows, :]
+        resid = following[part, rows, :] - start_point[part, rows, :]
+        steady = here - tv_step * ((here - preceding[part, rows, :]) - resid)
+        updated[part, rows, :] = steady + numer * inverse[rows, :]
+        updated_copy(index).start()
+
+    to_preceding.wait_recv()
+    to_following.wait_recv()
+
+    @pl.when(me.space == 0)
+    def _():
+        for index in count:
+            send_updated(index, False)
+
+    @pl.when(jnp.logical_and(me.space > 0, me.space != EDGE))
+    def _():
+        for index in count:
+            send_updated(index, True)
+
+    relay_on(3)
     for copy in copies:
         copy.wait()
     terms = PATCHES * lax.axis_size("phase") * lax.axis_size("space")
@@ -661,23 +722,8 @@
 
     lax.fori_loop(1, Z_SIZE, start_z_spread, 0)
 
-    for index in count:
-        part, rows = CHUNKS[index]
-        if index + 3 < len(CHUNKS):
-            relay_on(index + 3)
-
-        @pl.when(me.space > 0)
-        def _():
-            correction(index).wait_recv()
-            numer = numer_own[part, rows, :] + inc[part, rows, :]
-            updated[part, rows, :] = steady[part, rows, :] + numer * inverse[rows, :]
-
-        @pl.when(me.space == 0)
-        def _():
-            updated[part, rows, :] = steady[part, rows, :] + numer_own[part, rows, :] * inverse[rows, :]
-
-        updated_copy(index).start()
-
+    for index in range(4, len(CHUNKS)):
+        relay_on(index)
     lax.fori_loop(1, Z_SIZE, wait_z_spread, 0)
 
     copies = [
@@ -687,6 +733,12 @@
     for copy in copies:
         copy.start()
     f1[span(x, part2), :] = f2[...]
+
+    @pl.when(me.space == EDGE)
+    def _():
+        for index in count:
+            send_updated(index, True)
+
     for copy in copies:
         copy.wait()
 
@@ -701,6 +753,8 @@
 
     for index in count:
         updated_copy(index).wait()
+    to_preceding.wait_send()
+    to_following.wait_send()
 
     @pl.when(me.space < last)
     def _():
@@ -713,13 +767,14 @@
             relay(index).wait_send()
 
 
-def tail(numer_own, numer_next, inverse, steady, term):
+def tail(numer_own, numer_next, inverse, term, own, split, dual):
     part1 = GRAD_ROWS // CORES
     part2 = part1 // X_SIZE
     part3 = part2 // Z_SIZE
     f32 = jnp.float32
     dma = pltpu.SemaphoreType.DMA
     vmem = pl.BlockSpec(memory_space=pltpu.VMEM)
+    hbm = pl.BlockSpec(memory_space=pltpu.HBM)
     room = pltpu.VMEM((2, BAND, SIDE), f32)
     many = dma((len(CHUNKS),))
     band = jax.ShapeDtypeStruct((2, BAND, SIDE), f32)
@@ -728,11 +783,11 @@
         sems += [dma if count == 1 else dma((count,))] * 2
     return pl.pallas_call(
         tail_kernel,
-        in_specs=[vmem] * 5,
+        in_specs=[vmem, hbm, vmem, vmem, hbm, hbm, hbm],
         out_specs=[vmem] * 3,
         out_shape=[band, band, jax.ShapeDtypeStruct((2, SIDE, SIDE), f32)],
         scratch_shapes=[
-            room, room,
+            room, room, room, room, room, room, room, room,
             pltpu.VMEM((part1, HALF), f32),
             pltpu.VMEM((part1, HALF), f32),
             pltpu.VMEM((X_SIZE - 1, part2, HALF), f32),
@@ -743,7 +798,7 @@
             pltpu.VMEM((part2, HALF), f32),
             pltpu.VMEM((part1, HALF), f32),
             pltpu.VMEM((GRAD_ROWS, HALF), f32),
-            many, many, many, many, many, many,
+            dma((3,)), dma, dma, dma, dma, many, many, many, many, many, many,
             *sems,
         ],
         compiler_params=pltpu.CompilerParams(
@@ -751,7 +806,7 @@
         ),
         cost_estimate=pl.CostEstimate(flops=2**20, bytes_accessed=2**24, transcendentals=0),
         name="tail",
-    )(numer_own, numer_next, inverse, steady, term)
+    )(numer_own, numer_next, inverse, term, own, split, dual)
 
 
 def finish_kernel(updated, next_updated, dual, summed, out_object, out_split, out_dual, out_sum):
@@ -790,11 +845,13 @@
     own = object_field[:, 0]
     split_own = split_field[:, 0]
     dual_own = scaled_dual[:, 0]
-    halo, steady, behind = opening(own, split_own, dual_own, row_offsets, col_offsets)
+    halo, behind = opening(own, row_offsets, col_offsets)
     numer_own, numer_next, grad, inverse = patch_terms(
         row_offsets, col_offsets, behind, own, halo, probe, amplitudes
     )
-    updated, next_updated, summed = tail(numer_own, numer_next, inverse, steady, grad)
+    updated, next_updated, summed = tail(
+        numer_own, numer_next, inverse, grad, own, split_own, dual_own
+    )
     updated, new_split, new_dual, probe_gradient = finish(updated, next_updated, dual_own, summed)
     return (updated[:, None], new_split[:, None], new_dual[:, None], probe_gradient)
 

time: 102 us -> 104 us (1.020)
  Pallas kernels: 92.9 us -> 103 us
  local copies, waits for them, and re-layouts: 7.8 us -> 0 us
    unnamed x30 -> x0, local copies, waits for them, and re-layouts: 7.8 us -> none
    pallas_call x2, Pallas kernels: 76.9 us -> 82.6 us  [the longest x1 62 us: tail(): pl.pallas_call(tail_kernel, in_specs=[vmem, hbm, vmem, vmem, hbm, hbm, hb...]
    pallas_call x1, Pallas kernels: 14.3 us -> 17.7 us  [patch_terms(): pl.pallas_call(patch_kernel, grid=(count // GROUP,), in_specs=[scalars, s...]
where the time goes in v4:
time: 104 us
  Pallas kernels  103 us (99%)
    pallas_call x1, Pallas kernels, tail(): pl.pallas_call(tail_kernel, in_specs=[vmem, hbm, vmem, vmem, hbm, hbm, hb...  62 us
    pallas_call x1, Pallas kernels, opening(): pl.pallas_call(opening_kernel, in_specs=[pl.BlockSpec(memory_space=pltpu....  20.6 us
    pallas_call x1, Pallas kernels, patch_terms(): pl.pallas_call(patch_kernel, grid=(count // GROUP,), in_specs=[scalars, s...  17.7 us
    pallas_call x1, Pallas kernels, finish(): pl.pallas_call(finish_kernel, grid=(steps,), in_specs=[band, band, band,...  2.73 us

profile of v4, /device:TPU:1, one launch (start us, length us, event | category | flops | bytes accessed | tf_op | source)
XLA Modules:
  0.0 103.6 jit_solution(8789685076061137964)
XLA Ops:
  0.6 20.6 %opening.1 = (f32[2,272,256]{2,1,0:T(8,128)}, s32[8,128]{1,0:T(8,128)}) custom-call(f32[2,272,256]{2,1,0:T(8,128)} %bitcast.12, s32[1,6]{1,0:T(1,128)} %rows_s.1, s32[1,6]{1,0:T(1,128)} %cols_s.1), custom_call_target="tpu_custom_call" | custom-call | flops 1048576 | bytes 16777216 | tf_op jit(solution)/shard_map/opening/pallas_call | solution.py:506
  21.2 17.7 %patch_terms.1 = (f32[2,272,256]{2,1,0:T(8,128)}, f32[2,272,256]{2,1,0:T(8,128)}, f32[1024,128]{1,0:T(8,128)}, f32[272,256]{1,0:T(8,128)}) custom-call(s32[1,6]{1,0:T(1,128)} %rows_s.1, s32[1,6]{1,0:T(1,128)} %cols_s.1, s32[8,128]{1,0:T(8,128)} %get-tuple-element.17.behind, f32[2,272,256]{2,1,0:T(8,128)} %bitcast.13, f32[2,272,256]{2,1,0:T(8,128)} %get-tuple-element.18.halo, ...), custom_call_target="tpu_custom_call" | custom-call | flops 5234491392 | bytes 6291456 | tf_op jit(solution)/shard_map/patch_terms/pallas_call | solution.py:320
  38.9 62.0 %tail.1 = (f32[2,272,256]{2,1,0:T(8,128)}, f32[2,272,256]{2,1,0:T(8,128)}, f32[2,256,256]{2,1,0:T(8,128)}) custom-call(f32[2,272,256]{2,1,0:T(8,128)} %get-tuple-element.19.numer_own, f32[2,272,256]{2,1,0:T(8,128)} %get-tuple-element.20.numer_next, f32[272,256]{1,0:T(8,128)} %get-tuple-element.21.inverse, f32[1024,128]{1,0:T(8,128)} %get-tuple-element.22.term, ...), custom_call_target="tpu_custom_call" | custom-call | flops 1048576 | bytes 16777216 | tf_op jit(solution)/shard_map/tail/pallas_call | solution.py:784
  100.9 2.7 %finish.1 = (f32[2,272,256]{2,1,0:T(8,128)}, f32[2,272,256]{2,1,0:T(8,128)}, f32[2,272,256]{2,1,0:T(8,128)}, f32[2,256,256]{2,1,0:T(8,128)}) custom-call(f32[2,272,256]{2,1,0:T(8,128)} %get-tuple-element.23.updated, f32[2,272,256]{2,1,0:T(8,128)} %get-tuple-element.24.next_updated, f32[2,272,256]{2,1,0:T(8,128)} %bitcast.16, ...), custom_call_target="tpu_custom_call" | custom-call | flops 1048576 | bytes 4194304 | tf_op jit(solution)/shard_map/finish/pallas_call | solution.py:830

commit v5 on v4

--- a/solution.py
+++ b/solution.py
@@ -24,6 +24,12 @@
 PATCHES = 6
 VMEM_BYTES = 58 * 1024 * 1024
 GROUP = 2
+
+
+def passed_along(value, axis, steps):
+    count = lax.axis_size(axis)
+    pairs = [(source, (source + steps) % count) for source in range(count)]
+    return lax.ppermute(value, axis, pairs)
 
 
 def two_parts(table):
@@ -373,12 +379,8 @@
     def z_peer(self, k):
         return self.device(self.core, lax.rem(self.z + k, Z_SIZE), self.x, self.y)
 
-    def over_cut(self):
-        return self.device(self.core, self.z, X_SIZE - 1 - self.x, self.y)
-
-    def beside(self, k):
-        other = self.x + 1 - 2 * lax.rem(self.x, X_LO)
-        return self.device(self.core, self.z, other, lax.rem(self.y + k, Y_SIZE))
+    def y_mirror(self):
+        return self.device(self.core, self.z, self.x, Y_SIZE - 1 - self.y)
 
     def bin_at(self, k):
         count = lax.axis_size("phase")
@@ -414,58 +416,51 @@
     return ref.at[part, pl.ds(rows.start, rows.stop - rows.start), :]
 
 
+def by_ring(index):
+    return CHUNKS[index][0] == 1
+
+
 def opening_kernel(
-    own, rows_h, cols_h,
-    halo, behind,
-    rows, cols, offsets, via,
-    ls, hs, hv, rs, rv, os, ov,
+    own, split_h, dual_h, rows_h, cols_h,
+    halo, start_point, behind,
+    here, split, dual, rows, cols, offsets,
+    ls, hs, hv, rs, os, ov,
 ):
     me = Place()
     last = TILES - 1
     count = range(len(CHUNKS))
     loads = [
-        pltpu.make_async_copy(rows_h, rows, ls.at[0]),
-        pltpu.make_async_copy(cols_h, cols, ls.at[1]),
+        pltpu.make_async_copy(src, dst, ls.at[i])
+        for i, (src, dst) in enumerate(
+            ((rows_h, rows), (cols_h, cols), (own, here), (split_h, split), (dual_h, dual))
+        )
     ]
     for load in loads:
         load.start()
-    for target in (me.tile_at(1), me.tile_at(-1), me.over_cut(), me.beside(1), me.beside(Y_SIZE - 1)):
+    for target in (me.tile_at(1), me.tile_at(-1), me.tile_at(TILES // 2), me.y_mirror()):
         greet(target)
 
     @pl.when(me.space == 0)
     def _():
         behind[...] = jnp.zeros_like(behind)
 
-    pl.semaphore_wait(pltpu.get_barrier_semaphore(), 5)
+    pl.semaphore_wait(pltpu.get_barrier_semaphore(), 4)
 
     def halo_copy(index):
-        return remote(
-            chunk_of(own, index), chunk_of(halo, index), hs.at[index], hv.at[index], me.tile_at(-1)
-        )
-
-    def cut_copy(index):
-        return remote(
-            chunk_of(own, index), chunk_of(via, index), hs.at[index], rv.at[index], me.over_cut()
-        )
+        target = me.y_peer(Y_SIZE - 1) if by_ring(index) else me.tile_at(-1)
+        return remote(chunk_of(own, index), chunk_of(halo, index), hs.at[index], hv.at[index], target)
 
     def relay(index):
-        return remote(
-            chunk_of(via, index), chunk_of(halo, index), rs.at[index], hv.at[index],
-            me.beside(Y_SIZE - 1),
-        )
-
-    @pl.when(me.space == EDGE)
-    def _():
-        for index in count:
-            cut_copy(index).start()
-
-    @pl.when(jnp.logical_and(me.space > 0, me.space != EDGE))
+        place = chunk_of(halo, index)
+        return remote(place, place, rs.at[index], hv.at[index], me.tile_at(TILES // 2))
+
+    @pl.when(me.space > 0)
     def _():
         for index in count:
             halo_copy(index).start()
 
-    for load in loads:
-        load.wait()
+    loads[0].wait()
+    loads[1].wait()
     offsets[...] = jnp.zeros_like(offsets)
     offsets[0:1, 0 : rows.shape[1]] = rows[...]
     offsets[1:2, 0 : cols.shape[1]] = cols[...]
@@ -475,11 +470,16 @@
     def _():
         offsets_on.start()
 
-    @pl.when(me.space == 0)
-    def _():
-        for index in count:
-            cut_copy(index).wait_recv()
-            relay(index).start()
+    for load in loads[2:]:
+        load.wait()
+    start_point[...] = here[...] + split[...] - dual[...]
+
+    @pl.when(me.space == last)
+    def _():
+        for index in count:
+            if by_ring(index):
+                halo_copy(index).wait_recv()
+                relay(index).start()
 
     @pl.when(me.space > 0)
     def _():
@@ -493,45 +493,49 @@
         for index in count:
             halo_copy(index).wait_recv()
 
-    @pl.when(me.space == 0)
-    def _():
-        for index in count:
-            relay(index).wait_send()
-
-
-def opening(own, rows, cols):
+    @pl.when(me.space == last)
+    def _():
+        for index in count:
+            if by_ring(index):
+                relay(index).wait_send()
+
+
+def opening(own, split, dual, rows, cols):
     f32, i32 = jnp.float32, jnp.int32
     dma = pltpu.SemaphoreType.DMA
+    room = pltpu.VMEM((2, BAND, SIDE), f32)
     many = dma((len(CHUNKS),))
     return pl.pallas_call(
         opening_kernel,
-        in_specs=[pl.BlockSpec(memory_space=pltpu.HBM)] * 3,
+        in_specs=[pl.BlockSpec(memory_space=pltpu.HBM)] * 5,
         out_specs=[
             pl.BlockSpec(memory_space=pltpu.HBM),
+            pl.BlockSpec(memory_space=pltpu.VMEM),
             pl.BlockSpec(memory_space=pltpu.VMEM),
         ],
         out_shape=[
             jax.ShapeDtypeStruct((2, BAND, SIDE), f32),
+            jax.ShapeDtypeStruct((2, BAND, SIDE), f32),
             jax.ShapeDtypeStruct((8, HALF), i32),
         ],
         scratch_shapes=[
+            room, room, room,
             pltpu.VMEM(rows.shape, i32), pltpu.VMEM(cols.shape, i32), pltpu.VMEM((8, HALF), i32),
-            pltpu.VMEM((2, BAND, SIDE), f32),
-            dma((2,)), many, many, many, many, dma, dma,
+            dma((5,)), many, many, many, dma, dma,
         ],
         compiler_params=pltpu.CompilerParams(
             collective_id=0, has_side_effects=True, vmem_limit_bytes=VMEM_BYTES
         ),
         cost_estimate=pl.CostEstimate(flops=2**20, bytes_accessed=2**24, transcendentals=0),
         name="opening",
-    )(own, rows, cols)
+    )(own, split, dual, rows, cols)
 
 
 def tail_kernel(
-    numer_own, numer_next, inverse, term, own_h, split_h, dual_h,
+    numer_own, numer_next, inverse, term, own_h, start_h, following_h, preceding_h,
     updated, next_updated, out,
-    own, split, dual, start_point, following, preceding, inc, via, r1, a1, r2, a2, r3, r4, a4, f2, f1, f0,
-    ls, ns, nv, ps, pv, cs, cv, rs, rv, us, uv,
+    own, start_point, following, preceding, inc, r1, a1, r2, a2, r3, r4, a4, f2, f1, f0,
+    ls, cs, cv, rs, us, uv,
     s1, v1, s2, v2, s3, v3, s4, v4, s5, v5, s6, v6, s7, v7,
 ):
     me = Place()
@@ -540,7 +544,14 @@
 
     loads = [
         pltpu.make_async_copy(src, dst, ls.at[i])
-        for i, (src, dst) in enumerate(((own_h, own), (split_h, split), (dual_h, dual)))
+        for i, (src, dst) in enumerate(
+            (
+                (own_h, own),
+                (start_h, start_point),
+                (following_h, following),
+                (preceding_h, preceding),
+            )
+        )
     ]
     for load in loads:
         load.start()
@@ -549,7 +560,7 @@
         greet(me.x_peer(k))
     for k in range(1, Y_SIZE):
         greet(me.y_peer(k))
-    for target in (me.bin_at(1), me.bin_at(-1), me.beside(1), me.beside(Y_SIZE - 1)):
+    for target in (me.bin_at(1), me.bin_at(-1), me.tile_at(1), me.tile_at(-1)):
         greet(target)
 
     def greet_z(k, carry):
@@ -560,36 +571,17 @@
     pl.semaphore_wait(
         pltpu.get_barrier_semaphore(), 1 + (X_SIZE - 1) + (Y_SIZE - 1) + 4 + (Z_SIZE - 1)
     )
-    for load in loads:
-        load.wait()
-    start_point[...] = own[...] + split[...] - dual[...]
-    to_preceding = remote(own, following, ns, nv, me.bin_at(-1))
-    to_following = remote(start_point, preceding, ps, pv, me.bin_at(1))
-    first_end = jnp.logical_and(z == 0, core == 0)
-    last_end = jnp.logical_and(z == Z_SIZE - 1, core == CORES - 1)
-
     count = range(len(CHUNKS))
 
     def correction(index):
+        target = me.y_peer(1) if by_ring(index) else me.tile_at(1)
         return remote(
-            chunk_of(numer_next, index), chunk_of(inc, index), cs.at[index], cv.at[index], me.y_peer(1)
+            chunk_of(numer_next, index), chunk_of(inc, index), cs.at[index], cv.at[index], target
         )
 
-    def cut_copy(index):
-        return remote(
-            chunk_of(numer_next, index), chunk_of(via, index), cs.at[index], rv.at[index], me.over_cut()
-        )
-
     def relay(index):
-        return remote(
-            chunk_of(via, index), chunk_of(inc, index), rs.at[index], cv.at[index], me.beside(1)
-        )
-
-    def relay_on(index):
-        @pl.when(me.space == last)
-        def _():
-            cut_copy(index).wait_recv()
-            relay(index).start()
+        place = chunk_of(inc, index)
+        return remote(place, place, rs.at[index], cv.at[index], me.tile_at(TILES // 2))
 
     def updated_copy(index):
         return remote(
@@ -597,9 +589,11 @@
             me.bin_at(-1),
         )
 
-    @pl.when(jnp.logical_and(me.space < last, me.space != EDGE - 1))
-    def _():
-        for index in count:
+    for index in count:
+        early = last if by_ring(index) else EDGE - 1
+
+        @pl.when(jnp.logical_or(me.space < early, jnp.logical_and(me.space > EDGE - 1, me.space < last)))
+        def _():
             correction(index).start()
 
     part1 = GRAD_ROWS // CORES
@@ -611,15 +605,6 @@
 
     copy = remote(term.at[span(1 - core, part1)], r1, s1, v1, me.core_peer())
     copy.start()
-
-    @pl.when(jnp.logical_not(first_end))
-    def _():
-        to_preceding.start()
-
-    @pl.when(jnp.logical_not(last_end))
-    def _():
-        to_following.start()
-
     copy.wait()
     a1[...] = term[span(core, part1), :] + r1[...]
 
@@ -636,15 +621,8 @@
     @pl.when(me.space == EDGE - 1)
     def _():
         for index in count:
-            cut_copy(index).start()
-
-    @pl.when(first_end)
-    def _():
-        to_preceding.start()
-
-    @pl.when(last_end)
-    def _():
-        to_following.start()
+            if not by_ring(index):
+                correction(index).start()
 
     a2[...] = a1[span(x, part2), :] + r2[0] + r2[1] + r2[2]
 
@@ -661,9 +639,15 @@
         return carry
 
     lax.fori_loop(1, Z_SIZE, start_z_sum, 0)
+
+    @pl.when(me.space == 0)
+    def _():
+        for index in count:
+            if by_ring(index):
+                correction(index).wait_recv()
+                relay(index).start()
+
     lax.fori_loop(1, Z_SIZE, wait_z_sum, 0)
-    relay_on(0)
-    relay_on(1)
     total = a2[span(z, part3), :]
     for k in range(Z_SIZE - 1):
         total = total + r3[k]
@@ -674,7 +658,34 @@
     ]
     for copy in copies:
         copy.start()
-    relay_on(2)
+    for copy in copies:
+        copy.wait()
+    terms = PATCHES * lax.axis_size("phase") * lax.axis_size("space")
+    a4[...] = ((r4[0] + r4[1]) + (r4[2] + r4[3])) * (1.0 / math.sqrt(terms))
+
+    f2[span(z, part3), :] = a4[...]
+
+    def z_spread(k):
+        return remote(a4, f2.at[span(z, part3)], s5.at[k - 1], v5.at[k - 1], me.z_peer(k))
+
+    def start_z_spread(k, carry):
+        z_spread(k).start()
+        return carry
+
+    def wait_z_spread(k, carry):
+        z_spread(k).wait()
+        return carry
+
+    lax.fori_loop(1, Z_SIZE, start_z_spread, 0)
+    lax.fori_loop(1, Z_SIZE, wait_z_spread, 0)
+
+    copies = [
+        remote(f2, f1.at[span(x, part2)], s6.at[k - 1], v6.at[k - 1], me.x_peer(k))
+        for k in range(1, X_SIZE)
+    ]
+    for copy in copies:
+        copy.start()
+    f1[span(x, part2), :] = f2[...]
 
     def send_updated(index, corrected):
         part, rows = CHUNKS[index]
@@ -688,53 +699,15 @@
         updated[part, rows, :] = steady + numer * inverse[rows, :]
         updated_copy(index).start()
 
-    to_preceding.wait_recv()
-    to_following.wait_recv()
+    for load in loads:
+        load.wait()
 
     @pl.when(me.space == 0)
     def _():
         for index in count:
             send_updated(index, False)
 
-    @pl.when(jnp.logical_and(me.space > 0, me.space != EDGE))
-    def _():
-        for index in count:
-            send_updated(index, True)
-
-    relay_on(3)
-    for copy in copies:
-        copy.wait()
-    terms = PATCHES * lax.axis_size("phase") * lax.axis_size("space")
-    a4[...] = ((r4[0] + r4[1]) + (r4[2] + r4[3])) * (1.0 / math.sqrt(terms))
-
-    f2[span(z, part3), :] = a4[...]
-
-    def z_spread(k):
-        return remote(a4, f2.at[span(z, part3)], s5.at[k - 1], v5.at[k - 1], me.z_peer(k))
-
-    def start_z_spread(k, carry):
-        z_spread(k).start()
-        return carry
-
-    def wait_z_spread(k, carry):
-        z_spread(k).wait()
-        return carry
-
-    lax.fori_loop(1, Z_SIZE, start_z_spread, 0)
-
-    for index in range(4, len(CHUNKS)):
-        relay_on(index)
-    lax.fori_loop(1, Z_SIZE, wait_z_spread, 0)
-
-    copies = [
-        remote(f2, f1.at[span(x, part2)], s6.at[k - 1], v6.at[k - 1], me.x_peer(k))
-        for k in range(1, X_SIZE)
-    ]
-    for copy in copies:
-        copy.start()
-    f1[span(x, part2), :] = f2[...]
-
-    @pl.when(me.space == EDGE)
+    @pl.when(me.space > 0)
     def _():
         for index in count:
             send_updated(index, True)
@@ -753,21 +726,20 @@
 
     for index in count:
         updated_copy(index).wait()
-    to_preceding.wait_send()
-    to_following.wait_send()
 
     @pl.when(me.space < last)
     def _():
         for index in count:
             correction(index).wait_send()
 
-    @pl.when(me.space == last)
-    def _():
-        for index in count:
-            relay(index).wait_send()
-
-
-def tail(numer_own, numer_next, inverse, term, own, split, dual):
+    @pl.when(me.space == 0)
+    def _():
+        for index in count:
+            if by_ring(index):
+                relay(index).wait_send()
+
+
+def tail(numer_own, numer_next, inverse, term, own, start_point, following, preceding):
     part1 = GRAD_ROWS // CORES
     part2 = part1 // X_SIZE
     part3 = part2 // Z_SIZE
@@ -775,6 +747,7 @@
     dma = pltpu.SemaphoreType.DMA
     vmem = pl.BlockSpec(memory_space=pltpu.VMEM)
     hbm = pl.BlockSpec(memory_space=pltpu.HBM)
+    place = pl.BlockSpec(memory_space=pl.ANY)
     room = pltpu.VMEM((2, BAND, SIDE), f32)
     many = dma((len(CHUNKS),))
     band = jax.ShapeDtypeStruct((2, BAND, SIDE), f32)
@@ -783,11 +756,11 @@
         sems += [dma if count == 1 else dma((count,))] * 2
     return pl.pallas_call(
         tail_kernel,
-        in_specs=[vmem, hbm, vmem, vmem, hbm, hbm, hbm],
+        in_specs=[vmem, hbm, vmem, vmem, place, place, place, place],
         out_specs=[vmem] * 3,
         out_shape=[band, band, jax.ShapeDtypeStruct((2, SIDE, SIDE), f32)],
         scratch_shapes=[
-            room, room, room, room, room, room, room, room,
+            room, room, room, room, room,
             pltpu.VMEM((part1, HALF), f32),
             pltpu.VMEM((part1, HALF), f32),
             pltpu.VMEM((X_SIZE - 1, part2, HALF), f32),
@@ -798,7 +771,7 @@
             pltpu.VMEM((part2, HALF), f32),
             pltpu.VMEM((part1, HALF), f32),
             pltpu.VMEM((GRAD_ROWS, HALF), f32),
-            dma((3,)), dma, dma, dma, dma, many, many, many, many, many, many,
+            dma((4,)), many, many, many, many, many,
             *sems,
         ],
         compiler_params=pltpu.CompilerParams(
@@ -806,7 +779,7 @@
         ),
         cost_estimate=pl.CostEstimate(flops=2**20, bytes_accessed=2**24, transcendentals=0),
         name="tail",
-    )(numer_own, numer_next, inverse, term, own, split, dual)
+    )(numer_own, numer_next, inverse, term, own, start_point, following, preceding)
 
 
 def finish_kernel(updated, next_updated, dual, summed, out_object, out_split, out_dual, out_sum):
@@ -845,12 +818,15 @@
     own = object_field[:, 0]
     split_own = split_field[:, 0]
     dual_own = scaled_dual[:, 0]
-    halo, behind = opening(own, row_offsets, col_offsets)
+    halo, start_point, behind = opening(own, split_own, dual_own, row_offsets, col_offsets)
+    sent, halo = lax.optimization_barrier((own, halo))
+    following = passed_along(sent, "phase", -1)
+    preceding = passed_along(start_point, "phase", 1)
     numer_own, numer_next, grad, inverse = patch_terms(
         row_offsets, col_offsets, behind, own, halo, probe, amplitudes
     )
     updated, next_updated, summed = tail(
-        numer_own, numer_next, inverse, grad, own, split_own, dual_own
+        numer_own, numer_next, inverse, grad, own, start_point, following, preceding
     )
     updated, new_split, new_dual, probe_gradient = finish(updated, next_updated, dual_own, summed)
     return (updated[:, None], new_split[:, None], new_dual[:, None], probe_gradient)

time: 104 us -> 99.9 us (0.961)
  Pallas kernels: 103 us -> 88.1 us
  starting transfers between devices: 0 us -> 9.73 us
    pallas_call x1, Pallas kernels: 62 us -> 51.5 us  [tail(): pl.pallas_call(tail_kernel, in_specs=[vmem, hbm, vmem, vmem, place, place...]
    ppermute x0 -> x2, starting transfers between devices: none -> 9.73 us  [passed_along(): return lax.ppermute(value, axis, pairs)]
    pallas_call x1, Pallas kernels: 20.6 us -> 16.3 us  [opening(): pl.pallas_call(opening_kernel, in_specs=[pl.BlockSpec(memory_space=pltpu....]
  transfers between devices with their start and end apart: 0 -> 2, of which waited for: 0 -> 0; matrix products, arithmetic and copies ran while one was open for 0% -> 0% of each run, Pallas kernels for 0% -> 18%
where the time goes in v5:
time: 99.9 us; the launch traced here: 99.6 us
  Pallas kernels  88.1 us (88%)
  starting transfers between devices  9.73 us (10%)
    pallas_call x1, Pallas kernels, tail(): pl.pallas_call(tail_kernel, in_specs=[vmem, hbm, vmem, vmem, place, place...  51.5 us
    pallas_call x1, Pallas kernels, patch_terms(): pl.pallas_call(patch_kernel, grid=(count // GROUP,), in_specs=[scalars, s...  17.6 us
    pallas_call x1, Pallas kernels, opening(): pl.pallas_call(opening_kernel, in_specs=[pl.BlockSpec(memory_space=pltpu....  16.3 us
    ppermute x2, starting transfers between devices, passed_along(): return lax.ppermute(value, axis, pairs)  9.73 us
    pallas_call x1, Pallas kernels, finish(): pl.pallas_call(finish_kernel, grid=(steps,), in_specs=[band, band, band,...  2.73 us
  transfers between devices with their start and end apart: 2, of which 0 were waited for; matrix products, arithmetic and copies ran while one was open for 0% of the time, Pallas kernels for 18%

profile of v5, /device:TPU:1, one launch (start us, length us, event | category | flops | bytes accessed | tf_op | source)
XLA Modules:
  0.0 99.6 jit_solution(1289000083720626466)
XLA Ops:
  0.6 0.0 copy-start
  0.6 16.3 %opening.1 = (f32[2,272,256]{2,1,0:T(8,128)}, f32[2,272,256]{2,1,0:T(8,128)}, s32[8,128]{1,0:T(8,128)}) custom-call(f32[2,272,256]{2,1,0:T(8,128)} %bitcast.14, f32[2,272,256]{2,1,0:T(8,128)} %bitcast.18, f32[2,272,256]{2,1,0:T(8,128)} %bitcast.12, s32[1,6]{1,0:T(1,128)} %rows_s.1, s32[1,6]{1,0:T(1,128)} %cols_s.1), custom_call_target="tpu_custom_call" | custom-call | flops 1048576 | bytes 16777216 | tf_op jit(solution)/shard_map/opening/pallas_call | solution.py:508
  17.0 0.0 copy-done
  17.0 6.3 %collective-permute-start = (f32[2,272,256]{2,1,0:T(8,128)S(1)}, f32[2,272,256]{2,1,0:T(8,128)S(1)}, u32[]{:S(2)}, u32[]{:S(2)}) collective-permute-start(f32[2,272,256]{2,1,0:T(8,128)S(1)} %bitcast.17), channel_id=1, source_target_pairs={{0,504},{8,0},{16,8},{24,16},{32,24},{40,32},{48,40},{56,48},{64,5... | collective-permute-start | bytes 1671176 | tf_op jit(solution)/shard_map/ppermute | solution.py:32
  23.3 3.4 %collective-permute-start.1 = (f32[2,272,256]{2,1,0:T(8,128)}, f32[2,272,256]{2,1,0:T(8,128)S(1)}, u32[]{:S(2)}, u32[]{:S(2)}) collective-permute-start(f32[2,272,256]{2,1,0:T(8,128)} %get-tuple-element.27.start_h), channel_id=1, source_target_pairs={{0,8},{8,16},{16,24},{24,32},{32,40},{40,48},{48,56},{56,64},{64,7... | collective-permute-start | bytes 1671176 | tf_op jit(solution)/shard_map/ppermute | solution.py:32
  26.7 17.6 %patch_terms.1 = (f32[2,272,256]{2,1,0:T(8,128)}, f32[2,272,256]{2,1,0:T(8,128)}, f32[1024,128]{1,0:T(8,128)}, f32[272,256]{1,0:T(8,128)}) custom-call(s32[1,6]{1,0:T(1,128)} %rows_s.1, s32[1,6]{1,0:T(1,128)} %cols_s.1, s32[8,128]{1,0:T(8,128)} %get-tuple-element.20.behind, f32[2,272,256]{2,1,0:T(8,128)} %bitcast.15, f32[2,272,256]{2,1,0:T(8,128)} %get-tuple-element.22.halo, ...), custom_call_target="tpu_custom_call" | custom-call | flops 5234491392 | bytes 6291456 | tf_op jit(solution)/shard_map/patch_terms/pallas_call | solution.py:326
  44.3 0.0 collective-permute-done.following_h
  44.3 0.0 copy-start.1
  44.3 0.0 collective-permute-done.1.preceding_h
  44.3 0.0 copy-start.2
  44.4 0.8 copy-done.1
  45.1 0.2 copy-done.2
  45.3 51.5 %tail.1 = (f32[2,272,256]{2,1,0:T(8,128)}, f32[2,272,256]{2,1,0:T(8,128)}, f32[2,256,256]{2,1,0:T(8,128)}) custom-call(f32[2,272,256]{2,1,0:T(8,128)} %get-tuple-element.23.numer_own, f32[2,272,256]{2,1,0:T(8,128)} %get-tuple-element.24.numer_next, f32[272,256]{1,0:T(8,128)} %get-tuple-element.25.inverse, f32[1024,128]{1,0:T(8,128)} %get-tuple-element.26.term, ...), custom_call_target="tpu_custom_call" | custom-call | flops 1048576 | bytes 16777216 | tf_op jit(solution)/shard_map/tail/pallas_call | solution.py:757
  96.8 2.7 %finish.1 = (f32[2,272,256]{2,1,0:T(8,128)}, f32[2,272,256]{2,1,0:T(8,128)}, f32[2,272,256]{2,1,0:T(8,128)}, f32[2,256,256]{2,1,0:T(8,128)}) custom-call(f32[2,272,256]{2,1,0:T(8,128)} %get-tuple-element.29.updated, f32[2,272,256]{2,1,0:T(8,128)} %get-tuple-element.30.next_updated, f32[2,272,256]{2,1,0:T(8,128)} %bitcast.13, ...), custom_call_target="tpu_custom_call" | custom-call | flops 1048576 | bytes 4194304 | tf_op jit(solution)/shard_map/finish/pallas_call | solution.py:803
Async XLA Ops:
  0.6 16.4 %copy-start = (f32[2,1,272,256]{3,2,1,0:T(8,128)S(1)}, f32[2,1,272,256]{3,2,1,0:T(8,128)}, u32[]{:S(2)}) copy-start(f32[2,1,272,256]{3,2,1,0:T(8,128)} %param.11) | copy-start | bytes 1671172
  17.0 27.3 %collective-permute-start = (f32[2,272,256]{2,1,0:T(8,128)S(1)}, f32[2,272,256]{2,1,0:T(8,128)S(1)}, u32[]{:S(2)}, u32[]{:S(2)}) collective-permute-start(f32[2,272,256]{2,1,0:T(8,128)S(1)} %bitcast.17), channel_id=1, source_target_pairs={{0,504},{8,0},{16,8},{24,16},{32,24},{40,32},{48,40},{56,48},{64,5... | collective-permute-start | bytes 1671176 | tf_op jit(solution)/shard_map/ppermute | solution.py:32
  23.3 21.0 %collective-permute-start.1 = (f32[2,272,256]{2,1,0:T(8,128)}, f32[2,272,256]{2,1,0:T(8,128)S(1)}, u32[]{:S(2)}, u32[]{:S(2)}) collective-permute-start(f32[2,272,256]{2,1,0:T(8,128)} %get-tuple-element.27.start_h), channel_id=1, source_target_pairs={{0,8},{8,16},{16,24},{24,32},{32,40},{40,48},{48,56},{56,64},{64,7... | collective-permute-start | bytes 1671176 | tf_op jit(solution)/shard_map/ppermute | solution.py:32
  44.3 0.8 copy-start.1
  44.3 1.0 copy-start.2

commit v6 on v5

--- a/solution.py
+++ b/solution.py
@@ -19,17 +19,12 @@
 BAND = 272
 SPILL = BAND - SIDE
 CORES, Z_SIZE, X_LO, Y_SIZE, X_SIZE = 2, 16, 2, 4, 4
+NEAR = 4
 GRAD_ROWS = 1024
 TILES = X_SIZE // X_LO * Y_SIZE
 PATCHES = 6
 VMEM_BYTES = 58 * 1024 * 1024
 GROUP = 2
-
-
-def passed_along(value, axis, steps):
-    count = lax.axis_size(axis)
-    pairs = [(source, (source + steps) % count) for source in range(count)]
-    return lax.ppermute(value, axis, pairs)
 
 
 def two_parts(table):
@@ -376,11 +371,15 @@
     def y_peer(self, k):
         return self.device(self.core, self.z, self.x, lax.rem(self.y + k, Y_SIZE))
 
-    def z_peer(self, k):
-        return self.device(self.core, lax.rem(self.z + k, Z_SIZE), self.x, self.y)
-
     def y_mirror(self):
         return self.device(self.core, self.z, self.x, Y_SIZE - 1 - self.y)
+
+    def near_peer(self, k):
+        near = lax.rem(lax.rem(self.z, NEAR) + k, NEAR)
+        return self.device(self.core, self.z // NEAR * NEAR + near, self.x, self.y)
+
+    def far_peer(self, k):
+        return self.device(self.core, lax.rem(self.z + k * NEAR, Z_SIZE), self.x, self.y)
 
     def bin_at(self, k):
         count = lax.axis_size("phase")
@@ -404,7 +403,7 @@
     )
 
 
-ROW_CUTS = (0, 72, 136, 208, 272)
+ROW_CUTS = (0, 136, 272)
 CHUNKS = tuple(
     (part, slice(ROW_CUTS[i], ROW_CUTS[i + 1])) for i in range(len(ROW_CUTS) - 1) for part in range(2)
 )
@@ -422,9 +421,9 @@
 
 def opening_kernel(
     own, split_h, dual_h, rows_h, cols_h,
-    halo, start_point, behind,
-    here, split, dual, rows, cols, offsets,
-    ls, hs, hv, rs, os, ov,
+    halo, steady, behind,
+    here, split, dual, start_point, following, preceding, rows, cols, offsets,
+    ls, hs, hv, rs, ns, nv, ps, pv, os, ov,
 ):
     me = Place()
     last = TILES - 1
@@ -439,12 +438,14 @@
         load.start()
     for target in (me.tile_at(1), me.tile_at(-1), me.tile_at(TILES // 2), me.y_mirror()):
         greet(target)
+    for target in (me.bin_at(1), me.bin_at(-1)):
+        greet(target)
 
     @pl.when(me.space == 0)
     def _():
         behind[...] = jnp.zeros_like(behind)
 
-    pl.semaphore_wait(pltpu.get_barrier_semaphore(), 4)
+    pl.semaphore_wait(pltpu.get_barrier_semaphore(), 6)
 
     def halo_copy(index):
         target = me.y_peer(Y_SIZE - 1) if by_ring(index) else me.tile_at(-1)
@@ -459,8 +460,13 @@
         for index in count:
             halo_copy(index).start()
 
-    loads[0].wait()
-    loads[1].wait()
+    to_preceding = remote(own, following, ns, nv, me.bin_at(-1))
+    to_following = remote(start_point, preceding, ps, pv, me.bin_at(1))
+    to_preceding.start()
+    for load in loads:
+        load.wait()
+    start_point[...] = here[...] + split[...] - dual[...]
+    to_following.start()
     offsets[...] = jnp.zeros_like(offsets)
     offsets[0:1, 0 : rows.shape[1]] = rows[...]
     offsets[1:2, 0 : cols.shape[1]] = cols[...]
@@ -470,16 +476,18 @@
     def _():
         offsets_on.start()
 
-    for load in loads[2:]:
-        load.wait()
-    start_point[...] = here[...] + split[...] - dual[...]
-
     @pl.when(me.space == last)
     def _():
         for index in count:
             if by_ring(index):
                 halo_copy(index).wait_recv()
                 relay(index).start()
+
+    to_preceding.wait()
+    to_following.wait()
+    steady[...] = here[...] - tv_step * (
+        (here[...] - preceding[...]) - (following[...] - start_point[...])
+    )
 
     @pl.when(me.space > 0)
     def _():
@@ -519,9 +527,9 @@
             jax.ShapeDtypeStruct((8, HALF), i32),
         ],
         scratch_shapes=[
-            room, room, room,
+            room, room, room, room, room, room,
             pltpu.VMEM(rows.shape, i32), pltpu.VMEM(cols.shape, i32), pltpu.VMEM((8, HALF), i32),
-            dma((5,)), many, many, many, dma, dma,
+            dma((5,)), many, many, many, dma, dma, dma, dma, dma, dma,
         ],
         compiler_params=pltpu.CompilerParams(
             collective_id=0, has_side_effects=True, vmem_limit_bytes=VMEM_BYTES
@@ -532,45 +540,25 @@
 
 
 def tail_kernel(
-    numer_own, numer_next, inverse, term, own_h, start_h, following_h, preceding_h,
+    numer_own, numer_next, inverse, term, steady_h,
     updated, next_updated, out,
-    own, start_point, following, preceding, inc, r1, a1, r2, a2, r3, r4, a4, f2, f1, f0,
+    steady, inc, r1, a1, r2, a2, r3, a3, r4, r5, a5, f3, f2, f1, f0,
     ls, cs, cv, rs, us, uv,
-    s1, v1, s2, v2, s3, v3, s4, v4, s5, v5, s6, v6, s7, v7,
+    s1, v1, s2, v2, s3, v3, s4, v4, s5, v5, s6, v6, s7, v7, s8, v8, s9, v9,
 ):
     me = Place()
     core, x, y, z = me.core, me.x, me.y, me.z
     last = TILES - 1
 
-    loads = [
-        pltpu.make_async_copy(src, dst, ls.at[i])
-        for i, (src, dst) in enumerate(
-            (
-                (own_h, own),
-                (start_h, start_point),
-                (following_h, following),
-                (preceding_h, preceding),
-            )
-        )
-    ]
-    for load in loads:
-        load.start()
-    greet(me.core_peer())
-    for k in range(1, X_SIZE):
-        greet(me.x_peer(k))
-    for k in range(1, Y_SIZE):
-        greet(me.y_peer(k))
-    for target in (me.bin_at(1), me.bin_at(-1), me.tile_at(1), me.tile_at(-1)):
+    load = pltpu.make_async_copy(steady_h, steady, ls)
+    load.start()
+    peers = [me.core_peer(), me.bin_at(1), me.bin_at(-1), me.tile_at(1), me.tile_at(-1)]
+    peers += [me.x_peer(k) for k in range(1, X_SIZE)]
+    peers += [me.y_peer(k) for k in range(1, Y_SIZE)]
+    peers += [me.near_peer(k) for k in range(1, NEAR)] + [me.far_peer(k) for k in range(1, NEAR)]
+    for target in peers:
         greet(target)
-
-    def greet_z(k, carry):
-        greet(me.z_peer(k))
-        return carry
-
-    lax.fori_loop(1, Z_SIZE, greet_z, 0)
-    pl.semaphore_wait(
-        pltpu.get_barrier_semaphore(), 1 + (X_SIZE - 1) + (Y_SIZE - 1) + 4 + (Z_SIZE - 1)
-    )
+    pl.semaphore_wait(pltpu.get_barrier_semaphore(), len(peers))
     count = range(len(CHUNKS))
 
     def correction(index):
@@ -598,7 +586,8 @@
 
     part1 = GRAD_ROWS // CORES
     part2 = part1 // X_SIZE
-    part3 = part2 // Z_SIZE
+    part3 = part2 // NEAR
+    part4 = part3 // NEAR
 
     def span(index, size):
         return pl.ds(pl.multiple_of(index * size, size), size)
@@ -626,19 +615,15 @@
 
     a2[...] = a1[span(x, part2), :] + r2[0] + r2[1] + r2[2]
 
-    def z_sum(k):
-        target = lax.rem(z + k, Z_SIZE)
-        return remote(a2.at[span(target, part3)], r3.at[k - 1], s3.at[k - 1], v3.at[k - 1], me.z_peer(k))
-
-    def start_z_sum(k, carry):
-        z_sum(k).start()
-        return carry
-
-    def wait_z_sum(k, carry):
-        z_sum(k).wait()
-        return carry
-
-    lax.fori_loop(1, Z_SIZE, start_z_sum, 0)
+    near, far = lax.rem(z, NEAR), z // NEAR
+    copies = []
+    for k in range(1, NEAR):
+        target = lax.rem(near + k, NEAR)
+        copies.append(
+            remote(a2.at[span(target, part3)], r3.at[k - 1], s3.at[k - 1], v3.at[k - 1], me.near_peer(k))
+        )
+    for copy in copies:
+        copy.start()
 
     @pl.when(me.space == 0)
     def _():
@@ -647,40 +632,54 @@
                 correction(index).wait_recv()
                 relay(index).start()
 
-    lax.fori_loop(1, Z_SIZE, wait_z_sum, 0)
-    total = a2[span(z, part3), :]
-    for k in range(Z_SIZE - 1):
-        total = total + r3[k]
-
-    r4[y] = total
+    for copy in copies:
+        copy.wait()
+    a3[...] = a2[span(near, part3), :] + r3[0] + r3[1] + r3[2]
+
+    copies = []
+    for k in range(1, NEAR):
+        target = lax.rem(far + k, NEAR)
+        copies.append(
+            remote(a3.at[span(target, part4)], r4.at[k - 1], s4.at[k - 1], v4.at[k - 1], me.far_peer(k))
+        )
+    for copy in copies:
+        copy.start()
+    for copy in copies:
+        copy.wait()
+
+    r5[y] = a3[span(far, part4), :] + r4[0] + r4[1] + r4[2]
     copies = [
-        remote(r4.at[y], r4.at[y], s4.at[k - 1], v4.at[k - 1], me.y_peer(k)) for k in range(1, Y_SIZE)
+        remote(r5.at[y], r5.at[y], s5.at[k - 1], v5.at[k - 1], me.y_peer(k)) for k in range(1, Y_SIZE)
     ]
     for copy in copies:
         copy.start()
     for copy in copies:
         copy.wait()
     terms = PATCHES * lax.axis_size("phase") * lax.axis_size("space")
-    a4[...] = ((r4[0] + r4[1]) + (r4[2] + r4[3])) * (1.0 / math.sqrt(terms))
-
-    f2[span(z, part3), :] = a4[...]
-
-    def z_spread(k):
-        return remote(a4, f2.at[span(z, part3)], s5.at[k - 1], v5.at[k - 1], me.z_peer(k))
-
-    def start_z_spread(k, carry):
-        z_spread(k).start()
-        return carry
-
-    def wait_z_spread(k, carry):
-        z_spread(k).wait()
-        return carry
-
-    lax.fori_loop(1, Z_SIZE, start_z_spread, 0)
-    lax.fori_loop(1, Z_SIZE, wait_z_spread, 0)
+    a5[...] = ((r5[0] + r5[1]) + (r5[2] + r5[3])) * (1.0 / math.sqrt(terms))
 
     copies = [
-        remote(f2, f1.at[span(x, part2)], s6.at[k - 1], v6.at[k - 1], me.x_peer(k))
+        remote(a5, f3.at[span(far, part4)], s6.at[k - 1], v6.at[k - 1], me.far_peer(k))
+        for k in range(1, NEAR)
+    ]
+    for copy in copies:
+        copy.start()
+    f3[span(far, part4), :] = a5[...]
+    for copy in copies:
+        copy.wait()
+
+    copies = [
+        remote(f3, f2.at[span(near, part3)], s7.at[k - 1], v7.at[k - 1], me.near_peer(k))
+        for k in range(1, NEAR)
+    ]
+    for copy in copies:
+        copy.start()
+    f2[span(near, part3), :] = f3[...]
+    for copy in copies:
+        copy.wait()
+
+    copies = [
+        remote(f2, f1.at[span(x, part2)], s8.at[k - 1], v8.at[k - 1], me.x_peer(k))
         for k in range(1, X_SIZE)
     ]
     for copy in copies:
@@ -693,14 +692,10 @@
         if corrected:
             correction(index).wait_recv()
             numer = numer + inc[part, rows, :]
-        here = own[part, rows, :]
-        resid = following[part, rows, :] - start_point[part, rows, :]
-        steady = here - tv_step * ((here - preceding[part, rows, :]) - resid)
-        updated[part, rows, :] = steady + numer * inverse[rows, :]
+        updated[part, rows, :] = steady[part, rows, :] + numer * inverse[rows, :]
         updated_copy(index).start()
 
-    for load in loads:
-        load.wait()
+    load.wait()
 
     @pl.when(me.space == 0)
     def _():
@@ -715,7 +710,7 @@
     for copy in copies:
         copy.wait()
 
-    copy = remote(f1, f0.at[span(core, part1)], s7, v7, me.core_peer())
+    copy = remote(f1, f0.at[span(core, part1)], s9, v9, me.core_peer())
     copy.start()
     f0[span(core, part1), :] = f1[...]
     copy.wait()
@@ -739,39 +734,43 @@
                 relay(index).wait_send()
 
 
-def tail(numer_own, numer_next, inverse, term, own, start_point, following, preceding):
+def tail(numer_own, numer_next, inverse, term, steady):
     part1 = GRAD_ROWS // CORES
     part2 = part1 // X_SIZE
-    part3 = part2 // Z_SIZE
+    part3 = part2 // NEAR
+    part4 = part3 // NEAR
     f32 = jnp.float32
     dma = pltpu.SemaphoreType.DMA
     vmem = pl.BlockSpec(memory_space=pltpu.VMEM)
     hbm = pl.BlockSpec(memory_space=pltpu.HBM)
-    place = pl.BlockSpec(memory_space=pl.ANY)
     room = pltpu.VMEM((2, BAND, SIDE), f32)
     many = dma((len(CHUNKS),))
     band = jax.ShapeDtypeStruct((2, BAND, SIDE), f32)
     sems = []
-    for count in (1, X_SIZE - 1, Z_SIZE - 1, Y_SIZE - 1, Z_SIZE - 1, X_SIZE - 1, 1):
+    steps = (1, X_SIZE - 1, NEAR - 1, NEAR - 1, Y_SIZE - 1, NEAR - 1, NEAR - 1, X_SIZE - 1, 1)
+    for count in steps:
         sems += [dma if count == 1 else dma((count,))] * 2
     return pl.pallas_call(
         tail_kernel,
-        in_specs=[vmem, hbm, vmem, vmem, place, place, place, place],
+        in_specs=[vmem, hbm, vmem, vmem, hbm],
         out_specs=[vmem] * 3,
         out_shape=[band, band, jax.ShapeDtypeStruct((2, SIDE, SIDE), f32)],
         scratch_shapes=[
-            room, room, room, room, room,
+            room, room,
             pltpu.VMEM((part1, HALF), f32),
             pltpu.VMEM((part1, HALF), f32),
             pltpu.VMEM((X_SIZE - 1, part2, HALF), f32),
             pltpu.VMEM((part2, HALF), f32),
-            pltpu.VMEM((Z_SIZE - 1, part3, HALF), f32),
-            pltpu.VMEM((Y_SIZE, part3, HALF), f32),
+            pltpu.VMEM((NEAR - 1, part3, HALF), f32),
+            pltpu.VMEM((part3, HALF), f32),
+            pltpu.VMEM((NEAR - 1, part4, HALF), f32),
+            pltpu.VMEM((Y_SIZE, part4, HALF), f32),
+            pltpu.VMEM((part4, HALF), f32),
             pltpu.VMEM((part3, HALF), f32),
             pltpu.VMEM((part2, HALF), f32),
             pltpu.VMEM((part1, HALF), f32),
             pltpu.VMEM((GRAD_ROWS, HALF), f32),
-            dma((4,)), many, many, many, many, many,
+            dma, many, many, many, many, many,
             *sems,
         ],
         compiler_params=pltpu.CompilerParams(
@@ -779,7 +778,7 @@
         ),
         cost_estimate=pl.CostEstimate(flops=2**20, bytes_accessed=2**24, transcendentals=0),
         name="tail",
-    )(numer_own, numer_next, inverse, term, own, start_point, following, preceding)
+    )(numer_own, numer_next, inverse, term, steady)
 
 
 def finish_kernel(updated, next_updated, dual, summed, out_object, out_split, out_dual, out_sum):
@@ -818,16 +817,11 @@
     own = object_field[:, 0]
     split_own = split_field[:, 0]
     dual_own = scaled_dual[:, 0]
-    halo, start_point, behind = opening(own, split_own, dual_own, row_offsets, col_offsets)
-    sent, halo = lax.optimization_barrier((own, halo))
-    following = passed_along(sent, "phase", -1)
-    preceding = passed_along(start_point, "phase", 1)
+    halo, steady, behind = opening(own, split_own, dual_own, row_offsets, col_offsets)
     numer_own, numer_next, grad, inverse = patch_terms(
         row_offsets, col_offsets, behind, own, halo, probe, amplitudes
     )
-    updated, next_updated, summed = tail(
-        numer_own, numer_next, inverse, grad, own, start_point, following, preceding
-    )
+    updated, next_updated, summed = tail(numer_own, numer_next, inverse, grad, steady)
     updated, new_split, new_dual, probe_gradient = finish(updated, next_updated, dual_own, summed)
     return (updated[:, None], new_split[:, None], new_dual[:, None], probe_gradient)
 

time: 99.9 us -> 100 us (level)
  Pallas kernels: 88.1 us -> 99.2 us
  starting transfers between devices: 9.73 us -> 0 us
    ppermute x2 -> x0, starting transfers between devices: 9.73 us -> none  [passed_along(): return lax.ppermute(value, axis, pairs)]
    pallas_call x1, Pallas kernels: 51.5 us -> 60.7 us  [tail(): pl.pallas_call(tail_kernel, in_specs=[vmem, hbm, vmem, vmem, hbm], out_sp...]
    pallas_call x1, Pallas kernels: 16.3 us -> 18.2 us  [opening(): pl.pallas_call(opening_kernel, in_specs=[pl.BlockSpec(memory_space=pltpu....]
  transfers between devices with their start and end apart: 2 -> 0, of which waited for: 0 -> 0; matrix products, arithmetic and copies ran while one was open for 0% -> 0% of each run, Pallas kernels for 18% -> 0%
where the time goes in v6:
time: 100 us; the launch traced here: 99.9 us
  Pallas kernels  99.2 us (99%)
    pallas_call x1, Pallas kernels, tail(): pl.pallas_call(tail_kernel, in_specs=[vmem, hbm, vmem, vmem, hbm], out_sp...  60.7 us
    pallas_call x1, Pallas kernels, opening(): pl.pallas_call(opening_kernel, in_specs=[pl.BlockSpec(memory_space=pltpu....  18.2 us
    pallas_call x1, Pallas kernels, patch_terms(): pl.pallas_call(patch_kernel, grid=(count // GROUP,), in_specs=[scalars, s...  17.6 us
    pallas_call x1, Pallas kernels, finish(): pl.pallas_call(finish_kernel, grid=(steps,), in_specs=[band, band, band,...  2.73 us

profile of v6, /device:TPU:1, one launch (start us, length us, event | category | flops | bytes accessed | tf_op | source)
XLA Modules:
  0.0 99.9 jit_solution(2405332206656831920)
XLA Ops:
  0.6 18.2 %opening.1 = (f32[2,272,256]{2,1,0:T(8,128)}, f32[2,272,256]{2,1,0:T(8,128)}, s32[8,128]{1,0:T(8,128)}) custom-call(f32[2,272,256]{2,1,0:T(8,128)} %bitcast.15, f32[2,272,256]{2,1,0:T(8,128)} %bitcast.14, f32[2,272,256]{2,1,0:T(8,128)} %bitcast.12, s32[1,6]{1,0:T(1,128)} %rows_s.1, s32[1,6]{1,0:T(1,128)} %cols_s.1), custom_call_target="tpu_custom_call" | custom-call | flops 1048576 | bytes 16777216 | tf_op jit(solution)/shard_map/opening/pallas_call | solution.py:516
  18.8 17.6 %patch_terms.1 = (f32[2,272,256]{2,1,0:T(8,128)}, f32[2,272,256]{2,1,0:T(8,128)}, f32[1024,128]{1,0:T(8,128)}, f32[272,256]{1,0:T(8,128)}) custom-call(s32[1,6]{1,0:T(1,128)} %rows_s.1, s32[1,6]{1,0:T(1,128)} %cols_s.1, s32[8,128]{1,0:T(8,128)} %get-tuple-element.18.behind, f32[2,272,256]{2,1,0:T(8,128)} %bitcast.16, f32[2,272,256]{2,1,0:T(8,128)} %get-tuple-element.19.halo, ...), custom_call_target="tpu_custom_call" | custom-call | flops 5234491392 | bytes 6291456 | tf_op jit(solution)/shard_map/patch_terms/pallas_call | solution.py:321
  36.4 60.7 %tail.1 = (f32[2,272,256]{2,1,0:T(8,128)}, f32[2,272,256]{2,1,0:T(8,128)}, f32[2,256,256]{2,1,0:T(8,128)}) custom-call(f32[2,272,256]{2,1,0:T(8,128)} %get-tuple-element.20.numer_own, f32[2,272,256]{2,1,0:T(8,128)} %get-tuple-element.21.numer_next, f32[272,256]{1,0:T(8,128)} %get-tuple-element.22.inverse, f32[1024,128]{1,0:T(8,128)} %get-tuple-element.23.term, ...), custom_call_target="tpu_custom_call" | custom-call | flops 1048576 | bytes 16777216 | tf_op jit(solution)/shard_map/tail/pallas_call | solution.py:753
  97.2 2.7 %finish.1 = (f32[2,272,256]{2,1,0:T(8,128)}, f32[2,272,256]{2,1,0:T(8,128)}, f32[2,272,256]{2,1,0:T(8,128)}, f32[2,256,256]{2,1,0:T(8,128)}) custom-call(f32[2,272,256]{2,1,0:T(8,128)} %get-tuple-element.25.updated, f32[2,272,256]{2,1,0:T(8,128)} %get-tuple-element.26.next_updated, f32[2,272,256]{2,1,0:T(8,128)} %bitcast.13, ...), custom_call_target="tpu_custom_call" | custom-call | flops 1048576 | bytes 4194304 | tf_op jit(solution)/shard_map/finish/pallas_call | solution.py:802

commit v7 on v5

--- a/solution.py
+++ b/solution.py
@@ -23,13 +23,8 @@
 TILES = X_SIZE // X_LO * Y_SIZE
 PATCHES = 6
 VMEM_BYTES = 58 * 1024 * 1024
-GROUP = 2
-
-
-def passed_along(value, axis, steps):
-    count = lax.axis_size(axis)
-    pairs = [(source, (source + steps) % count) for source in range(count)]
-    return lax.ppermute(value, axis, pairs)
+SETS = 3
+LAG = 3
 
 
 def two_parts(table):
@@ -94,48 +89,36 @@
     numer_own, numer_next, grad, weight,
     power, sorter, le, let, lo, lot, amp, table_sems, amp_sems, *scratch,
 ):
-    group = pl.program_id(0)
-    groups = amp.shape[0] // GROUP
-    tables = [
+    loads = [
         pltpu.make_async_copy(src, dst, table_sems.at[i])
         for i, (src, dst) in enumerate(((le_h, le), (let_h, let), (lo_h, lo), (lot_h, lot)))
     ]
-
-    def amp_load(index):
-        rows = pl.ds(index * GROUP, GROUP)
-        return pltpu.make_async_copy(amp_h.at[0, rows], amp.at[rows], amp_sems.at[index])
-
-    first_slot = pl.program_id(0) * GROUP
+    count = amp.shape[0]
+    amp_loads = [
+        pltpu.make_async_copy(amp_h.at[0, slot], amp.at[slot], amp_sems.at[slot])
+        for slot in range(count)
+    ]
+    for load in loads + amp_loads:
+        load.start()
     step = 16
     row_id = lax.broadcasted_iota(jnp.int32, (step, HALF), 0)
     lane_id = lax.broadcasted_iota(jnp.int32, (step, HALF), 1)
     re_half, im_half = slice(0, HALF), slice(HALF, SIDE)
 
-    @pl.when(group == 0)
-    def _():
-        for load in tables:
-            load.start()
-        for index in range(groups):
-            amp_load(index).start()
-        numer_own[...] = jnp.zeros_like(numer_own)
-        numer_next[...] = jnp.zeros_like(numer_next)
-        grad[...] = jnp.zeros_like(grad)
-        weight[...] = jnp.full_like(weight, ridge)
-        power[...] = probe[0] * probe[0] + probe[1] * probe[1]
-        place = lax.broadcasted_iota(jnp.int32, (SIDE, SIDE), 0)
-        target = lax.broadcasted_iota(jnp.int32, (SIDE, SIDE), 1)
-        source = jnp.where(target < HALF, 2 * target, 2 * (target - HALF) + 1)
-        sorter[...] = jnp.where(place == source, 1.0, 0.0).astype(jnp.bfloat16)
-        for load in tables:
-            load.wait()
-
-    amp_load(group).wait()
-
-    def stages(member):
+    numer_own[...] = jnp.zeros_like(numer_own)
+    numer_next[...] = jnp.zeros_like(numer_next)
+    grad[...] = jnp.zeros_like(grad)
+    weight[...] = jnp.full_like(weight, ridge)
+    power[...] = probe[0] * probe[0] + probe[1] * probe[1]
+    place = lax.broadcasted_iota(jnp.int32, (SIDE, SIDE), 0)
+    target = lax.broadcasted_iota(jnp.int32, (SIDE, SIDE), 1)
+    source = jnp.where(target < HALF, 2 * target, 2 * (target - HALF) + 1)
+    sorter[...] = jnp.where(place == source, 1.0, 0.0).astype(jnp.bfloat16)
+
+    def stages(slot):
         brow, prow, pc, piece_s, wave_s, grow, xe, xo, ze, zo, amp_s, amp_c = scratch[
-            member * 12 : member * 12 + 12
+            slot % SETS * 12 : slot % SETS * 12 + 12
         ]
-        slot = first_slot + member
         top, left = rows_s[0, slot], cols_s[0, slot]
         top_b, left_b = behind[0, slot], behind[1, slot]
         row_in = row_id >= top
@@ -149,6 +132,10 @@
             rolled_probe(power, brow, left_b)
 
         def sort_amplitudes():
+            if slot == 0:
+                for load in loads:
+                    load.wait()
+            amp_loads[slot].wait()
             for side in range(2):
                 amp_c[side] = amp[slot, :, side * HALF : (side + 1) * HALF]
             for odd in range(2):
@@ -284,7 +271,7 @@
         return [
             turn_probe,
             waves,
-            lambda: (over_rows(0), sort_amplitudes(), over_rows(1)),
+            lambda: (sort_amplitudes(), over_rows(0), over_rows(1)),
             lambda: (over_columns(0), over_columns(1)),
             back_columns,
             back_rows,
@@ -292,25 +279,20 @@
             gradient,
         ]
 
-    ahead, after = stages(0), stages(1)
-    lag = 3
-    for turn in range(len(ahead) + lag):
-        if turn < len(ahead):
-            ahead[turn]()
-        if turn >= lag:
-            after[turn - lag]()
-
-    @pl.when(pl.program_id(0) == pl.num_programs(0) - 1)
-    def _():
-        weight[...] = 1.0 / weight[...]
+    lines = [stages(slot) for slot in range(count)]
+    for turn in range(len(lines[0]) + LAG * (count - 1)):
+        for slot, line in enumerate(lines):
+            if 0 <= turn - LAG * slot < len(line):
+                line[turn - LAG * slot]()
+
+    weight[...] = 1.0 / weight[...]
 
 
 def patch_terms(rows, cols, behind, own, halo, probe, amplitudes):
     count = amplitudes.shape[1]
     tables = half_tables()
-    whole = lambda *shape: pl.BlockSpec(shape, lambda k: (0,) * len(shape))
+    vmem = pl.BlockSpec(memory_space=pltpu.VMEM)
     scalars = pl.BlockSpec(memory_space=pltpu.SMEM)
-    band = whole(2, BAND, SIDE)
     f32, bf16 = jnp.float32, jnp.bfloat16
     split = pltpu.VMEM((2, SIDE, SIDE), bf16)
     square = pltpu.VMEM((2, SIDE, SIDE), f32)
@@ -325,10 +307,9 @@
     ]
     return pl.pallas_call(
         patch_kernel,
-        grid=(count // GROUP,),
-        in_specs=[scalars, scalars, scalars, band, band, whole(2, SIDE, SIDE)]
+        in_specs=[scalars, scalars, scalars, vmem, vmem, vmem]
         + [pl.BlockSpec(memory_space=pltpu.HBM)] * 5,
-        out_specs=[band, band, whole(GRAD_ROWS, HALF), whole(BAND, SIDE)],
+        out_specs=[vmem] * 4,
         out_shape=[
             jax.ShapeDtypeStruct((2, BAND, SIDE), f32),
             jax.ShapeDtypeStruct((2, BAND, SIDE), f32),
@@ -340,12 +321,10 @@
         + [
             pltpu.VMEM((count, SIDE, SIDE), f32),
             pltpu.SemaphoreType.DMA((4,)),
-            pltpu.SemaphoreType.DMA((count // GROUP,)),
+            pltpu.SemaphoreType.DMA((count,)),
         ]
-        + member * GROUP,
-        compiler_params=pltpu.CompilerParams(
-            dimension_semantics=("arbitrary",), vmem_limit_bytes=VMEM_BYTES
-        ),
+        + member * SETS,
+        compiler_params=pltpu.CompilerParams(vmem_limit_bytes=VMEM_BYTES),
         cost_estimate=pl.CostEstimate(
             flops=count * 26 * 2 * SIDE**3, bytes_accessed=6 * 2**20, transcendentals=0
         ),
@@ -376,11 +355,11 @@
     def y_peer(self, k):
         return self.device(self.core, self.z, self.x, lax.rem(self.y + k, Y_SIZE))
 
+    def y_mirror(self):
+        return self.device(self.core, self.z, self.x, Y_SIZE - 1 - self.y)
+
     def z_peer(self, k):
         return self.device(self.core, lax.rem(self.z + k, Z_SIZE), self.x, self.y)
-
-    def y_mirror(self):
-        return self.device(self.core, self.z, self.x, Y_SIZE - 1 - self.y)
 
     def bin_at(self, k):
         count = lax.axis_size("phase")
@@ -404,7 +383,7 @@
     )
 
 
-ROW_CUTS = (0, 72, 136, 208, 272)
+ROW_CUTS = (0, 136, 272)
 CHUNKS = tuple(
     (part, slice(ROW_CUTS[i], ROW_CUTS[i + 1])) for i in range(len(ROW_CUTS) - 1) for part in range(2)
 )
@@ -422,9 +401,9 @@
 
 def opening_kernel(
     own, split_h, dual_h, rows_h, cols_h,
-    halo, start_point, behind,
-    here, split, dual, rows, cols, offsets,
-    ls, hs, hv, rs, os, ov,
+    halo, steady, behind,
+    here, split, dual, start_point, following, preceding, rows, cols, offsets,
+    ls, hs, hv, rs, ns, nv, ps, pv, os, ov,
 ):
     me = Place()
     last = TILES - 1
@@ -439,12 +418,14 @@
         load.start()
     for target in (me.tile_at(1), me.tile_at(-1), me.tile_at(TILES // 2), me.y_mirror()):
         greet(target)
+    for target in (me.bin_at(1), me.bin_at(-1)):
+        greet(target)
 
     @pl.when(me.space == 0)
     def _():
         behind[...] = jnp.zeros_like(behind)
 
-    pl.semaphore_wait(pltpu.get_barrier_semaphore(), 4)
+    pl.semaphore_wait(pltpu.get_barrier_semaphore(), 6)
 
     def halo_copy(index):
         target = me.y_peer(Y_SIZE - 1) if by_ring(index) else me.tile_at(-1)
@@ -459,8 +440,13 @@
         for index in count:
             halo_copy(index).start()
 
-    loads[0].wait()
-    loads[1].wait()
+    to_preceding = remote(own, following, ns, nv, me.bin_at(-1))
+    to_following = remote(start_point, preceding, ps, pv, me.bin_at(1))
+    to_preceding.start()
+    for load in loads:
+        load.wait()
+    start_point[...] = here[...] + split[...] - dual[...]
+    to_following.start()
     offsets[...] = jnp.zeros_like(offsets)
     offsets[0:1, 0 : rows.shape[1]] = rows[...]
     offsets[1:2, 0 : cols.shape[1]] = cols[...]
@@ -470,16 +456,18 @@
     def _():
         offsets_on.start()
 
-    for load in loads[2:]:
-        load.wait()
-    start_point[...] = here[...] + split[...] - dual[...]
-
     @pl.when(me.space == last)
     def _():
         for index in count:
             if by_ring(index):
                 halo_copy(index).wait_recv()
                 relay(index).start()
+
+    to_preceding.wait()
+    to_following.wait()
+    steady[...] = here[...] - tv_step * (
+        (here[...] - preceding[...]) - (following[...] - start_point[...])
+    )
 
     @pl.when(me.space > 0)
     def _():
@@ -519,9 +507,9 @@
             jax.ShapeDtypeStruct((8, HALF), i32),
         ],
         scratch_shapes=[
-            room, room, room,
+            room, room, room, room, room, room,
             pltpu.VMEM(rows.shape, i32), pltpu.VMEM(cols.shape, i32), pltpu.VMEM((8, HALF), i32),
-            dma((5,)), many, many, many, dma, dma,
+            dma((5,)), many, many, many, dma, dma, dma, dma, dma, dma,
         ],
         compiler_params=pltpu.CompilerParams(
             collective_id=0, has_side_effects=True, vmem_limit_bytes=VMEM_BYTES
@@ -532,9 +520,9 @@
 
 
 def tail_kernel(
-    numer_own, numer_next, inverse, term, own_h, start_h, following_h, preceding_h,
+    numer_own, numer_next, inverse, term, steady_h,
     updated, next_updated, out,
-    own, start_point, following, preceding, inc, r1, a1, r2, a2, r3, r4, a4, f2, f1, f0,
+    steady, inc, r1, a1, r2, a2, r3, r4, a4, f2, f1, f0,
     ls, cs, cv, rs, us, uv,
     s1, v1, s2, v2, s3, v3, s4, v4, s5, v5, s6, v6, s7, v7,
 ):
@@ -542,25 +530,14 @@
     core, x, y, z = me.core, me.x, me.y, me.z
     last = TILES - 1
 
-    loads = [
-        pltpu.make_async_copy(src, dst, ls.at[i])
-        for i, (src, dst) in enumerate(
-            (
-                (own_h, own),
-                (start_h, start_point),
-                (following_h, following),
-                (preceding_h, preceding),
-            )
-        )
-    ]
-    for load in loads:
-        load.start()
+    load = pltpu.make_async_copy(steady_h, steady, ls)
+    load.start()
     greet(me.core_peer())
     for k in range(1, X_SIZE):
         greet(me.x_peer(k))
     for k in range(1, Y_SIZE):
         greet(me.y_peer(k))
-    for target in (me.bin_at(1), me.bin_at(-1), me.tile_at(1), me.tile_at(-1)):
+    for target in (me.tile_at(1), me.tile_at(-1), me.bin_at(1), me.bin_at(-1)):
         greet(target)
 
     def greet_z(k, carry):
@@ -571,7 +548,6 @@
     pl.semaphore_wait(
         pltpu.get_barrier_semaphore(), 1 + (X_SIZE - 1) + (Y_SIZE - 1) + 4 + (Z_SIZE - 1)
     )
-    count = range(len(CHUNKS))
 
     def correction(index):
         target = me.y_peer(1) if by_ring(index) else me.tile_at(1)
@@ -589,12 +565,19 @@
             me.bin_at(-1),
         )
 
-    for index in count:
-        early = last if by_ring(index) else EDGE - 1
-
-        @pl.when(jnp.logical_or(me.space < early, jnp.logical_and(me.space > EDGE - 1, me.space < last)))
+    order = range(len(CHUNKS))
+    ringed = [index for index in order if by_ring(index)]
+
+    @pl.when(me.space < last)
+    def _():
+        for index in order:
+            correction(index).start()
+
+    def relay_on(index):
+        @pl.when(me.space == 0)
         def _():
-            correction(index).start()
+            correction(index).wait_recv()
+            relay(index).start()
 
     part1 = GRAD_ROWS // CORES
     part2 = part1 // X_SIZE
@@ -616,14 +599,9 @@
         )
     for copy in copies:
         copy.start()
+    relay_on(ringed[0])
     for copy in copies:
         copy.wait()
-    @pl.when(me.space == EDGE - 1)
-    def _():
-        for index in count:
-            if not by_ring(index):
-                correction(index).start()
-
     a2[...] = a1[span(x, part2), :] + r2[0] + r2[1] + r2[2]
 
     def z_sum(k):
@@ -639,14 +617,7 @@
         return carry
 
     lax.fori_loop(1, Z_SIZE, start_z_sum, 0)
-
-    @pl.when(me.space == 0)
-    def _():
-        for index in count:
-            if by_ring(index):
-                correction(index).wait_recv()
-                relay(index).start()
-
+    relay_on(ringed[1])
     lax.fori_loop(1, Z_SIZE, wait_z_sum, 0)
     total = a2[span(z, part3), :]
     for k in range(Z_SIZE - 1):
@@ -660,8 +631,8 @@
         copy.start()
     for copy in copies:
         copy.wait()
-    terms = PATCHES * lax.axis_size("phase") * lax.axis_size("space")
-    a4[...] = ((r4[0] + r4[1]) + (r4[2] + r4[3])) * (1.0 / math.sqrt(terms))
+    count = PATCHES * lax.axis_size("phase") * lax.axis_size("space")
+    a4[...] = ((r4[0] + r4[1]) + (r4[2] + r4[3])) * (1.0 / math.sqrt(count))
 
     f2[span(z, part3), :] = a4[...]
 
@@ -677,6 +648,23 @@
         return carry
 
     lax.fori_loop(1, Z_SIZE, start_z_spread, 0)
+    load.wait()
+
+    for index in order:
+        part, rows = CHUNKS[index]
+
+        @pl.when(me.space > 0)
+        def _():
+            correction(index).wait_recv()
+            numer = numer_own[part, rows, :] + inc[part, rows, :]
+            updated[part, rows, :] = steady[part, rows, :] + numer * inverse[rows, :]
+
+        @pl.when(me.space == 0)
+        def _():
+            updated[part, rows, :] = steady[part, rows, :] + numer_own[part, rows, :] * inverse[rows, :]
+
+        updated_copy(index).start()
+
     lax.fori_loop(1, Z_SIZE, wait_z_spread, 0)
 
     copies = [
@@ -686,32 +674,6 @@
     for copy in copies:
         copy.start()
     f1[span(x, part2), :] = f2[...]
-
-    def send_updated(index, corrected):
-        part, rows = CHUNKS[index]
-        numer = numer_own[part, rows, :]
-        if corrected:
-            correction(index).wait_recv()
-            numer = numer + inc[part, rows, :]
-        here = own[part, rows, :]
-        resid = following[part, rows, :] - start_point[part, rows, :]
-        steady = here - tv_step * ((here - preceding[part, rows, :]) - resid)
-        updated[part, rows, :] = steady + numer * inverse[rows, :]
-        updated_copy(index).start()
-
-    for load in loads:
-        load.wait()
-
-    @pl.when(me.space == 0)
-    def _():
-        for index in count:
-            send_updated(index, False)
-
-    @pl.when(me.space > 0)
-    def _():
-        for index in count:
-            send_updated(index, True)
-
     for copy in copies:
         copy.wait()
 
@@ -724,22 +686,21 @@
             begin = (2 * c + side) * SIDE
             out[c, :, side * HALF : (side + 1) * HALF] = f0[begin : begin + SIDE, :]
 
-    for index in count:
+    for index in order:
         updated_copy(index).wait()
 
     @pl.when(me.space < last)
     def _():
-        for index in count:
+        for index in order:
             correction(index).wait_send()
 
     @pl.when(me.space == 0)
     def _():
-        for index in count:
-            if by_ring(index):
-                relay(index).wait_send()
-
-
-def tail(numer_own, numer_next, inverse, term, own, start_point, following, preceding):
+        for index in ringed:
+            relay(index).wait_send()
+
+
+def tail(numer_own, numer_next, inverse, term, steady):
     part1 = GRAD_ROWS // CORES
     part2 = part1 // X_SIZE
     part3 = part2 // Z_SIZE
@@ -747,7 +708,6 @@
     dma = pltpu.SemaphoreType.DMA
     vmem = pl.BlockSpec(memory_space=pltpu.VMEM)
     hbm = pl.BlockSpec(memory_space=pltpu.HBM)
-    place = pl.BlockSpec(memory_space=pl.ANY)
     room = pltpu.VMEM((2, BAND, SIDE), f32)
     many = dma((len(CHUNKS),))
     band = jax.ShapeDtypeStruct((2, BAND, SIDE), f32)
@@ -756,11 +716,11 @@
         sems += [dma if count == 1 else dma((count,))] * 2
     return pl.pallas_call(
         tail_kernel,
-        in_specs=[vmem, hbm, vmem, vmem, place, place, place, place],
+        in_specs=[vmem, hbm, vmem, vmem, hbm],
         out_specs=[vmem] * 3,
         out_shape=[band, band, jax.ShapeDtypeStruct((2, SIDE, SIDE), f32)],
         scratch_shapes=[
-            room, room, room, room, room,
+            room, room,
             pltpu.VMEM((part1, HALF), f32),
             pltpu.VMEM((part1, HALF), f32),
             pltpu.VMEM((X_SIZE - 1, part2, HALF), f32),
@@ -771,7 +731,7 @@
             pltpu.VMEM((part2, HALF), f32),
             pltpu.VMEM((part1, HALF), f32),
             pltpu.VMEM((GRAD_ROWS, HALF), f32),
-            dma((4,)), many, many, many, many, many,
+            dma, many, many, many, many, many,
             *sems,
         ],
         compiler_params=pltpu.CompilerParams(
@@ -779,7 +739,7 @@
         ),
         cost_estimate=pl.CostEstimate(flops=2**20, bytes_accessed=2**24, transcendentals=0),
         name="tail",
-    )(numer_own, numer_next, inverse, term, own, start_point, following, preceding)
+    )(numer_own, numer_next, inverse, term, steady)
 
 
 def finish_kernel(updated, next_updated, dual, summed, out_object, out_split, out_dual, out_sum):
@@ -818,16 +778,11 @@
     own = object_field[:, 0]
     split_own = split_field[:, 0]
     dual_own = scaled_dual[:, 0]
-    halo, start_point, behind = opening(own, split_own, dual_own, row_offsets, col_offsets)
-    sent, halo = lax.optimization_barrier((own, halo))
-    following = passed_along(sent, "phase", -1)
-    preceding = passed_along(start_point, "phase", 1)
+    halo, steady, behind = opening(own, split_own, dual_own, row_offsets, col_offsets)
     numer_own, numer_next, grad, inverse = patch_terms(
         row_offsets, col_offsets, behind, own, halo, probe, amplitudes
     )
-    updated, next_updated, summed = tail(
-        numer_own, numer_next, inverse, grad, own, start_point, following, preceding
-    )
+    updated, next_updated, summed = tail(numer_own, numer_next, inverse, grad, steady)
     updated, new_split, new_dual, probe_gradient = finish(updated, next_updated, dual_own, summed)
     return (updated[:, None], new_split[:, None], new_dual[:, None], probe_gradient)
 

time: 99.9 us -> 96.5 us (0.966)
  starting transfers between devices: 9.73 us -> 0 us
  Pallas kernels: 88.1 us -> 95.6 us
    ppermute x2 -> x0, starting transfers between devices: 9.73 us -> none  [passed_along(): return lax.ppermute(value, axis, pairs)]
    pallas_call x2, Pallas kernels: 69.1 us -> 74.7 us  [the longest x1 57.9 us: tail(): pl.pallas_call(tail_kernel, in_specs=[vmem, hbm, vmem, vmem, hbm], out_sp...]
    pallas_call x1, Pallas kernels: 16.3 us -> 18.2 us  [opening(): pl.pallas_call(opening_kernel, in_specs=[pl.BlockSpec(memory_space=pltpu....]
  transfers between devices with their start and end apart: 2 -> 0, of which waited for: 0 -> 0; matrix products, arithmetic and copies ran while one was open for 0% -> 0% of each run, Pallas kernels for 18% -> 0%
where the time goes in v7:
time: 96.5 us; the launch traced here: 96.3 us
  Pallas kernels  95.6 us (99%)
    pallas_call x1, Pallas kernels, tail(): pl.pallas_call(tail_kernel, in_specs=[vmem, hbm, vmem, vmem, hbm], out_sp...  57.9 us
    pallas_call x1, Pallas kernels, opening(): pl.pallas_call(opening_kernel, in_specs=[pl.BlockSpec(memory_space=pltpu....  18.2 us
    pallas_call x1, Pallas kernels, patch_terms(): pl.pallas_call(patch_kernel, in_specs=[scalars, scalars, scalars, vmem, v...  16.8 us
    pallas_call x1, Pallas kernels, finish(): pl.pallas_call(finish_kernel, grid=(steps,), in_specs=[band, band, band,...  2.73 us

profile of v7, /device:TPU:1, one launch (start us, length us, event | category | flops | bytes accessed | tf_op | source)
XLA Modules:
  0.0 96.3 jit_solution(4405369645441664030)
XLA Ops:
  0.6 18.2 %opening.1 = (f32[2,272,256]{2,1,0:T(8,128)}, f32[2,272,256]{2,1,0:T(8,128)}, s32[8,128]{1,0:T(8,128)}) custom-call(f32[2,272,256]{2,1,0:T(8,128)} %bitcast.15, f32[2,272,256]{2,1,0:T(8,128)} %bitcast.14, f32[2,272,256]{2,1,0:T(8,128)} %bitcast.12, s32[1,6]{1,0:T(1,128)} %rows_s.1, s32[1,6]{1,0:T(1,128)} %cols_s.1), custom_call_target="tpu_custom_call" | custom-call | flops 1048576 | bytes 16777216 | tf_op jit(solution)/shard_map/opening/pallas_call | solution.py:496
  18.8 16.8 %patch_terms.1 = (f32[2,272,256]{2,1,0:T(8,128)}, f32[2,272,256]{2,1,0:T(8,128)}, f32[1024,128]{1,0:T(8,128)}, f32[272,256]{1,0:T(8,128)}) custom-call(s32[1,6]{1,0:T(1,128)} %rows_s.1, s32[1,6]{1,0:T(1,128)} %cols_s.1, s32[8,128]{1,0:T(8,128)} %get-tuple-element.18.behind, f32[2,272,256]{2,1,0:T(8,128)} %bitcast.16, f32[2,272,256]{2,1,0:T(8,128)} %get-tuple-element.19.halo, ...), custom_call_target="tpu_custom_call" | custom-call | flops 5234491392 | bytes 6291456 | tf_op jit(solution)/shard_map/patch_terms/pallas_call | solution.py:308
  35.6 57.9 %tail.1 = (f32[2,272,256]{2,1,0:T(8,128)}, f32[2,272,256]{2,1,0:T(8,128)}, f32[2,256,256]{2,1,0:T(8,128)}) custom-call(f32[2,272,256]{2,1,0:T(8,128)} %get-tuple-element.20.numer_own, f32[2,272,256]{2,1,0:T(8,128)} %get-tuple-element.21.numer_next, f32[272,256]{1,0:T(8,128)} %get-tuple-element.22.inverse, f32[1024,128]{1,0:T(8,128)} %get-tuple-element.23.term, ...), custom_call_target="tpu_custom_call" | custom-call | flops 1048576 | bytes 16777216 | tf_op jit(solution)/shard_map/tail/pallas_call | solution.py:717
  93.5 2.7 %finish.1 = (f32[2,272,256]{2,1,0:T(8,128)}, f32[2,272,256]{2,1,0:T(8,128)}, f32[2,272,256]{2,1,0:T(8,128)}, f32[2,256,256]{2,1,0:T(8,128)}) custom-call(f32[2,272,256]{2,1,0:T(8,128)} %get-tuple-element.25.updated, f32[2,272,256]{2,1,0:T(8,128)} %get-tuple-element.26.next_updated, f32[2,272,256]{2,1,0:T(8,128)} %bitcast.13, ...), custom_call_target="tpu_custom_call" | custom-call | flops 1048576 | bytes 4194304 | tf_op jit(solution)/shard_map/finish/pallas_call | solution.py:763
